TPU v7x, 32 devices: a whole 2x2x4 slice. The times are simulated.
32 devices in a mesh: groups: 2 (over x), ctx: 16 (over z, y, core).
Axes of the slice: x: 2, y: 2, z: 4, core: 2. Of those that a mesh axis runs over, the one named last changes fastest.
Arguments:
- queries: bfloat16 [8192, 2560], P(('groups', 'ctx')), parts along dimension 0, may hold values from -6 to 6
- keys: bfloat16 [8192, 2560], P(('groups', 'ctx')), parts along dimension 0, may hold values from -6 to 6
- values: bfloat16 [8192, 2560], P(('groups', 'ctx')), parts along dimension 0, may hold values from -6 to 6
- kv_lists: int32 [16, 4, 2, 8], P('ctx'), may hold values from 0 to 7, as said below
- kv_counts: int32 [16, 4, 2], P('ctx'), may hold values from 0 to 8, as said below
Outputs:
- attended: bfloat16 [8192, 2560], P(('groups', 'ctx')), parts along dimension 0
There are 2 independent parts, one for each index of `groups`. A program takes and returns all parts, laid end to end along the dimension named above; an argument that names none is the same for every part. Nothing has to cross between parts.
Inputs may be any that keep to these rules, and one draw needn't show every extreme that they name: For every device d, level k and side s, the first 8 // 2**k entries of kv_lists[d, k, s] are distinct block indices; later entries are never read. kv_counts[d, k, s] is at most 8 // 2**k and reaches it for some device at every level and side; it is 0 exactly where the partner d - 2**k (s = 0) or d + 2**k (s = 1) lies outside 0 to 15, else 1 or more.
All inputs are finite; a program needn't handle non-finite values.
Results may differ from a plain program's by a relative error of at most 0.005.
Values may be sent and summed in bfloat16 or wider, within the bound.
No kernel may reach another device: no remote copies, remote signals or barrier semaphores. Data moves between devices by JAX's collectives and lax.ppermute only.
A program may use at most 128 MiB of HBM per device.

v0:
```python
import math

import jax
import jax.numpy as jnp
from jax import lax
from jax.sharding import PartitionSpec as P

HEAD = 128


masked_score = -1e30


def from_behind(block, axis, distance):
    devices = range(lax.axis_size(axis))
    route = [(i - distance, i) for i in devices if i - distance in devices]
    return lax.ppermute(block, axis, route)


def attend(carried, query_heads, key_rows, value_rows, allowed):
    best_score, weight_total, weighted = carried
    head_count = query_heads.shape[1]
    head_size = query_heads.shape[2]
    key_heads = key_rows.reshape(key_rows.shape[0], head_count, head_size)
    value_heads = value_rows.reshape(value_rows.shape[0], head_count, head_size)
    scores = jnp.einsum(
        "qhd,khd->hqk", query_heads, key_heads, preferred_element_type=jnp.float32
    ) * (1.0 / math.sqrt(head_size))
    if allowed is not None:
        scores = jnp.where(allowed[None, None, :], scores, masked_score)
    fresh_best = jnp.maximum(best_score, jnp.max(scores, axis=-1))
    weights = jnp.exp(scores - fresh_best[:, :, None])
    factor = jnp.exp(best_score - fresh_best)
    weight_total = weight_total * factor + jnp.sum(weights, axis=-1)
    mixed_values = jnp.einsum(
        "hqk,khd->qhd",
        weights.astype(jnp.bfloat16),
        value_heads,
        preferred_element_type=jnp.float32,
    )
    weighted = weighted * jnp.transpose(factor)[:, :, None] + mixed_values
    return (fresh_best, weight_total, weighted)


def shards(queries, keys, values, kv_lists, kv_counts):
    row_count = queries.shape[0]
    width = queries.shape[1]
    head_count = width // HEAD
    block_count = kv_lists.shape[3]
    level_count = kv_lists.shape[1]
    block_rows = row_count // block_count
    query_heads = queries.reshape(row_count, head_count, HEAD)
    carried = (
        jnp.full((head_count, row_count), masked_score, jnp.float32),
        jnp.zeros((head_count, row_count), jnp.float32),
        jnp.zeros((row_count, head_count, HEAD), jnp.float32),
    )
    carried = attend(carried, query_heads, keys, values, None)
    key_blocks = keys.reshape(block_count, block_rows, width)
    value_blocks = values.reshape(block_count, block_rows, width)
    every_list = lax.all_gather(kv_lists, "ctx", axis=0, tiled=True)
    here_index = lax.axis_index("ctx")
    ctx_count = lax.axis_size("ctx")
    for level_id in range(level_count):
        distance = 1 << level_id
        capacity = block_count >> level_id
        for side_id in range(2):
            offset = distance if side_id == 0 else -distance
            counted = kv_counts[0, level_id, side_id]
            allowed = jnp.arange(capacity * block_rows, dtype=jnp.int32) // block_rows < counted
            target = jnp.clip(here_index + offset, 0, ctx_count - 1)
            wanted = lax.dynamic_index_in_dim(every_list, target, 0, keepdims=False)[
                level_id, side_id, :capacity
            ]
            packed = jnp.stack(
                [jnp.take(key_blocks, wanted, axis=0), jnp.take(value_blocks, wanted, axis=0)]
            )
            arrived = from_behind(packed, "ctx", offset)
            far_keys = arrived[0]
            far_values = arrived[1]
            carried = attend(
                carried,
                query_heads,
                far_keys.reshape(capacity * block_rows, width),
                far_values.reshape(capacity * block_rows, width),
                allowed,
            )
    best_score, weight_total, weighted = carried
    result = weighted / jnp.transpose(weight_total)[:, :, None]
    return result.reshape(row_count, width).astype(jnp.bfloat16)


def solution(mesh):
    in_specs = (
        P(("groups", "ctx"), None),
        P(("groups", "ctx"), None),
        P(("groups", "ctx"), None),
        P("ctx", None, None, None),
        P("ctx", None, None),
    )
    out_specs = P(("groups", "ctx"), None)
    return jax.shard_map(shards, mesh=mesh, in_specs=in_specs, out_specs=out_specs, check_vma=False)
```

profile of v0, /device:TPU:8, one launch (start us, length us, event | category | flops | bytes accessed | tf_op | source)
XLA Modules:
  0.0 219.9 jit_solution(879587065999367864)
XLA Ops:
  0.8 19.0 %all_gather.3 = s32[16,4,2,8]{3,1,2,0:T(4,128)S(1)} all-gather(s32[1,4,2,8]{3,1,2,0:T(4,128)S(1)} %copy.64), channel_id=1, replica_groups=mesh['groups'=2,'ctx'=16] {'ctx'}, dimensions={0}, use_global_device_ids=true | all-gather | bytes 4352 | tf_op jit(solution)/shard_map/all_gather | solution.py:61
  26.8 2.4 %collective-permute-start.1 = (bf16[2,8,32,2560]{3,2,1,0:T(8,128)(2,1)}, bf16[2,8,32,2560]{3,2,1,0:T(8,128)(2,1)}, u32[]{:S(2)}, u32[]{:S(2)}) collective-permute-start(bf16[2,8,32,2560]{3,2,1,0:T(8,128)(2,1)} %pad_maximum_fusion.1), channel_id=1, source_target_pairs={{1,0},{2,1},{3,2},{4,3},{5,4},{6,5},{7,6},{8,7},{9,8},{10,9},{11,1... | collective-permute-start | bytes 7864328 | tf_op jit(solution)/shard_map/ppermute | solution.py:17
  42.9 6.1 %collective-permute-start.3 = (bf16[2,4,32,2560]{3,2,1,0:T(8,128)(2,1)}, bf16[2,4,32,2560]{3,2,1,0:T(8,128)(2,1)}, u32[]{:S(2)}, u32[]{:S(2)}) collective-permute-start(bf16[2,4,32,2560]{3,2,1,0:T(8,128)(2,1)} %pad_maximum_fusion.3), channel_id=1, source_target_pairs={{2,0},{3,1},{4,2},{5,3},{6,4},{7,5},{8,6},{9,7},{10,8},{11,9},{12,... | collective-permute-start | bytes 3932168 | tf_op jit(solution)/shard_map/ppermute | solution.py:17
  79.9 3.2 %multiply_reduce_fusion = (f32[20,256]{1,0:T(8,128)S(1)}, f32[20,256,256]{1,2,0:T(8,128)}) fusion(bf16[256,20,128]{0,2,1:T(8,128)(2,1)S(1)} %bitcast.392, bf16[256,20,128]{0,2,1:T(8,128)(2,1)S(1)} %bitcast.417), kind=kOutput, calls=%fused_computation.21 | convolution fusion | flops 338160640 | bytes 7884800 | tf_op jit(solution)/shard_map/qhd,khd->hqk/dot_general | solution.py:26
  83.2 11.3 %collective-permute-done.7 = bf16[2,1,32,2560]{3,2,1,0:T(8,128)(2,1)} collective-permute-done((bf16[2,1,32,2560]{3,2,1,0:T(8,128)(2,1)}, bf16[2,1,32,2560]{3,2,1,0:T(8,128)(2,1)}, u32[]{:S(2)}, u32[]{:S(2)}) %collective-permute-start.7) | collective-permute-done | bytes 327712 | tf_op jit(solution)/shard_map/ppermute | solution.py:17
  96.9 3.5 %collective-permute-done.6 = bf16[2,1,32,2560]{3,2,1,0:T(8,128)(2,1)S(1)} collective-permute-done((bf16[2,1,32,2560]{3,2,1,0:T(8,128)(2,1)S(1)}, bf16[2,1,32,2560]{3,2,1,0:T(8,128)(2,1)S(1)}, u32[]{:S(2)}, u32[]{:S(2)}) %collective-permute-start.6) | collective-permute-done | bytes 327712 | tf_op jit(solution)/shard_map/ppermute | solution.py:17
  100.5 9.0 %collective-permute-start.5 = (bf16[2,2,32,2560]{3,2,1,0:T(8,128)(2,1)}, bf16[2,2,32,2560]{3,2,1,0:T(8,128)(2,1)}, u32[]{:S(2)}, u32[]{:S(2)}) collective-permute-start(bf16[2,2,32,2560]{3,2,1,0:T(8,128)(2,1)} %pad_maximum_fusion.5), channel_id=1, source_target_pairs={{4,0},{5,1},{6,2},{7,3},{8,4},{9,5},{10,6},{11,7},{12,8},{13,9},{1... | collective-permute-start | bytes 1966088 | tf_op jit(solution)/shard_map/ppermute | solution.py:17
  113.4 6.9 %collective-permute-done.5 = bf16[2,2,32,2560]{3,2,1,0:T(8,128)(2,1)} collective-permute-done((bf16[2,2,32,2560]{3,2,1,0:T(8,128)(2,1)}, bf16[2,2,32,2560]{3,2,1,0:T(8,128)(2,1)}, u32[]{:S(2)}, u32[]{:S(2)}) %collective-permute-start.5) | collective-permute-done | bytes 655392 | tf_op jit(solution)/shard_map/ppermute | solution.py:17
  120.3 3.9 %collective-permute-start.4 = (bf16[2,2,32,2560]{3,2,1,0:T(8,128)(2,1)}, bf16[2,2,32,2560]{3,2,1,0:T(8,128)(2,1)}, u32[]{:S(2)}, u32[]{:S(2)}) collective-permute-start(bf16[2,2,32,2560]{3,2,1,0:T(8,128)(2,1)} %pad_maximum_fusion.4), channel_id=1, source_target_pairs={{0,4},{1,5},{2,6},{3,7},{4,8},{5,9},{6,10},{7,11},{8,12},{9,13},{1... | collective-permute-start | bytes 1966088 | tf_op jit(solution)/shard_map/ppermute | solution.py:17
  126.3 6.8 %collective-permute-done.4 = bf16[2,2,32,2560]{3,2,1,0:T(8,128)(2,1)} collective-permute-done((bf16[2,2,32,2560]{3,2,1,0:T(8,128)(2,1)}, bf16[2,2,32,2560]{3,2,1,0:T(8,128)(2,1)}, u32[]{:S(2)}, u32[]{:S(2)}) %collective-permute-start.4) | collective-permute-done | bytes 655392 | tf_op jit(solution)/shard_map/ppermute | solution.py:17
  141.1 3.8 %collective-permute-done.3 = bf16[2,4,32,2560]{3,2,1,0:T(8,128)(2,1)} collective-permute-done((bf16[2,4,32,2560]{3,2,1,0:T(8,128)(2,1)}, bf16[2,4,32,2560]{3,2,1,0:T(8,128)(2,1)}, u32[]{:S(2)}, u32[]{:S(2)}) %collective-permute-start.3) | collective-permute-done | bytes 1310752 | tf_op jit(solution)/shard_map/ppermute | solution.py:17
  144.9 2.5 %fusion.127 = (bf16[1,4,32,2560]{3,2,1,0:T(8,128)(2,1)}, bf16[1,4,32,2560]{3,2,1,0:T(8,128)(2,1)}) fusion(bf16[2,4,32,2560]{3,2,1,0:T(8,128)(2,1)} %collective-permute-done.3), kind=kLoop, calls=%fused_computation.273 | loop fusion | bytes 2621440 | tf_op jit(solution)/shard_map/slice | solution.py:80
  149.7 2.5 %fusion.126 = (bf16[1,4,32,2560]{3,2,1,0:T(8,128)(2,1)}, bf16[1,4,32,2560]{3,2,1,0:T(8,128)(2,1)}) fusion(bf16[2,4,32,2560]{3,2,1,0:T(8,128)(2,1)} %collective-permute-done.2), kind=kLoop, calls=%fused_computation.272 | loop fusion | bytes 2621440 | tf_op jit(solution)/shard_map/slice | solution.py:80
  158.8 3.9 %bitcast_reduce_fusion.2 = (f32[20,256]{1,0:T(8,128)}, f32[20,128,256]{2,1,0:T(8,128)}) fusion(pred[128]{0:T(512)(128)(4,1)S(1)} %get-tuple-element.131, bf16[256,20,128]{0,2,1:T(8,128)(2,1)S(1)} %bitcast.397, bf16[128,20,128]{2,1,0:T(8,128)(2,1)} %reshape_reshape_squeeze.54), kind=kOutput, calls=%fused_computation.45 | convolution fusion | flops 169733120 | bytes 4608128 | tf_op jit(solution)/shard_map/qhd,khd->hqk/dot_general | solution.py:26
  164.8 3.5 %fusion.125 = (bf16[1,8,32,2560]{3,2,1,0:T(8,128)(2,1)}, bf16[1,8,32,2560]{3,2,1,0:T(8,128)(2,1)}) fusion(bf16[2,8,32,2560]{3,2,1,0:T(8,128)(2,1)} %collective-permute-done.1), kind=kLoop, calls=%fused_computation.271 | loop fusion | bytes 5242880 | tf_op jit(solution)/shard_map/slice | solution.py:80
  168.3 3.5 %reshape_reshape_squeeze.50 = bf16[256,20,128]{2,1,0:T(8,128)(2,1)} reshape(bf16[1,8,32,2560]{3,2,1,0:T(8,128)(2,1)} %get-tuple-element.53) | data formatting | bytes 2621440 | tf_op jit(solution)/shard_map/reshape;reshape;squeeze | solution.py:24
  171.8 3.5 %fusion.124 = (bf16[1,8,32,2560]{3,2,1,0:T(8,128)(2,1)}, bf16[1,8,32,2560]{3,2,1,0:T(8,128)(2,1)}) fusion(bf16[2,8,32,2560]{3,2,1,0:T(8,128)(2,1)} %collective-permute-done), kind=kLoop, calls=%fused_computation.270 | loop fusion | bytes 5242880 | tf_op jit(solution)/shard_map/slice | solution.py:80
  175.3 3.5 %reshape_reshape_squeeze.48 = bf16[256,20,128]{2,1,0:T(8,128)(2,1)} reshape(bf16[1,8,32,2560]{3,2,1,0:T(8,128)(2,1)} %get-tuple-element.51) | data formatting | bytes 2621440 | tf_op jit(solution)/shard_map/reshape;reshape;squeeze | solution.py:24
  178.8 3.5 %reshape_reshape_squeeze.49 = bf16[256,20,128]{2,1,0:T(8,128)(2,1)} reshape(bf16[1,8,32,2560]{3,2,1,0:T(8,128)(2,1)} %get-tuple-element.50) | data formatting | bytes 2621440 | tf_op jit(solution)/shard_map/reshape;reshape;squeeze | solution.py:25
  182.3 5.2 %bitcast_reduce_fusion = (f32[20,256]{1,0:T(8,128)S(1)}, f32[20,256,256]{1,2,0:T(8,128)}) fusion(pred[256]{0:T(512)(128)(4,1)S(1)} %get-tuple-element.125, bf16[256,20,128]{0,2,1:T(8,128)(2,1)S(1)} %bitcast.399, bf16[256,20,128]{2,1,0:T(8,128)(2,1)} %reshape_reshape_squeeze.50), kind=kOutput, calls=%fused_computation.13 | convolution fusion | flops 339471360 | bytes 7885056 | tf_op jit(solution)/shard_map/qhd,khd->hqk/dot_general | solution.py:26
  190.6 2.4 %fusion.4 = f32[20,256]{1,0:T(8,128)} fusion(f32[20,256,256]{1,2,0:T(8,128)S(1)} %get-tuple-element.116, f32[20,256]{1,0:T(8,128)S(1)} %get-tuple-element.37, pred[256]{0:T(512)(128)(4,1)S(1)} %copy-done.48), kind=kLoop, calls=%fused_computation.24 | loop fusion | flops 5237760 | bytes 5284096 | tf_op jit(solution)/shard_map/reduce_sum | solution.py:34
  193.0 3.0 %fusion.10 = f32[20,128,256]{2,1,0:T(8,128)} fusion(f32[20,256,256]{1,2,0:T(8,128)S(1)} %get-tuple-element.116, f32[20,256]{1,0:T(8,128)S(1)} %get-tuple-element.37, pred[256]{0:T(512)(128)(4,1)S(1)} %copy-done.48, bf16[256,20,128]{2,1,0:T(8,128)(2,1)S(1)} %copy-done.8), kind=kOutput, calls=%fused_computation.29 | convolution fusion | flops 340787200 | bytes 9195776 | tf_op jit(solution)/shard_map/hqk,khd->qhd/dot_general | solution.py:35
  197.7 3.7 %fusion.6 = f32[20,256]{1,0:T(8,128)S(1)} fusion(f32[20,256,256]{1,2,0:T(8,128)} %get-tuple-element.114, f32[20,256]{1,0:T(8,128)} %get-tuple-element.36, pred[256]{0:T(512)(128)(4,1)} %copy-done.46), kind=kLoop, calls=%fused_computation.26 | loop fusion | flops 5237760 | bytes 5284096 | tf_op jit(solution)/shard_map/reduce_sum | solution.py:34
  201.4 3.9 %fusion.8 = f32[20,128,256]{2,1,0:T(8,128)S(1)} fusion(f32[20,256,256]{1,2,0:T(8,128)} %get-tuple-element.114, f32[20,256]{1,0:T(8,128)S(1)} %copy-done.38, pred[256]{0:T(512)(128)(4,1)S(1)} %copy-done.47, bf16[256,20,128]{2,1,0:T(8,128)(2,1)S(1)} %copy-done.9), kind=kOutput, calls=%fused_computation.28 | convolution fusion | flops 340787200 | bytes 9195776 | tf_op jit(solution)/shard_map/hqk,khd->qhd/dot_general | solution.py:35
  (207 shorter events, 94.4 us)
Async XLA Ops:
  0.0 21.8 %copy-start.1 = (bf16[256,2560]{1,0:T(8,128)(2,1)S(1)}, bf16[256,2560]{1,0:T(8,128)(2,1)}, u32[]{:S(2)}) copy-start(bf16[256,2560]{1,0:T(8,128)(2,1)} %param.15) | copy-start | bytes 3932164
  25.1 4.1 %copy-start = (bf16[256,2560]{1,0:T(8,128)(2,1)S(1)}, bf16[256,2560]{1,0:T(8,128)(2,1)}, u32[]{:S(2)}) copy-start(bf16[256,2560]{1,0:T(8,128)(2,1)} %param.14) | copy-start | bytes 3932164
  26.8 137.9 %collective-permute-start.1 = (bf16[2,8,32,2560]{3,2,1,0:T(8,128)(2,1)}, bf16[2,8,32,2560]{3,2,1,0:T(8,128)(2,1)}, u32[]{:S(2)}, u32[]{:S(2)}) collective-permute-start(bf16[2,8,32,2560]{3,2,1,0:T(8,128)(2,1)} %pad_maximum_fusion.1), channel_id=1, source_target_pairs={{1,0},{2,1},{3,2},{4,3},{5,4},{6,5},{7,6},{8,7},{9,8},{10,9},{11,1... | collective-permute-start | bytes 7864328 | tf_op jit(solution)/shard_map/ppermute | solution.py:17
  36.5 135.3 %collective-permute-start = (bf16[2,8,32,2560]{3,2,1,0:T(8,128)(2,1)}, bf16[2,8,32,2560]{3,2,1,0:T(8,128)(2,1)}, u32[]{:S(2)}, u32[]{:S(2)}) collective-permute-start(bf16[2,8,32,2560]{3,2,1,0:T(8,128)(2,1)} %pad_maximum_fusion), channel_id=1, source_target_pairs={{0,1},{1,2},{2,3},{3,4},{4,5},{5,6},{6,7},{7,8},{8,9},{9,10},{10,1... | collective-permute-start | bytes 7864328 | tf_op jit(solution)/shard_map/ppermute | solution.py:17
  42.9 102.0 %collective-permute-start.3 = (bf16[2,4,32,2560]{3,2,1,0:T(8,128)(2,1)}, bf16[2,4,32,2560]{3,2,1,0:T(8,128)(2,1)}, u32[]{:S(2)}, u32[]{:S(2)}) collective-permute-start(bf16[2,4,32,2560]{3,2,1,0:T(8,128)(2,1)} %pad_maximum_fusion.3), channel_id=1, source_target_pairs={{2,0},{3,1},{4,2},{5,3},{6,4},{7,5},{8,6},{9,7},{10,8},{11,9},{12,... | collective-permute-start | bytes 3932168 | tf_op jit(solution)/shard_map/ppermute | solution.py:17
  53.5 96.1 %collective-permute-start.2 = (bf16[2,4,32,2560]{3,2,1,0:T(8,128)(2,1)}, bf16[2,4,32,2560]{3,2,1,0:T(8,128)(2,1)}, u32[]{:S(2)}, u32[]{:S(2)}) collective-permute-start(bf16[2,4,32,2560]{3,2,1,0:T(8,128)(2,1)} %pad_maximum_fusion.2), channel_id=1, source_target_pairs={{0,2},{1,3},{2,4},{3,5},{4,6},{5,7},{6,8},{7,9},{8,10},{9,11},{10,... | collective-permute-start | bytes 3932168 | tf_op jit(solution)/shard_map/ppermute | solution.py:17
  62.0 32.5 %collective-permute-start.7 = (bf16[2,1,32,2560]{3,2,1,0:T(8,128)(2,1)}, bf16[2,1,32,2560]{3,2,1,0:T(8,128)(2,1)}, u32[]{:S(2)}, u32[]{:S(2)}) collective-permute-start(bf16[2,1,32,2560]{3,2,1,0:T(8,128)(2,1)} %pad_maximum_fusion.7), channel_id=1, source_target_pairs={{8,0},{9,1},{10,2},{11,3},{12,4},{13,5},{14,6},{15,7},{24,16},{25,... | collective-permute-start | bytes 983048 | tf_op jit(solution)/shard_map/ppermute | solution.py:17
  70.0 5.3 %copy-start.19 = (bf16[2,32,2560]{2,1,0:T(8,128)(2,1)S(1)}, bf16[2,32,2560]{2,1,0:T(8,128)(2,1)}, u32[]{:S(2)}) copy-start(bf16[2,32,2560]{2,1,0:T(8,128)(2,1)} %gather_fusion.10) | copy-start | bytes 983044
  70.0 5.3 %copy-start.20 = (bf16[2,32,2560]{2,1,0:T(8,128)(2,1)S(1)}, bf16[2,32,2560]{2,1,0:T(8,128)(2,1)}, u32[]{:S(2)}) copy-start(bf16[2,32,2560]{2,1,0:T(8,128)(2,1)} %gather_fusion.11) | copy-start | bytes 983044
  74.0 108.3 %copy-start.46 = (pred[256]{0:T(512)(128)(4,1)}, pred[256]{0:T(512)(128)(4,1)S(1)}, u32[]{:S(2)}) copy-start(pred[256]{0:T(512)(128)(4,1)S(1)} %get-tuple-element.125) | copy-start | bytes 772
  75.3 4.6 %copy-start.11 = (bf16[256,2560]{0,1:T(8,128)(2,1)S(1)}, bf16[256,2560]{0,1:T(8,128)(2,1)}, u32[]{:S(2)}) copy-start(bf16[256,2560]{0,1:T(8,128)(2,1)} %copy.59) | copy-start | bytes 3932164
  79.9 3.2 %copy-start.22 = (bf16[1,1,32,2560]{3,2,1,0:T(8,128)(2,1)S(1)}, bf16[1,1,32,2560]{3,2,1,0:T(8,128)(2,1)}, u32[]{:S(2)}) copy-start(bf16[1,1,32,2560]{3,2,1,0:T(8,128)(2,1)} %get-tuple-element.61) | copy-start | bytes 491524
  94.5 6.0 %collective-permute-start.6 = (bf16[2,1,32,2560]{3,2,1,0:T(8,128)(2,1)S(1)}, bf16[2,1,32,2560]{3,2,1,0:T(8,128)(2,1)S(1)}, u32[]{:S(2)}, u32[]{:S(2)}) collective-permute-start(bf16[2,1,32,2560]{3,2,1,0:T(8,128)(2,1)S(1)} %pad_maximum_fusion.6), channel_id=1, source_target_pairs={{0,8},{1,9},{2,10},{3,11},{4,12},{5,13},{6,14},{7,15},{16,24},{17,... | collective-permute-start | bytes 983048 | tf_op jit(solution)/shard_map/ppermute | solution.py:17
  100.5 19.8 %collective-permute-start.5 = (bf16[2,2,32,2560]{3,2,1,0:T(8,128)(2,1)}, bf16[2,2,32,2560]{3,2,1,0:T(8,128)(2,1)}, u32[]{:S(2)}, u32[]{:S(2)}) collective-permute-start(bf16[2,2,32,2560]{3,2,1,0:T(8,128)(2,1)} %pad_maximum_fusion.5), channel_id=1, source_target_pairs={{4,0},{5,1},{6,2},{7,3},{8,4},{9,5},{10,6},{11,7},{12,8},{13,9},{1... | collective-permute-start | bytes 1966088 | tf_op jit(solution)/shard_map/ppermute | solution.py:17
  120.3 12.8 %collective-permute-start.4 = (bf16[2,2,32,2560]{3,2,1,0:T(8,128)(2,1)}, bf16[2,2,32,2560]{3,2,1,0:T(8,128)(2,1)}, u32[]{:S(2)}, u32[]{:S(2)}) collective-permute-start(bf16[2,2,32,2560]{3,2,1,0:T(8,128)(2,1)} %pad_maximum_fusion.4), channel_id=1, source_target_pairs={{0,4},{1,5},{2,6},{3,7},{4,8},{5,9},{6,10},{7,11},{8,12},{9,13},{1... | collective-permute-start | bytes 1966088 | tf_op jit(solution)/shard_map/ppermute | solution.py:17
  158.8 3.9 %copy-start.15 = (bf16[128,20,128]{2,1,0:T(8,128)(2,1)S(1)}, bf16[128,20,128]{2,1,0:T(8,128)(2,1)}, u32[]{:S(2)}) copy-start(bf16[128,20,128]{2,1,0:T(8,128)(2,1)} %reshape_reshape_squeeze.52) | copy-start | bytes 1966084
  182.3 5.2 %copy-start.7 = (bf16[256,20,128]{2,1,0:T(8,128)(2,1)S(1)}, bf16[256,20,128]{2,1,0:T(8,128)(2,1)}, u32[]{:S(2)}) copy-start(bf16[256,20,128]{2,1,0:T(8,128)(2,1)} %reshape_reshape_squeeze.48) | copy-start | bytes 3932164
  182.3 5.2 %copy-start.48 = (pred[256]{0:T(512)(128)(4,1)S(1)}, pred[256]{0:T(512)(128)(4,1)}, u32[]{:S(2)}) copy-start(pred[256]{0:T(512)(128)(4,1)} %get-tuple-element.126) | copy-start | bytes 772
  197.7 3.7 %copy-start.9 = (bf16[256,20,128]{2,1,0:T(8,128)(2,1)S(1)}, bf16[256,20,128]{2,1,0:T(8,128)(2,1)}, u32[]{:S(2)}) copy-start(bf16[256,20,128]{2,1,0:T(8,128)(2,1)} %reshape_reshape_squeeze.51) | copy-start | bytes 3932164
  197.7 3.7 %copy-start.38 = (f32[20,256]{1,0:T(8,128)S(1)}, f32[20,256]{1,0:T(8,128)}, u32[]{:S(2)}) copy-start(f32[20,256]{1,0:T(8,128)} %get-tuple-element.36) | copy-start | bytes 61444
  197.7 3.7 %copy-start.47 = (pred[256]{0:T(512)(128)(4,1)S(1)}, pred[256]{0:T(512)(128)(4,1)}, u32[]{:S(2)}) copy-start(pred[256]{0:T(512)(128)(4,1)} %copy-done.46) | copy-start | bytes 772
  201.4 4.0 %copy-start.3 = (f32[20,128,256]{2,1,0:T(8,128)S(1)}, f32[20,128,256]{2,1,0:T(8,128)}, u32[]{:S(2)}) copy-start(f32[20,128,256]{2,1,0:T(8,128)} %get-tuple-element.112) | copy-start | bytes 7864324
  201.4 4.0 %copy-start.24 = (f32[20,256]{1,0:T(8,128)S(1)}, f32[20,256]{1,0:T(8,128)}, u32[]{:S(2)}) copy-start(f32[20,256]{1,0:T(8,128)} %get-tuple-element.35) | copy-start | bytes 61444
  206.5 3.2 %slice-start = ((s8[5242880]{0:T(1024)(128)(4,1)}), s8[4194304]{0:T(1024)(128)(4,1)S(1)}, s32[]{:S(2)}) async-start(s8[5242880]{0:T(1024)(128)(4,1)} %bitcast.401), calls=%async_computation | async-start | bytes 8388608
  (35 other events, 54.5 us)
where the time goes:
time: 221 us; the launch traced here: 220 us
  local copies, waits for them, and re-layouts  67.7 us (31%)
  matrix products  36.2 us (16%)
  waiting for transfers between devices  32.4 us (15%)
  other arithmetic  31.7 us (14%)
  starting transfers between devices  27.9 us (13%)
  blocking collectives  19 us (9%)
  between operations  4.86 us (2%)
    ppermute x8, waiting for transfers between devices, from_behind(): return lax.ppermute(block, axis, route)  32.4 us
    ppermute x8, starting transfers between devices, from_behind(): return lax.ppermute(block, axis, route)  27.9 us
    dot_general x9, matrix products, attend(): jnp.einsum('qhd,khd->hqk', query_heads, key_heads, preferred_element_type...  22.7 us
    all_gather x1, blocking collectives, shards(): every_list = lax.all_gather(kv_lists, 'ctx', axis=0, tiled=True)  19 us
    another operation x16, other arithmetic, shards(): jnp.stack([jnp.take(key_blocks, wanted, axis=0), jnp.take(value_blocks, w...  15.7 us
    slice x8, local copies, waits for them, and re-layouts, shards(): far_values = arrived[1]  15.3 us
    another operation x8, local copies, waits for them, and re-layouts, attend(): key_heads = key_rows.reshape(key_rows.shape[0], head_count, head_size)  13.6 us
    dot_general x9, matrix products, attend(): jnp.einsum('hqk,khd->qhd', weights.astype(jnp.bfloat16), value_heads, pre...  13.6 us
  transfers between devices with their start and end apart: 8, of which 5 were waited for; matrix products, arithmetic and copies ran while one was open for 37% of the time, Pallas kernels for 0%

commit v1 on v0

v1 whole, which is shorter than its diff:
```python
import functools
import math

import jax
import jax.numpy as jnp
from jax import lax
from jax.experimental import pallas as pl
from jax.experimental.pallas import tpu as pltpu
from jax.sharding import PartitionSpec as P

HEAD = 128
UNROLL = 20
MASKED = -1e30
F32 = jnp.float32
BF16 = jnp.bfloat16
VMEM = 16 * 1024 * 1024
COST = pl.CostEstimate(flops=1000, bytes_accessed=1000, transcendentals=0)


def permute(block, count, route):
    pairs = [(a, b) for a, b in route if 0 <= a < count and 0 <= b < count]
    return lax.ppermute(block, "ctx", pairs)


def listed(lists, device, level, side, j, shape):
    device = jnp.clip(device, 0, shape["devices"] - 1)
    return lists[device, (level * 2 + side) * shape["blocks"] + j]


def others(found, lists, device, side, shape):
    blocks = shape["blocks"]
    half = blocks // 2
    names = [listed(lists, device, 1, side, j, shape) for j in range(half)]
    place = jnp.int32(0)
    for b in range(blocks):
        named = functools.reduce(jnp.logical_or, [n == b for n in names])
        found[place] = jnp.int32(b)
        place = place + jnp.where(named, 0, 1)


def rows_at(ref, block, rows):
    return ref.at[pl.ds(pl.multiple_of(block * rows, rows), rows)]


class Copies:
    def __init__(self, sems):
        self.sems = sems
        self.started = []

    def start(self, source, target):
        copy = pltpu.make_async_copy(source, target, self.sems.at[len(self.started)])
        copy.start()
        self.started.append(copy)

    def wait(self):
        for copy in self.started:
            copy.wait()


def first_pack(shape, lists, keys, values, second, along, *rest):
    far = rest[: -2]
    found, sems = rest[-2:]
    rows = shape["rows"]
    half = shape["blocks"] // 2
    me = lax.axis_index("ctx")
    spot = me % 4
    outer = jnp.logical_or(spot == 0, spot == 3)

    def gather(copies, target, names):
        n = len(names)
        for j, name in enumerate(names):
            copies.start(rows_at(keys, name, rows), target.at[pl.ds(j * rows, rows)])
            copies.start(rows_at(values, name, rows), target.at[pl.ds((n + j) * rows, rows)])

    reader = jnp.where(spot == 0, me + 2, me - 2)
    side = jnp.where(spot == 0, 0, 1)
    others(found, lists, reader, side, shape)
    copies = Copies(sems)
    at = 0
    for level in range(2, shape["levels"]):
        for way in range(2):
            device = me + (1 << level) * (1 - 2 * way)
            capacity = shape["blocks"] >> level
            gather(copies, far[at], [listed(lists, device, level, way, j, shape) for j in range(capacity)])
            at += 1

    @pl.when(outer)
    def _():
        more = Copies(sems.at[pl.ds(len(copies.started), 4 * half)])
        gather(more, along, [found[j] for j in range(half)])
        gather(more, second, [listed(lists, reader, 1, side, j, shape) for j in range(half)])
        more.wait()

    @pl.when(jnp.logical_not(outer))
    def _():
        copy = pltpu.make_async_copy(values, second, sems.at[len(copies.started)])
        copy.start()
        copy.wait()

    copies.wait()


def second_pack(shape, lists, keys, values, along, across, third, sems):
    rows = shape["rows"]
    half = shape["blocks"] // 2
    me = lax.axis_index("ctx")
    spot = me % 4
    outer = jnp.logical_or(spot == 0, spot == 3)

    @pl.when(outer)
    def _():
        copies = Copies(sems)
        copies.start(values, across)
        copies.start(along, third)
        copies.wait()

    @pl.when(jnp.logical_not(outer))
    def _():
        copies = Copies(sems)
        near = jnp.where(spot == 1, me - 1, me + 1)
        far = jnp.where(spot == 1, me + 3, me - 3)
        near_side = jnp.where(spot == 1, 1, 0)
        far_side = jnp.where(spot == 1, 0, 1)
        for target, device, side in ((third, far, far_side), (across, near, near_side)):
            for j in range(half):
                name = listed(lists, device, 1, side, j, shape)
                copies.start(rows_at(keys, name, rows), target.at[pl.ds(j * rows, rows)])
                copies.start(rows_at(values, name, rows), target.at[pl.ds((half + j) * rows, rows)])
        copies.wait()


def pack_call(body, shape, lists, arrays, out_rows, scratch, copies):
    width = shape["width"]
    outs = tuple(jax.ShapeDtypeStruct((r, width), BF16) for r in out_rows)
    return pl.pallas_call(
        functools.partial(body, shape),
        out_shape=outs,
        in_specs=[pl.BlockSpec(memory_space=pltpu.SMEM)] + [pl.BlockSpec(memory_space=pltpu.HBM)] * len(arrays),
        out_specs=tuple([pl.BlockSpec(memory_space=pltpu.VMEM)] * len(outs)),
        scratch_shapes=scratch + [pltpu.SemaphoreType.DMA((copies,))],
        cost_estimate=COST,
        compiler_params=pltpu.CompilerParams(vmem_limit_bytes=VMEM),
    )(lists, *arrays)


def lanes(column, n):
    wide = jnp.concatenate([column] * -(-n // column.shape[1]), axis=1)
    return wide[:, :n]


def attend(query, state, keys, values, masks):
    scale = math.log2(math.e) / math.sqrt(HEAD)
    raw = lax.dot_general(query, keys, (((1,), (1,)), ((), ())), preferred_element_type=F32)
    scores = []
    at = 0
    for n, mask in masks:
        part = raw[:, at : at + n] * scale
        scores.append(part if mask is None else part + mask)
        at += n
    scores = scores[0] if len(scores) == 1 else jnp.concatenate(scores, axis=1)
    best = jnp.broadcast_to(jnp.max(scores, axis=1, keepdims=True), query.shape)
    if state is not None:
        best = jnp.maximum(best, state[0])
    weights = jnp.exp2(scores - lanes(best, scores.shape[1])).astype(BF16)
    both = jnp.dot(weights, jnp.concatenate([values, jnp.ones_like(values)], axis=1), preferred_element_type=F32)
    weighted, total = both[:, :HEAD], both[:, HEAD:]
    if state is not None:
        factor = jnp.exp2(state[0] - best)
        total = total + state[1] * factor
        weighted = weighted + state[2] * factor
    return best, total, weighted


def member_flags(flags, at, ids, lists, counts, me, level, side, shape):
    counted = counts[0, level, side]
    names = [listed(lists, me, level, side, j, shape) for j in range(shape["blocks"] >> level)]
    for n, b in enumerate(ids):
        seen = functools.reduce(
            jnp.logical_or, [jnp.logical_and(j < counted, name == b) for j, name in enumerate(names)]
        )
        flags[at + n] = jnp.where(seen, 0.0, MASKED).astype(F32)


def order_flags(flags, at, capacity, counts, level, side):
    counted = counts[0, level, side]
    for j in range(capacity):
        flags[at + j] = jnp.where(j < counted, 0.0, MASKED).astype(F32)


def spread(flags, at, count, rows):
    place = lax.broadcasted_iota(jnp.int32, (1, count * rows), 1)
    row = jnp.full((1, count * rows), flags[at], F32)
    for b in range(1, count):
        row = jnp.where(place >= b * rows, flags[at + b], row)
    return row


def over_heads(width, body):
    def step(h, _):
        body(pl.ds(pl.multiple_of(h * HEAD, HEAD), HEAD))
        return 0

    lax.fori_loop(0, width // HEAD, step, 0, unroll=math.gcd(UNROLL, width // HEAD))


def load_state(refs, c):
    return tuple(ref[:, c] for ref in refs)


def store_state(refs, c, state):
    for ref, part in zip(refs, state):
        ref[:, c] = part


def near_kernel(shape, lists, counts, q, k, v, ak, av, best, total, weighted, flags):
    me = lax.axis_index("ctx")
    blocks = shape["blocks"]
    member_flags(flags, 0, range(blocks), lists, counts, me, 0, 1 - me % 2, shape)
    mask = spread(flags, 0, blocks, shape["rows"])

    def head(c):
        keys = jnp.concatenate([k[:, c], ak[:, c]], axis=0)
        values = jnp.concatenate([v[:, c], av[:, c]], axis=0)
        state = attend(q[:, c], None, keys, values, [(k.shape[0], None), (ak.shape[0], mask)])
        store_state((best, total, weighted), c, state)

    over_heads(shape["width"], head)


def packed(refs, c, filler=0):
    keys = [ref[: ref.shape[0] // 2, c] for ref in refs]
    values = [ref[ref.shape[0] // 2 :, c] for ref in refs]
    if filler:
        keys.append(jnp.zeros((filler, HEAD), BF16))
        values.append(jnp.zeros((filler, HEAD), BF16))
    return jnp.concatenate(keys, axis=0), jnp.concatenate(values, axis=0)


def listed_kernel(shape, sides, lists, counts, q, *refs):
    n = len(sides)
    sources, before, after, flags = refs[:n], refs[n : n + 3], refs[n + 3 : n + 6], refs[-1]
    me = lax.axis_index("ctx")
    at = 0
    for level, side in sides:
        capacity = shape["blocks"] >> level
        order_flags(flags, at, capacity, counts, level, side(me))
        at += capacity
    rows = shape["rows"]
    filler = -at % shape["blocks"]
    for b in range(filler):
        flags[at + b] = jnp.float32(MASKED)
    mask = spread(flags, 0, at + filler, rows)

    def head(c):
        keys, values = packed(sources, c, filler * rows)
        store_state(after, c, attend(q[:, c], load_state(before, c), keys, values, [(keys.shape[0], mask)]))

    over_heads(shape["width"], head)


def giver_ids(found, lists, device, side, shape):
    half = shape["blocks"] // 2
    others(found, lists, device, side, shape)
    return [listed(lists, device, 1, side, j, shape) for j in range(half)] + [found[j] for j in range(half)]


def full_kernel(shape, lists, counts, q, zeroth, second, third, fourth, *refs):
    before, after, flags, found = refs[:3], refs[3:6], refs[6], refs[7]
    me = lax.axis_index("ctx")
    spot = me % 4
    blocks = shape["blocks"]
    outer = jnp.logical_or(spot == 0, spot == 3)
    ids = giver_ids(found, lists, jnp.where(spot == 0, me - 3, me + 3), jnp.where(spot == 0, 1, 0), shape)
    ids = [jnp.where(outer, name, b) for b, name in enumerate(ids)]
    member_flags(flags, 0, ids, lists, counts, me, 0, me % 2, shape)

    def head(c, keys, values):
        mask = spread(flags, 0, blocks, shape["rows"])
        store_state(after, c, attend(q[:, c], load_state(before, c), keys, values, [(keys.shape[0], mask)]))

    @pl.when(outer)
    def _():
        over_heads(shape["width"], lambda c: head(c, *packed([fourth, third], c)))

    @pl.when(jnp.logical_not(outer))
    def _():
        over_heads(shape["width"], lambda c: head(c, zeroth[:, c], second[:, c]))


def last_kernel(shape, lists, counts, q, fourth, third, *refs):
    before, out, flags, found = refs[:3], refs[3], refs[4], refs[5]
    me = lax.axis_index("ctx")
    spot = me % 4
    blocks = shape["blocks"]
    half = blocks // 2
    outer = jnp.logical_or(spot == 0, spot == 3)
    side = jnp.where(spot < 2, 0, 1)

    @pl.when(outer)
    def _():
        for j in range(half):
            flags[j] = jnp.float32(MASKED)
        order_flags(flags, half, half, counts, 1, side)

    @pl.when(jnp.logical_not(outer))
    def _():
        ids = giver_ids(found, lists, jnp.where(spot == 1, me - 4, me + 4), jnp.where(spot == 1, 1, 0), shape)
        member_flags(flags, 0, ids, lists, counts, me, 1, side, shape)

    mask = spread(flags, 0, blocks, shape["rows"])

    def head(c):
        keys, values = packed([fourth, third], c)
        _, total, weighted = attend(q[:, c], load_state(before, c), keys, values, [(keys.shape[0], mask)])
        out[:, c] = (weighted / total).astype(BF16)

    over_heads(shape["width"], head)


def attend_call(body, shape, lists, counts, arrays, state, last, scratch, blocks_seen):
    queries, width = arrays[0].shape
    smem = pl.BlockSpec(memory_space=pltpu.SMEM)
    vmem = pl.BlockSpec(memory_space=pltpu.VMEM)
    return pl.pallas_call(
        functools.partial(body, shape),
        out_shape=jax.ShapeDtypeStruct((queries, width), BF16)
        if last
        else tuple([jax.ShapeDtypeStruct((queries, width), F32)] * 3),
        in_specs=[smem, smem] + [vmem] * (len(arrays) + len(state)),
        out_specs=vmem if last else tuple([vmem] * 3),
        scratch_shapes=[pltpu.SMEM((shape["blocks"] * 4,), F32)] + scratch,
        cost_estimate=COST,
        compiler_params=pltpu.CompilerParams(vmem_limit_bytes=VMEM),
    )(lists, counts, *arrays, *state)


def shards(queries, keys, values, kv_lists, kv_counts):
    row_count, width = queries.shape
    blocks = kv_lists.shape[3]
    levels = kv_lists.shape[1]
    devices = lax.axis_size("ctx")
    half = blocks // 2
    rows = row_count // blocks
    shape = {
        "devices": devices,
        "blocks": blocks,
        "levels": levels,
        "rows": rows,
        "width": width,
    }
    every = range(devices)
    spot = {i: [d for d in every if d % 4 == i] for i in range(4)}
    other_core = [(d, d ^ 1) for d in every]
    inner_swap = [(d, d ^ 3) for d in spot[1] + spot[2]]
    outer_swap = [(d, d ^ 3) for d in spot[0] + spot[3]]
    outer_along = [(d, d + 4) for d in spot[3]] + [(d, d - 4) for d in spot[0]]
    outer_on = [(d, d + 4) for d in spot[0]] + [(d, d - 4) for d in spot[3]]
    outer_in = [(d, d ^ 1) for d in spot[0] + spot[3]]
    inner_on = [(d, d + 4) for d in spot[1]] + [(d, d - 4) for d in spot[2]]

    zeroth = permute(keys, devices, inner_swap)
    sent = jnp.broadcast_to(kv_lists.reshape(1, -1), (devices, levels * 2 * blocks))
    lists = lax.all_to_all(sent, "ctx", 0, 0, tiled=True)

    far_levels = [(level, way) for level in range(2, levels) for way in range(2)]
    far_rows = [2 * (blocks >> level) * rows for level, _ in far_levels]
    packs = pack_call(
        first_pack,
        shape,
        lists,
        (keys, values),
        [row_count, row_count] + far_rows,
        [pltpu.SMEM((blocks + 1,), jnp.int32)],
        4 * half + sum(2 * (blocks >> level) for level, _ in far_levels),
    )
    along = permute(packs[1], devices, outer_along)
    second = permute(packs[0], devices, inner_swap + outer_swap)
    far = []
    for (level, way), pack in zip(far_levels, packs[2:]):
        step = (1 << level) * (1 - 2 * way)
        far.append(permute(pack, devices, [(d, d + step) for d in every]))
    other_keys = permute(keys, devices, other_core)
    other_values = permute(values, devices, other_core)

    state = attend_call(
        near_kernel, shape, lists, kv_counts, (queries, keys, values, other_keys, other_values), (), False, [], 2 * blocks
    )

    fourth = permute(second, devices, outer_on)
    across, third_out = pack_call(
        second_pack, shape, lists, (zeroth, second, along), [row_count, row_count], [], 4 * half
    )
    third = permute(third_out, devices, inner_on + outer_swap)
    middle = permute(across, devices, other_core)

    sides = [(1, lambda me: jnp.where(me % 4 < 2, 1, 0))]
    sides += [(level, lambda me, way=way: way) for level, way in far_levels]
    state = attend_call(
        functools.partial(rename, listed_kernel, sides),
        shape,
        lists,
        kv_counts,
        (queries, middle, *far),
        state,
        False,
        [],
        half + sum(blocks >> level for level, _ in far_levels),
    )
    handed = permute(third, devices, other_core)
    handed_fourth = permute(fourth, devices, outer_in)
    state = attend_call(
        full_kernel,
        shape,
        lists,
        kv_counts,
        (queries, zeroth, second, third, fourth),
        state,
        False,
        [pltpu.SMEM((blocks + 1,), jnp.int32)],
        blocks,
    )
    return attend_call(
        last_kernel,
        shape,
        lists,
        kv_counts,
        (queries, handed_fourth, handed),
        state,
        True,
        [pltpu.SMEM((blocks + 1,), jnp.int32)],
        blocks,
    )


def rename(body, sides, shape, *refs):
    return body(shape, sides, *refs)


def solution(mesh):
    in_specs = (
        P(("groups", "ctx"), None),
        P(("groups", "ctx"), None),
        P(("groups", "ctx"), None),
        P("ctx", None, None, None),
        P("ctx", None, None),
    )
    out_specs = P(("groups", "ctx"), None)
    return jax.shard_map(shards, mesh=mesh, in_specs=in_specs, out_specs=out_specs, check_vma=False)
```

time: 221 us -> 162 us (0.73)
  the two profiles are of different devices: /device:TPU:8 before, /device:TPU:0 now
where the time goes in v1:
time: 162 us; the launch traced here: 161 us
  waiting for transfers between devices  87.9 us (54%)
  Pallas kernels  30.1 us (19%)
  starting transfers between devices  29.9 us (18%)
  local copies, waits for them, and re-layouts  13.1 us (8%)
    ppermute x14, waiting for transfers between devices, permute(): return lax.ppermute(block, 'ctx', pairs)  82.3 us
    ppermute x14, starting transfers between devices, permute(): return lax.ppermute(block, 'ctx', pairs)  22.5 us
    pallas_call x4, Pallas kernels, attend_call(): pl.pallas_call(functools.partial(body, shape), out_shape=jax.ShapeDtypeSt...  20 us
    unnamed x37, local copies, waits for them, and re-layouts  11.7 us
    pallas_call x2, Pallas kernels, pack_call(): pl.pallas_call(functools.partial(body, shape), out_shape=outs, in_specs=[...  10.1 us
    all_to_all x1, starting transfers between devices, shards(): lists = lax.all_to_all(sent, 'ctx', 0, 0, tiled=True)  7.39 us
    all_to_all x1, waiting for transfers between devices, shards(): lists = lax.all_to_all(sent, 'ctx', 0, 0, tiled=True)  5.58 us
  transfers between devices with their start and end apart: 15, of which 6 were waited for; matrix products, arithmetic and copies ran while one was open for 0% of the time, Pallas kernels for 14%

profile of v1, /device:TPU:0, one launch (start us, length us, event | category | flops | bytes accessed | tf_op | source)
XLA Modules:
  0.0 161.2 jit_solution(14304396867153767645)
XLA Ops:
  1.4 7.4 %all-to-all-start = ((s32[16,1,64]{2,1,0:T(1,128)}), s32[16,1,64]{2,1,0:T(1,128)S(1)}, u32[]{:S(2)}, u32[]{:S(2)}) async-start(s32[16,1,64]{2,1,0:T(1,128)} %broadcast_in_dim.8), calls=%async_computation | async-start | bytes 16384 | tf_op jit(solution)/shard_map/all_to_all | solution.py:363
  9.5 5.6 %all-to-all-done = s32[16,1,64]{2,1,0:T(1,128)S(1)} async-done(((s32[16,1,64]{2,1,0:T(1,128)}), s32[16,1,64]{2,1,0:T(1,128)S(1)}, u32[]{:S(2)}, u32[]{:S(2)}) %all-to-all-start) | async-done | bytes 4128 | tf_op jit(solution)/shard_map/all_to_all | solution.py:363
  15.1 1.3 copy-done.3
  16.4 1.3 copy-done.6
  17.7 8.0 %shard_map.55 = (bf16[256,2560]{1,0:T(8,128)(2,1)S(1)}, bf16[256,2560]{1,0:T(8,128)(2,1)S(1)}, bf16[128,2560]{1,0:T(8,128)(2,1)}, bf16[128,2560]{1,0:T(8,128)(2,...) custom-call(s32[16,64]{1,0:T(8,128)S(1)} %bitcast.1, bf16[256,2560]{1,0:T(8,128)(2,1)S(1)} %copy-done.3, ...), custom_call_target="tpu_custom_call" | custom-call | flops 1000 | bytes 1000 | tf_op jit(solution)/shard_map/pallas_call | solution.py:135
  25.9 1.6 collective-permute-start.4
  27.5 29.1 %collective-permute-done.values.second = bf16[256,2560]{1,0:T(8,128)(2,1)S(1)} collective-permute-done((bf16[256,2560]{1,0:T(8,128)(2,1)S(1)}, bf16[256,2560]{1,0:T(8,128)(2,1)S(1)}, u32[]{:S(2)}, u32[]{:S(2)}) %collective-permute-start) | collective-permute-done | bytes 1310752 | tf_op jit(solution)/shard_map/ppermute | solution.py:22
  56.6 2.1 %shard_map.56 = (bf16[256,2560]{1,0:T(8,128)(2,1)}, bf16[256,2560]{1,0:T(8,128)(2,1)S(1)}) custom-call(s32[16,64]{1,0:T(8,128)S(1)} %bitcast.2, bf16[256,2560]{1,0:T(8,128)(2,1)S(1)} %collective-permute-done.3.keys.zeroth, bf16[256,2560]{1,0:T(8,128)(2,1)S(1)} %collective-permute-done.values.second, bf16[256,2560]{1,0:T(8,128)(2,1)S(1)} %collective-permute-done.4.along), custom_call_target="tpu_custom_call" | custom-call | flops 1000 | bytes 1000 | tf_op jit(solution)/shard_map/pallas_call | solution.py:135
  58.7 2.6 %collective-permute-start.5 = (bf16[256,2560]{1,0:T(8,128)(2,1)S(1)}, bf16[256,2560]{1,0:T(8,128)(2,1)}, u32[]{:S(2)}, u32[]{:S(2)}) collective-permute-start(bf16[256,2560]{1,0:T(8,128)(2,1)S(1)} %get-tuple-element.24), channel_id=1, source_target_pairs={{1,5},{5,9},{9,13},{6,2},{10,6},{14,10},{0,3},{4,7},{8,11},{12,15}... | collective-permute-start | bytes 3932168 | tf_op jit(solution)/shard_map/ppermute | solution.py:22
  61.3 3.5 %collective-permute-start.1 = (bf16[256,2560]{1,0:T(8,128)(2,1)S(1)}, bf16[256,2560]{1,0:T(8,128)(2,1)}, u32[]{:S(2)}, u32[]{:S(2)}) collective-permute-start(bf16[256,2560]{1,0:T(8,128)(2,1)S(1)} %collective-permute-done.values.second), channel_id=1, source_target_pairs={{0,4},{4,8},{8,12},{7,3},{11,7},{15,11},{16,20},{20,24},{24,28},{2... | collective-permute-start | bytes 3932168 | tf_op jit(solution)/shard_map/ppermute | solution.py:22
  64.8 3.1 %collective-permute-start.12 = (bf16[256,2560]{1,0:T(8,128)(2,1)S(1)}, bf16[256,2560]{1,0:T(8,128)(2,1)S(1)}, u32[]{:S(2)}, u32[]{:S(2)}) collective-permute-start(bf16[256,2560]{1,0:T(8,128)(2,1)S(1)} %copy-done.4), channel_id=1, source_target_pairs={{0,1},{1,0},{2,3},{3,2},{4,5},{5,4},{6,7},{7,6},{8,9},{9,8},{10,11... | collective-permute-start | bytes 3932168 | tf_op jit(solution)/shard_map/ppermute | solution.py:22
  67.9 3.2 %collective-permute-start.10 = (bf16[64,2560]{1,0:T(8,128)(2,1)S(1)}, bf16[64,2560]{1,0:T(8,128)(2,1)S(1)}, u32[]{:S(2)}, u32[]{:S(2)}) collective-permute-start(bf16[64,2560]{1,0:T(8,128)(2,1)S(1)} %get-tuple-element.28), channel_id=1, source_target_pairs={{0,8},{1,9},{2,10},{3,11},{4,12},{5,13},{6,14},{7,15},{16,24},{17,... | collective-permute-start | bytes 983048 | tf_op jit(solution)/shard_map/ppermute | solution.py:22
  71.2 28.1 %collective-permute-done.10.refs_6_ = bf16[64,2560]{1,0:T(8,128)(2,1)S(1)} collective-permute-done((bf16[64,2560]{1,0:T(8,128)(2,1)S(1)}, bf16[64,2560]{1,0:T(8,128)(2,1)S(1)}, u32[]{:S(2)}, u32[]{:S(2)}) %collective-permute-start.10) | collective-permute-done | bytes 327712 | tf_op jit(solution)/shard_map/ppermute | solution.py:22
  101.4 18.9 %collective-permute-done.11.refs_7_ = bf16[64,2560]{1,0:T(8,128)(2,1)S(1)} collective-permute-done((bf16[64,2560]{1,0:T(8,128)(2,1)S(1)}, bf16[64,2560]{1,0:T(8,128)(2,1)S(1)}, u32[]{:S(2)}, u32[]{:S(2)}) %collective-permute-start.11) | collective-permute-done | bytes 327712 | tf_op jit(solution)/shard_map/ppermute | solution.py:22
  121.5 3.0 %collective-permute-start.2 = (bf16[256,2560]{1,0:T(8,128)(2,1)}, bf16[256,2560]{1,0:T(8,128)(2,1)}, u32[]{:S(2)}, u32[]{:S(2)}) collective-permute-start(bf16[256,2560]{1,0:T(8,128)(2,1)} %collective-permute-done.1.fourth), channel_id=1, source_target_pairs={{0,1},{4,5},{8,9},{12,13},{3,2},{7,6},{11,10},{15,14},{16,17},{20,... | collective-permute-start | bytes 3932168 | tf_op jit(solution)/shard_map/ppermute | solution.py:22
  125.6 1.6 collective-permute-start.8
  129.7 1.3 copy-done.5
  131.1 1.3 copy-done.8
  132.4 1.3 copy-done.10
  135.0 4.0 %shard_map.57 = (f32[256,2560]{1,0:T(8,128)S(1)}, f32[256,2560]{1,0:T(8,128)S(1)}, f32[256,2560]{1,0:T(8,128)S(1)}) custom-call(s32[16,64]{1,0:T(8,128)S(1)} %bitcast.3, s32[1,4,2]{2,1,0:T(4,128)S(1)} %copy.13.counts.refs_1_, bf16[256,2560]{1,0:T(8,128)(2,1)S(1)} %copy-done, bf16[256,2560]{1,0:T(8,128)(2,1)S(1)} %copy-done.5, ...), custom_call_target="tpu_custom_call" | custom-call | flops 1000 | bytes 1000 | tf_op jit(solution)/shard_map/pallas_call | solution.py:324
  140.0 5.2 %collective-permute-done.9.refs_5_ = bf16[128,2560]{1,0:T(8,128)(2,1)} collective-permute-done((bf16[128,2560]{1,0:T(8,128)(2,1)}, bf16[128,2560]{1,0:T(8,128)(2,1)}, u32[]{:S(2)}, u32[]{:S(2)}) %collective-permute-start.9) | collective-permute-done | bytes 655392 | tf_op jit(solution)/shard_map/ppermute | solution.py:22
  145.2 6.5 %shard_map.58 = (f32[256,2560]{1,0:T(8,128)S(1)}, f32[256,2560]{1,0:T(8,128)S(1)}, f32[256,2560]{1,0:T(8,128)S(1)}) custom-call(s32[16,64]{1,0:T(8,128)S(1)} %bitcast.4, s32[1,4,2]{2,1,0:T(4,128)S(1)} %copy.13.counts.refs_1_, bf16[256,2560]{1,0:T(8,128)(2,1)S(1)} %copy-done, bf16[256,2560]{1,0:T(8,128)(2,1)} %collective-permute-done.7.refs_3_, ...), custom_call_target="tpu_custom_call" | custom-call | flops 1000 | bytes 1000 | tf_op jit(solution)/shard_map/pallas_call | solution.py:324
  151.7 4.3 %shard_map.59 = (f32[256,2560]{1,0:T(8,128)S(1)}, f32[256,2560]{1,0:T(8,128)S(1)}, f32[256,2560]{1,0:T(8,128)S(1)}) custom-call(s32[16,64]{1,0:T(8,128)S(1)} %bitcast.5, s32[1,4,2]{2,1,0:T(4,128)S(1)} %copy.13.counts.refs_1_, bf16[256,2560]{1,0:T(8,128)(2,1)S(1)} %copy-done, bf16[256,2560]{1,0:T(8,128)(2,1)S(1)} %collective-permute-done.3.keys.zeroth, ...), custom_call_target="tpu_custom_call" | custom-call | flops 1000 | bytes 1000 | tf_op jit(solution)/shard_map/pallas_call | solution.py:324
  156.1 5.2 %shard_map.60 = bf16[256,2560]{1,0:T(8,128)(2,1)} custom-call(s32[16,64]{1,0:T(8,128)S(1)} %bitcast.6, s32[1,4,2]{2,1,0:T(4,128)S(1)} %copy.13.counts.refs_1_, bf16[256,2560]{1,0:T(8,128)(2,1)S(1)} %copy-done, bf16[256,2560]{1,0:T(8,128)(2,1)} %collective-permute-done.2.fourth, bf16[256,2560]{1,0:T(8,128)(2,1)} %collective-permute-done.6.third, ...), custom_call_target="tpu_custom_call" | custom-call | flops 1000 | bytes 1000 | tf_op jit(solution)/shard_map/pallas_call | solution.py:324
  (51 shorter events, 11.4 us)
Async XLA Ops:
  1.4 13.7 %all-to-all-start = ((s32[16,1,64]{2,1,0:T(1,128)}), s32[16,1,64]{2,1,0:T(1,128)S(1)}, u32[]{:S(2)}, u32[]{:S(2)}) async-start(s32[16,1,64]{2,1,0:T(1,128)} %broadcast_in_dim.8), calls=%async_computation | async-start | bytes 16384 | tf_op jit(solution)/shard_map/all_to_all | solution.py:363
  8.8 18.7 %collective-permute-start.3 = (bf16[256,2560]{1,0:T(8,128)(2,1)}, bf16[256,2560]{1,0:T(8,128)(2,1)S(1)}, u32[]{:S(2)}, u32[]{:S(2)}) collective-permute-start(bf16[256,2560]{1,0:T(8,128)(2,1)} %k.1), channel_id=1, source_target_pairs={{1,2},{5,6},{9,10},{13,14},{2,1},{6,5},{10,9},{14,13},{17,18},{21,... | collective-permute-start | bytes 3932168 | tf_op jit(solution)/shard_map/ppermute | solution.py:22
  25.8 30.8 %collective-permute-start = (bf16[256,2560]{1,0:T(8,128)(2,1)S(1)}, bf16[256,2560]{1,0:T(8,128)(2,1)S(1)}, u32[]{:S(2)}, u32[]{:S(2)}) collective-permute-start(bf16[256,2560]{1,0:T(8,128)(2,1)S(1)} %get-tuple-element.22), channel_id=1, source_target_pairs={{1,2},{5,6},{9,10},{13,14},{2,1},{6,5},{10,9},{14,13},{0,3},{4,7},... | collective-permute-start | bytes 3932168 | tf_op jit(solution)/shard_map/ppermute | solution.py:22
  25.8 38.9 %copy-start.4 = (bf16[256,2560]{1,0:T(8,128)(2,1)S(1)}, bf16[256,2560]{1,0:T(8,128)(2,1)}, u32[]{:S(2)}) copy-start(bf16[256,2560]{1,0:T(8,128)(2,1)} %k.1) | copy-start | bytes 3932164
  25.8 45.3 %copy-start.7 = (bf16[256,2560]{1,0:T(8,128)(2,1)S(1)}, bf16[256,2560]{1,0:T(8,128)(2,1)}, u32[]{:S(2)}) copy-start(bf16[256,2560]{1,0:T(8,128)(2,1)} %v.1) | copy-start | bytes 3932164
  25.9 103.8 %copy-start.17 = (s32[1,4,2]{1,2,0:T(2,128)S(1)}, s32[1,4,2]{1,2,0:T(2,128)}, u32[]{:S(2)}) copy-start(s32[1,4,2]{1,2,0:T(2,128)} %param.9) | copy-start | bytes 100
  25.9 103.9 %copy-start = (bf16[256,2560]{1,0:T(8,128)(2,1)S(1)}, bf16[256,2560]{1,0:T(8,128)(2,1)}, u32[]{:S(2)}) copy-start(bf16[256,2560]{1,0:T(8,128)(2,1)} %q.5) | copy-start | bytes 3932164
  25.9 30.7 %collective-permute-start.4 = (bf16[256,2560]{1,0:T(8,128)(2,1)S(1)}, bf16[256,2560]{1,0:T(8,128)(2,1)S(1)}, u32[]{:S(2)}, u32[]{:S(2)}) collective-permute-start(bf16[256,2560]{1,0:T(8,128)(2,1)S(1)} %get-tuple-element.23), channel_id=1, source_target_pairs={{3,7},{7,11},{11,15},{4,0},{8,4},{12,8},{19,23},{23,27},{27,31},{2... | collective-permute-start | bytes 3932168 | tf_op jit(solution)/shard_map/ppermute | solution.py:22
  56.6 4.7 %copy-start.1 = (bf16[256,2560]{1,0:T(8,128)(2,1)}, bf16[256,2560]{1,0:T(8,128)(2,1)S(1)}, u32[]{:S(2)}) copy-start(bf16[256,2560]{1,0:T(8,128)(2,1)S(1)} %collective-permute-done.values.second) | copy-start | bytes 3932164
  58.7 62.3 %collective-permute-start.5 = (bf16[256,2560]{1,0:T(8,128)(2,1)S(1)}, bf16[256,2560]{1,0:T(8,128)(2,1)}, u32[]{:S(2)}, u32[]{:S(2)}) collective-permute-start(bf16[256,2560]{1,0:T(8,128)(2,1)S(1)} %get-tuple-element.24), channel_id=1, source_target_pairs={{1,5},{5,9},{9,13},{6,2},{10,6},{14,10},{0,3},{4,7},{8,11},{12,15}... | collective-permute-start | bytes 3932168 | tf_op jit(solution)/shard_map/ppermute | solution.py:22
  61.3 60.2 %collective-permute-start.1 = (bf16[256,2560]{1,0:T(8,128)(2,1)S(1)}, bf16[256,2560]{1,0:T(8,128)(2,1)}, u32[]{:S(2)}, u32[]{:S(2)}) collective-permute-start(bf16[256,2560]{1,0:T(8,128)(2,1)S(1)} %collective-permute-done.values.second), channel_id=1, source_target_pairs={{0,4},{4,8},{8,12},{7,3},{11,7},{15,11},{16,20},{20,24},{24,28},{2... | collective-permute-start | bytes 3932168 | tf_op jit(solution)/shard_map/ppermute | solution.py:22
  64.8 59.7 %collective-permute-start.12 = (bf16[256,2560]{1,0:T(8,128)(2,1)S(1)}, bf16[256,2560]{1,0:T(8,128)(2,1)S(1)}, u32[]{:S(2)}, u32[]{:S(2)}) collective-permute-start(bf16[256,2560]{1,0:T(8,128)(2,1)S(1)} %copy-done.4), channel_id=1, source_target_pairs={{0,1},{1,0},{2,3},{3,2},{4,5},{5,4},{6,7},{7,6},{8,9},{9,8},{10,11... | collective-permute-start | bytes 3932168 | tf_op jit(solution)/shard_map/ppermute | solution.py:22
  67.9 31.4 %collective-permute-start.10 = (bf16[64,2560]{1,0:T(8,128)(2,1)S(1)}, bf16[64,2560]{1,0:T(8,128)(2,1)S(1)}, u32[]{:S(2)}, u32[]{:S(2)}) collective-permute-start(bf16[64,2560]{1,0:T(8,128)(2,1)S(1)} %get-tuple-element.28), channel_id=1, source_target_pairs={{0,8},{1,9},{2,10},{3,11},{4,12},{5,13},{6,14},{7,15},{16,24},{17,... | collective-permute-start | bytes 983048 | tf_op jit(solution)/shard_map/ppermute | solution.py:22
  71.1 56.1 %collective-permute-start.13 = (bf16[256,2560]{1,0:T(8,128)(2,1)S(1)}, bf16[256,2560]{1,0:T(8,128)(2,1)S(1)}, u32[]{:S(2)}, u32[]{:S(2)}) collective-permute-start(bf16[256,2560]{1,0:T(8,128)(2,1)S(1)} %copy-done.7), channel_id=1, source_target_pairs={{0,1},{1,0},{2,3},{3,2},{4,5},{5,4},{6,7},{7,6},{8,9},{9,8},{10,11... | collective-permute-start | bytes 3932168 | tf_op jit(solution)/shard_map/ppermute | solution.py:22
  100.1 20.1 %collective-permute-start.11 = (bf16[64,2560]{1,0:T(8,128)(2,1)S(1)}, bf16[64,2560]{1,0:T(8,128)(2,1)S(1)}, u32[]{:S(2)}, u32[]{:S(2)}) collective-permute-start(bf16[64,2560]{1,0:T(8,128)(2,1)S(1)} %get-tuple-element.29), channel_id=1, source_target_pairs={{8,0},{9,1},{10,2},{11,3},{12,4},{13,5},{14,6},{15,7},{24,16},{25,... | collective-permute-start | bytes 983048 | tf_op jit(solution)/shard_map/ppermute | solution.py:22
  121.0 24.2 %collective-permute-start.7 = (bf16[256,2560]{1,0:T(8,128)(2,1)}, bf16[256,2560]{1,0:T(8,128)(2,1)}, u32[]{:S(2)}, u32[]{:S(2)}) collective-permute-start(bf16[256,2560]{1,0:T(8,128)(2,1)} %get-tuple-element.25), channel_id=1, source_target_pairs={{0,1},{1,0},{2,3},{3,2},{4,5},{5,4},{6,7},{7,6},{8,9},{9,8},{10,11... | collective-permute-start | bytes 3932168 | tf_op jit(solution)/shard_map/ppermute | solution.py:22
  121.0 35.1 %collective-permute-start.6 = (bf16[256,2560]{1,0:T(8,128)(2,1)}, bf16[256,2560]{1,0:T(8,128)(2,1)}, u32[]{:S(2)}, u32[]{:S(2)}) collective-permute-start(bf16[256,2560]{1,0:T(8,128)(2,1)} %collective-permute-done.5.third), channel_id=1, source_target_pairs={{0,1},{1,0},{2,3},{3,2},{4,5},{5,4},{6,7},{7,6},{8,9},{9,8},{10,11... | collective-permute-start | bytes 3932168 | tf_op jit(solution)/shard_map/ppermute | solution.py:22
  121.5 34.6 %collective-permute-start.2 = (bf16[256,2560]{1,0:T(8,128)(2,1)}, bf16[256,2560]{1,0:T(8,128)(2,1)}, u32[]{:S(2)}, u32[]{:S(2)}) collective-permute-start(bf16[256,2560]{1,0:T(8,128)(2,1)} %collective-permute-done.1.fourth), channel_id=1, source_target_pairs={{0,1},{4,5},{8,9},{12,13},{3,2},{7,6},{11,10},{15,14},{16,17},{20,... | collective-permute-start | bytes 3932168 | tf_op jit(solution)/shard_map/ppermute | solution.py:22
  125.6 14.3 %collective-permute-start.8 = (bf16[128,2560]{1,0:T(8,128)(2,1)}, bf16[128,2560]{1,0:T(8,128)(2,1)S(1)}, u32[]{:S(2)}, u32[]{:S(2)}) collective-permute-start(bf16[128,2560]{1,0:T(8,128)(2,1)} %get-tuple-element.26), channel_id=1, source_target_pairs={{0,4},{1,5},{2,6},{3,7},{4,8},{5,9},{6,10},{7,11},{8,12},{9,13},{1... | collective-permute-start | bytes 1966088 | tf_op jit(solution)/shard_map/ppermute | solution.py:22
  128.3 16.9 %collective-permute-start.9 = (bf16[128,2560]{1,0:T(8,128)(2,1)}, bf16[128,2560]{1,0:T(8,128)(2,1)}, u32[]{:S(2)}, u32[]{:S(2)}) collective-permute-start(bf16[128,2560]{1,0:T(8,128)(2,1)} %get-tuple-element.27), channel_id=1, source_target_pairs={{4,0},{5,1},{6,2},{7,3},{8,4},{9,5},{10,6},{11,7},{12,8},{13,9},{1... | collective-permute-start | bytes 1966088 | tf_op jit(solution)/shard_map/ppermute | solution.py:22
  129.7 1.3 copy-start.5
  135.0 10.2 %copy-start.14 = (bf16[64,2560]{1,0:T(8,128)(2,1)S(1)}, bf16[64,2560]{1,0:T(8,128)(2,1)}, u32[]{:S(2)}) copy-start(bf16[64,2560]{1,0:T(8,128)(2,1)} %copy-done.13) | copy-start | bytes 983044
  135.0 10.2 %copy-start.16 = (bf16[64,2560]{1,0:T(8,128)(2,1)S(1)}, bf16[64,2560]{1,0:T(8,128)(2,1)}, u32[]{:S(2)}) copy-start(bf16[64,2560]{1,0:T(8,128)(2,1)} %copy-done.15) | copy-start | bytes 983044
  145.2 6.5 %copy-start.2 = (bf16[256,2560]{1,0:T(8,128)(2,1)S(1)}, bf16[256,2560]{1,0:T(8,128)(2,1)}, u32[]{:S(2)}) copy-start(bf16[256,2560]{1,0:T(8,128)(2,1)} %copy-done.1) | copy-start | bytes 3932164
  (9 other events, 10.3 us)

commit v2 on v1

v2 whole, which is shorter than its diff:
```python
import functools
import math

import jax
import jax.numpy as jnp
from jax import lax
from jax.experimental import pallas as pl
from jax.experimental.pallas import tpu as pltpu
from jax.sharding import PartitionSpec as P

HEAD = 128
UNROLL = 20
MASKED = -1e30
F32 = jnp.float32
BF16 = jnp.bfloat16
VMEM = 8 * 1024 * 1024
COST = pl.CostEstimate(flops=1000, bytes_accessed=1000, transcendentals=0)


def permute(block, count, route):
    pairs = [(a, b) for a, b in route if 0 <= a < count and 0 <= b < count]
    return lax.ppermute(block, "ctx", pairs)


def listed(lists, device, level, side, j, shape):
    device = jnp.clip(device, 0, shape["devices"] - 1)
    return lists[device, (level * 2 + side) * shape["blocks"] + j]


def others(found, names, blocks):
    place = jnp.int32(0)
    for b in range(blocks):
        named = functools.reduce(jnp.logical_or, [n == b for n in names])
        found[place] = jnp.int32(b)
        place = place + jnp.where(named, 0, 1)


def gather(source, target, names, rows, at=0):
    below = source.shape[0] // 2
    for shift in (0, below):
        for name in names:
            target[at : at + rows] = source[pl.ds(pl.multiple_of(name * rows + shift, rows), rows)]
            at += rows
    return at


def far_pack(shape, lists, own, *far):
    me = lax.axis_index("ctx")
    for (level, way), out in zip(shape["far"], far):
        device = me + (1 << level) * (1 - 2 * way)
        names = [listed(lists, device, level, way, j, shape) for j in range(shape["blocks"] >> level)]
        gather(own, out, names, shape["rows"])


def crossing_names(found, lists, me, inner, shape):
    first = inner % 4 == 1
    half = shape["blocks"] // 2
    reader = jnp.where(first, inner - 2, inner + 2)
    names = [listed(lists, reader, 1, jnp.where(first, 1, 0), j, shape) for j in range(half)]
    others(found, names, shape["blocks"])
    return names, [found[j] for j in range(half)]


def reader_names(lists, me, shape):
    first = me % 4 == 0
    reader = jnp.where(first, me + 2, me - 2)
    return [listed(lists, reader, 1, jnp.where(first, 0, 1), j, shape) for j in range(shape["blocks"] // 2)]


def first_pack(shape, lists, own, crossing, *refs):
    far, found = refs[:-1], refs[-1]
    far_pack(shape, lists, own, *far)
    half = shape["blocks"] // 2
    me = lax.axis_index("ctx")
    spot = me % 4
    outer = jnp.logical_or(spot == 0, spot == 3)

    @pl.when(outer)
    def _():
        gather(own, crossing, reader_names(lists, me, shape), shape["rows"])

    @pl.when(jnp.logical_not(outer))
    def _():
        names, _ = crossing_names(found, lists, me, me, shape)
        gather(own, crossing, names, shape["rows"])


def second_pack(shape, lists, own, other, out, along, found):
    me = lax.axis_index("ctx")
    spot = me % 4
    outer = jnp.logical_or(spot == 0, spot == 3)
    quarter = shape["blocks"] // 4

    @pl.when(outer)
    def _():
        _, rest = crossing_names(found, lists, me, jnp.where(spot == 0, me + 1, me - 1), shape)
        gather(other, out, rest[quarter:], shape["rows"])
        others(found, reader_names(lists, me, shape), shape["blocks"])
        gather(own, along, [found[j] for j in range(2 * quarter)], shape["rows"])

    @pl.when(jnp.logical_not(outer))
    def _():
        _, rest = crossing_names(found, lists, me, me, shape)
        gather(own, out, rest[:quarter], shape["rows"])


SMEM = pl.BlockSpec(memory_space=pltpu.SMEM)
IN_VMEM = pl.BlockSpec(memory_space=pltpu.VMEM)


def pack_call(body, shape, lists, arrays, out_rows, scratch=()):
    width = arrays[0].shape[1]
    return pl.pallas_call(
        functools.partial(body, shape),
        out_shape=tuple(jax.ShapeDtypeStruct((r, width), BF16) for r in out_rows),
        in_specs=[SMEM] + [IN_VMEM] * len(arrays),
        out_specs=tuple([IN_VMEM] * len(out_rows)),
        scratch_shapes=list(scratch),
        cost_estimate=COST,
        compiler_params=pltpu.CompilerParams(vmem_limit_bytes=VMEM),
    )(lists, *arrays)


def lanes(column, n):
    wide = jnp.concatenate([column] * -(-n // column.shape[1]), axis=1)
    return wide[:, :n]


def attend(query, state, keys, values, masks):
    scale = math.log2(math.e) / math.sqrt(HEAD)
    raw = lax.dot_general(query, keys, (((1,), (1,)), ((), ())), preferred_element_type=F32)
    scores = []
    at = 0
    for n, mask in masks:
        part = raw[:, at : at + n] * scale
        scores.append(part if mask is None else part + mask)
        at += n
    scores = scores[0] if len(scores) == 1 else jnp.concatenate(scores, axis=1)
    best = jnp.broadcast_to(jnp.max(scores, axis=1, keepdims=True), query.shape)
    if state is not None:
        best = jnp.maximum(best, state[0])
    weights = jnp.exp2(scores - lanes(best, scores.shape[1])).astype(BF16)
    both = jnp.dot(weights, jnp.concatenate([values, jnp.ones_like(values)], axis=1), preferred_element_type=F32)
    weighted, total = both[:, :HEAD], both[:, HEAD:]
    if state is not None:
        factor = jnp.exp2(state[0] - best)
        total = total + state[1] * factor
        weighted = weighted + state[2] * factor
    return best, total, weighted


def member_flags(flags, at, ids, lists, counts, me, level, side, shape):
    counted = counts[0, level, side]
    names = [listed(lists, me, level, side, j, shape) for j in range(shape["blocks"] >> level)]
    for n, b in enumerate(ids):
        seen = functools.reduce(
            jnp.logical_or, [jnp.logical_and(j < counted, name == b) for j, name in enumerate(names)]
        )
        flags[at + n] = jnp.where(seen, 0.0, MASKED).astype(F32)


def order_flags(flags, at, capacity, counts, level, side):
    counted = counts[0, level, side]
    for j in range(capacity):
        flags[at + j] = jnp.where(j < counted, 0.0, MASKED).astype(F32)


def spread(flags, at, count, rows):
    place = lax.broadcasted_iota(jnp.int32, (1, count * rows), 1)
    row = jnp.full((1, count * rows), flags[at], F32)
    for b in range(1, count):
        row = jnp.where(place >= b * rows, flags[at + b], row)
    return row


def over_heads(width, body):
    def step(h, _):
        body(pl.ds(pl.multiple_of(h * HEAD, HEAD), HEAD))
        return 0

    lax.fori_loop(0, width // HEAD, step, 0, unroll=math.gcd(UNROLL, width // HEAD))


def load_state(refs, c):
    return tuple(ref[:, c] for ref in refs)


def store_state(refs, c, state):
    for ref, part in zip(refs, state):
        ref[:, c] = part


def far_sources(parts, refs, flags, at, counts, shape):
    sources = []
    for number, level, side in parts:
        capacity = shape["blocks"] >> level
        order_flags(flags, at, capacity, counts, level, side)
        sources.append((refs[number], 0, 2 * capacity * shape["rows"]))
        at += capacity
    return sources, at


def near_kernel(shape, lists, counts, q, own, other, *refs):
    after, flags = refs[-4:-1], refs[-1]
    me = lax.axis_index("ctx")
    blocks = shape["blocks"]
    member_flags(flags, 0, range(blocks), lists, counts, me, 0, 1 - me % 2, shape)
    mask = spread(flags, 0, blocks, shape["rows"])

    def head(c):
        keys, values = packed([own, other], c)
        masks = [(own.shape[0] // 2, None), (other.shape[0] // 2, mask)]
        store_state(after, c, attend(q[:, c], None, keys, values, masks))

    over_heads(shape["width"], head)


def packed(refs, c, filler=0):
    keys, values = [], []
    for ref in refs:
        ref, at, count = ref if isinstance(ref, tuple) else (ref, 0, ref.shape[0])
        keys.append(ref[at : at + count // 2, c])
        values.append(ref[at + count // 2 : at + count, c])
    if filler:
        keys.append(jnp.zeros((filler, HEAD), BF16))
        values.append(jnp.zeros((filler, HEAD), BF16))
    return jnp.concatenate(keys, axis=0), jnp.concatenate(values, axis=0)


def more_heads(shape, flags, count, q, before, after, sources):
    filler = -count % shape["blocks"]
    for b in range(count, count + filler):
        flags[b] = jnp.float32(MASKED)
    mask = spread(flags, 0, count + filler, shape["rows"])

    def head(c):
        keys, values = packed(sources, c, filler * shape["rows"])
        store_state(after, c, attend(q[:, c], load_state(before, c), keys, values, [(keys.shape[0], mask)]))

    over_heads(shape["width"], head)


def quad_kernel(shape, lists, counts, q, crossed, crossed_core, *refs):
    far, before, after, flags, found = refs[:-8], refs[-8:-5], refs[-5:-2], refs[-2], refs[-1]
    me = lax.axis_index("ctx")
    spot = me % 4
    blocks = shape["blocks"]
    half = blocks // 2
    begun = 0
    for level, way in shape["far"]:
        order_flags(flags, begun, blocks >> level, counts, level, way)
        begun += blocks >> level
    near_side = jnp.where(spot < 2, 1, 0)
    outer = jnp.logical_or(spot == 0, spot == 3)

    @pl.when(outer)
    def _():
        names, _ = crossing_names(found, lists, me, jnp.where(spot == 0, me + 2, me - 2), shape)
        member_flags(flags, begun, names, lists, counts, me, 1, near_side, shape)
        more_heads(shape, flags, begun + half, q, before, after, [*far, crossed])

    @pl.when(jnp.logical_not(outer))
    def _():
        order_flags(flags, begun, half, counts, 1, near_side)
        names, _ = crossing_names(found, lists, me, jnp.where(spot == 1, me + 1, me - 1), shape)
        member_flags(flags, begun + half, names, lists, counts, me, 0, me % 2, shape)
        more_heads(shape, flags, begun + 2 * half, q, before, after, [*far, crossed, crossed_core])


def giver_names(found, lists, me, shape):
    spot = me % 4
    outer = jnp.logical_or(spot == 0, spot == 3)
    step = jnp.where(outer, 3, 4)
    giver = jnp.where(spot < 2, me - step, me + step)
    half = shape["blocks"] // 2
    names = [listed(lists, giver, 1, jnp.where(spot < 2, 1, 0), j, shape) for j in range(half)]
    others(found, names, shape["blocks"])
    return names, [found[j] for j in range(half)]


def passed_kernel(shape, lists, counts, q, rest, rest_core, passed, *refs):
    before, after, flags, found = refs[:3], refs[3:6], refs[6], refs[7]
    me = lax.axis_index("ctx")
    spot = me % 4
    blocks = shape["blocks"]
    half = blocks // 2
    quarter = blocks // 4
    outer = jnp.logical_or(spot == 0, spot == 3)
    far_side = jnp.where(spot < 2, 0, 1)

    @pl.when(outer)
    def _():
        _, others_ = crossing_names(found, lists, me, jnp.where(spot == 0, me + 2, me - 2), shape)
        member_flags(flags, 0, others_, lists, counts, me, 1, jnp.where(spot < 2, 1, 0), shape)
        order_flags(flags, half, half, counts, 1, far_side)

    @pl.when(jnp.logical_not(outer))
    def _():
        _, others_ = crossing_names(found, lists, me, jnp.where(spot == 1, me + 1, me - 1), shape)
        member_flags(flags, 0, others_[quarter:] + others_[:quarter], lists, counts, me, 0, me % 2, shape)
        names, _ = giver_names(found, lists, me, shape)
        member_flags(flags, half, names, lists, counts, me, 1, far_side, shape)

    more_heads(shape, flags, 2 * half, q, before, after, [rest, rest_core, passed])


def last_kernel(shape, lists, counts, q, passed_core, third, third_core, *refs):
    before, out, flags, found = refs[:3], refs[3], refs[4], refs[5]
    me = lax.axis_index("ctx")
    spot = me % 4
    blocks = shape["blocks"]
    half = blocks // 2
    names, rest = giver_names(found, lists, me, shape)
    outer = jnp.logical_or(spot == 0, spot == 3)

    def heads(sources):
        mask = spread(flags, 0, blocks, shape["rows"])

        def head(c):
            keys, values = packed(sources, c, (blocks - half * len(sources)) * shape["rows"])
            _, total, weighted = attend(q[:, c], load_state(before, c), keys, values, [(keys.shape[0], mask)])
            out[:, c] = (weighted / total).astype(BF16)

        over_heads(shape["width"], head)

    @pl.when(outer)
    def _():
        member_flags(flags, 0, names + rest, lists, counts, me, 0, me % 2, shape)
        heads([passed_core, third])

    @pl.when(jnp.logical_not(outer))
    def _():
        member_flags(flags, 0, rest, lists, counts, me, 1, jnp.where(spot < 2, 0, 1), shape)
        for b in range(half, blocks):
            flags[b] = jnp.float32(MASKED)
        heads([third_core])


def attend_call(body, shape, smem, arrays, state=(), last=False, scratch=()):
    queries, width = arrays[0].shape
    return pl.pallas_call(
        functools.partial(body, shape),
        out_shape=jax.ShapeDtypeStruct((queries, width), BF16)
        if last
        else tuple([jax.ShapeDtypeStruct((queries, width), F32)] * 3),
        in_specs=[SMEM] * len(smem) + [IN_VMEM] * (len(arrays) + len(state)),
        out_specs=IN_VMEM if last else tuple([IN_VMEM] * 3),
        scratch_shapes=[pltpu.SMEM((64,), F32), *scratch],
        cost_estimate=COST,
        compiler_params=pltpu.CompilerParams(vmem_limit_bytes=VMEM),
    )(*smem, *arrays, *state)


def after(value, *events):
    return lax.optimization_barrier((value, *events))[0]


def shards(queries, keys, values, kv_lists, kv_counts):
    row_count, width = queries.shape
    blocks = kv_lists.shape[3]
    levels = kv_lists.shape[1]
    devices = lax.axis_size("ctx")
    half = blocks // 2
    rows = row_count // blocks
    shape = {"devices": devices, "blocks": blocks, "rows": rows, "width": width, "far": [(level, way) for level in range(2, levels) for way in range(2)]}
    every = range(devices)
    spot = {i: [d for d in every if d % 4 == i] for i in range(4)}
    other_core = [(d, d ^ 1) for d in every]
    over_y = [(d, d ^ 2) for d in every]
    outer_swap = [(d, d ^ 3) for d in spot[0] + spot[3]]
    outer_along = [(d, d + 4) for d in spot[3]] + [(d, d - 4) for d in spot[0]]
    pass_on = [(d, d + 4) for d in spot[0] + spot[1]] + [(d, d - 4) for d in spot[2] + spot[3]]
    outer_in = [(d, d ^ 1) for d in spot[0] + spot[3]]
    inner_out = [(d, d ^ 1) for d in spot[1] + spot[2]]
    chosen = [pltpu.SMEM((blocks + 1,), jnp.int32)]

    sent = jnp.broadcast_to(kv_lists.reshape(1, -1), (devices, levels * 2 * blocks))
    lists = lax.all_to_all(sent, "ctx", 0, 0, tiled=True)
    smem = (lists, kv_counts)
    own = jnp.concatenate([after(keys, sent), values], axis=0)
    other = permute(own, devices, other_core)
    far_rows = [2 * (blocks >> level) * rows for level, _ in shape["far"]]
    crossing, *far_packs = pack_call(first_pack, shape, lists, (own,), [row_count, *far_rows], chosen)
    crossed = permute(crossing, devices, over_y)
    far = []
    for (level, way), pack in zip(shape["far"], far_packs):
        step = (1 << level) * (1 - 2 * way)
        far.append(permute(pack, devices, [(d, d + step) for d in every]))
    rest_pack, along_pack = pack_call(
        second_pack, shape, lists, (own, other), [row_count // 2, row_count], chosen
    )
    state = attend_call(near_kernel, shape, smem, (queries, own, other))

    crossed, rest_pack, state, *far[:2] = lax.optimization_barrier((crossed, rest_pack, state, *far[:2]))
    passed = permute(crossed, devices, pass_on)
    rest = permute(rest_pack, devices, over_y)
    crossed_core = permute(crossed, devices, outer_in)
    along = permute(after(along_pack, *far), devices, outer_along)
    state = attend_call(quad_kernel, shape, smem, (queries, crossed, crossed_core, *far), state, False, chosen)

    along, rest, state = lax.optimization_barrier((along, rest, state))
    third = permute(along, devices, outer_swap)
    rest_core = permute(rest, devices, other_core)
    passed_core = permute(after(passed, rest_core), devices, inner_out)
    third_core = permute(after(third, passed_core), devices, outer_in)
    state = attend_call(passed_kernel, shape, smem, (queries, rest, rest_core, passed), state, False, chosen)
    return attend_call(last_kernel, shape, smem, (queries, passed_core, third, third_core), state, True, chosen)


def solution(mesh):
    in_specs = (
        P(("groups", "ctx"), None),
        P(("groups", "ctx"), None),
        P(("groups", "ctx"), None),
        P("ctx", None, None, None),
        P("ctx", None, None),
    )
    out_specs = P(("groups", "ctx"), None)
    return jax.shard_map(shards, mesh=mesh, in_specs=in_specs, out_specs=out_specs, check_vma=False)
```

time: 162 us -> 101 us (0.62)
  waiting for transfers between devices: 87.9 us -> 38 us
  blocking collectives: 0 us -> 13.3 us
  local copies, waits for them, and re-layouts: 13.1 us -> 0.24 us
  starting transfers between devices: 29.9 us -> 23.3 us
  Pallas kernels: 30.1 us -> 23.7 us
  other arithmetic: 0 us -> 1.89 us
    ppermute x14, waiting for transfers between devices: 82.3 us -> 38 us  [permute(): return lax.ppermute(block, 'ctx', pairs)]
    all_to_all x0 -> x1, blocking collectives: none -> 13.3 us  [shards(): lists = lax.all_to_all(sent, 'ctx', 0, 0, tiled=True)]
    unnamed x37 -> x7, local copies, waits for them, and re-layouts: 11.7 us -> 0.15 us
    all_to_all x1 -> x0, starting transfers between devices: 7.39 us -> none  [shards(): lists = lax.all_to_all(sent, 'ctx', 0, 0, tiled=True)]
    all_to_all x1 -> x0, waiting for transfers between devices: 5.58 us -> none  [shards(): lists = lax.all_to_all(sent, 'ctx', 0, 0, tiled=True)]
    pallas_call x2, Pallas kernels: 10.1 us -> 4.67 us  [pack_call(): pl.pallas_call(functools.partial(body, shape), out_shape=tuple((jax.Shape...]
    concatenate x0 -> x1, other arithmetic: none -> 1.89 us  [shards(): own = jnp.concatenate([after(keys, sent), values], axis=0)]
  transfers between devices with their start and end apart: 15 -> 14, of which waited for: 6 -> 8; matrix products, arithmetic and copies ran while one was open for 0% -> 0% of each run, Pallas kernels for 14% -> 19%
where the time goes in v2:
time: 101 us
  waiting for transfers between devices  38 us (38%)
  Pallas kernels  23.7 us (23%)
  starting transfers between devices  23.3 us (23%)
  blocking collectives  13.3 us (13%)
  other arithmetic  1.89 us (2%)
    ppermute x14, waiting for transfers between devices, permute(): return lax.ppermute(block, 'ctx', pairs)  38 us
    ppermute x14, starting transfers between devices, permute(): return lax.ppermute(block, 'ctx', pairs)  23.3 us
    pallas_call x4, Pallas kernels, attend_call(): pl.pallas_call(functools.partial(body, shape), out_shape=jax.ShapeDtypeSt...  19.1 us
    all_to_all x1, blocking collectives, shards(): lists = lax.all_to_all(sent, 'ctx', 0, 0, tiled=True)  13.3 us
    pallas_call x2, Pallas kernels, pack_call(): pl.pallas_call(functools.partial(body, shape), out_shape=tuple((jax.Shape...  4.67 us
  transfers between devices with their start and end apart: 14, of which 8 were waited for; matrix products, arithmetic and copies ran while one was open for 0% of the time, Pallas kernels for 19%

profile of v2, /device:TPU:0, one launch (start us, length us, event | category | flops | bytes accessed | tf_op | source)
XLA Modules:
  0.0 100.6 jit_solution(14188238588640894239)
XLA Ops:
  0.0 1.9 %pad_maximum_fusion.own = bf16[512,2560]{1,0:T(8,128)(2,1)S(1)} fusion(bf16[256,2560]{1,0:T(8,128)(2,1)} %param.7, bf16[256,2560]{1,0:T(8,128)(2,1)} %param.6), kind=kLoop, calls=%fused_computation | loop fusion | flops 5242880 | bytes 5242880 | tf_op jit(solution)/shard_map/concatenate | solution.py:380
  2.5 13.3 %all_to_all.8 = s32[16,1,64]{2,1,0:T(1,128)S(1)} all-to-all(s32[16,1,64]{2,1,0:T(1,128)S(1)} %broadcast_in_dim.8), channel_id=1, replica_groups=mesh['groups'=2,'ctx'=16] {'ctx'}, dimensions={0} | all-to-all | bytes 8192 | tf_op jit(solution)/shard_map/all_to_all | solution.py:378
  15.8 2.6 %shard_map.55 = (bf16[256,2560]{1,0:T(8,128)(2,1)}, bf16[128,2560]{1,0:T(8,128)(2,1)}, bf16[128,2560]{1,0:T(8,128)(2,1)}, bf16[64,2560]{1,0:T(8,128)(2,1)}, bf16[64,2560]{1,0:T(8,128)(2,1)}) custom-call(s32[16,64]{1,0:T(8,128)S(1)} %bitcast.1, bf16[512,2560]{1,0:T(8,128)(2,1)S(1)} %pad_maximum_fusion.own), custom_call_target="tpu_custom_call" | custom-call | flops 1000 | bytes 1000 | tf_op jit(solution)/shard_map/pallas_call | solution.py:113
  18.9 2.5 %collective-permute-start.2 = (bf16[128,2560]{1,0:T(8,128)(2,1)}, bf16[128,2560]{1,0:T(8,128)(2,1)S(1)}, u32[]{:S(2)}, u32[]{:S(2)}) collective-permute-start(bf16[128,2560]{1,0:T(8,128)(2,1)} %get-tuple-element.41), channel_id=1, source_target_pairs={{0,4},{1,5},{2,6},{3,7},{4,8},{5,9},{6,10},{7,11},{8,12},{9,13},{1... | collective-permute-start | bytes 1966088 | tf_op jit(solution)/shard_map/ppermute | solution.py:22
  21.4 1.3 %collective-permute-start.3 = (bf16[128,2560]{1,0:T(8,128)(2,1)}, bf16[128,2560]{1,0:T(8,128)(2,1)}, u32[]{:S(2)}, u32[]{:S(2)}) collective-permute-start(bf16[128,2560]{1,0:T(8,128)(2,1)} %get-tuple-element.42), channel_id=1, source_target_pairs={{4,0},{5,1},{6,2},{7,3},{8,4},{9,5},{10,6},{11,7},{12,8},{13,9},{1... | collective-permute-start | bytes 1966088 | tf_op jit(solution)/shard_map/ppermute | solution.py:22
  22.7 5.3 %collective-permute-start.5 = (bf16[64,2560]{1,0:T(8,128)(2,1)}, bf16[64,2560]{1,0:T(8,128)(2,1)}, u32[]{:S(2)}, u32[]{:S(2)}) collective-permute-start(bf16[64,2560]{1,0:T(8,128)(2,1)} %get-tuple-element.47), channel_id=1, source_target_pairs={{0,8},{1,9},{2,10},{3,11},{4,12},{5,13},{6,14},{7,15},{16,24},{17,... | collective-permute-start | bytes 983048 | tf_op jit(solution)/shard_map/ppermute | solution.py:22
  28.0 1.3 %collective-permute-start.6 = (bf16[64,2560]{1,0:T(8,128)(2,1)}, bf16[64,2560]{1,0:T(8,128)(2,1)}, u32[]{:S(2)}, u32[]{:S(2)}) collective-permute-start(bf16[64,2560]{1,0:T(8,128)(2,1)} %get-tuple-element.48), channel_id=1, source_target_pairs={{8,0},{9,1},{10,2},{11,3},{12,4},{13,5},{14,6},{15,7},{24,16},{25,... | collective-permute-start | bytes 983048 | tf_op jit(solution)/shard_map/ppermute | solution.py:22
  29.4 2.0 %shard_map.56 = (bf16[128,2560]{1,0:T(8,128)(2,1)S(1)}, bf16[256,2560]{1,0:T(8,128)(2,1)S(1)}) custom-call(s32[16,64]{1,0:T(8,128)S(1)} %bitcast.2, bf16[512,2560]{1,0:T(8,128)(2,1)S(1)} %pad_maximum_fusion.own, bf16[512,2560]{1,0:T(8,128)(2,1)} %collective-permute-done.1.other), custom_call_target="tpu_custom_call" | custom-call | flops 1000 | bytes 1000 | tf_op jit(solution)/shard_map/pallas_call | solution.py:113
  31.5 5.1 %shard_map.57 = (f32[256,2560]{1,0:T(8,128)S(1)}, f32[256,2560]{1,0:T(8,128)S(1)}, f32[256,2560]{1,0:T(8,128)S(1)}) custom-call(s32[16,64]{1,0:T(8,128)S(1)} %bitcast.3, s32[1,4,2]{2,1,0:T(4,128)S(1)} %copy.13.counts, bf16[256,2560]{1,0:T(8,128)(2,1)S(1)} %copy-done, bf16[512,2560]{1,0:T(8,128)(2,1)S(1)} %pad_maximum_fusion.own, ...), custom_call_target="tpu_custom_call" | custom-call | flops 1000 | bytes 1000 | tf_op jit(solution)/shard_map/pallas_call | solution.py:341
  36.9 3.3 %collective-permute-done.3.refs_1_ = bf16[128,2560]{1,0:T(8,128)(2,1)} collective-permute-done((bf16[128,2560]{1,0:T(8,128)(2,1)}, bf16[128,2560]{1,0:T(8,128)(2,1)}, u32[]{:S(2)}, u32[]{:S(2)}) %collective-permute-start.3) | collective-permute-done | bytes 655392 | tf_op jit(solution)/shard_map/ppermute | solution.py:22
  40.2 9.0 %collective-permute-done.crossed = bf16[256,2560]{1,0:T(8,128)(2,1)} collective-permute-done((bf16[256,2560]{1,0:T(8,128)(2,1)}, bf16[256,2560]{1,0:T(8,128)(2,1)}, u32[]{:S(2)}, u32[]{:S(2)}) %collective-permute-start) | collective-permute-done | bytes 1310752 | tf_op jit(solution)/shard_map/ppermute | solution.py:22
  49.2 1.4 %collective-permute-start.9 = (bf16[256,2560]{1,0:T(8,128)(2,1)}, bf16[256,2560]{1,0:T(8,128)(2,1)S(1)}, u32[]{:S(2)}, u32[]{:S(2)}) collective-permute-start(bf16[256,2560]{1,0:T(8,128)(2,1)} %collective-permute-done.crossed), channel_id=1, source_target_pairs={{0,1},{4,5},{8,9},{12,13},{3,2},{7,6},{11,10},{15,14},{16,17},{20,... | collective-permute-start | bytes 3932168 | tf_op jit(solution)/shard_map/ppermute | solution.py:22
  50.6 3.0 %collective-permute-done.6.refs_3_ = bf16[64,2560]{1,0:T(8,128)(2,1)} collective-permute-done((bf16[64,2560]{1,0:T(8,128)(2,1)}, bf16[64,2560]{1,0:T(8,128)(2,1)}, u32[]{:S(2)}, u32[]{:S(2)}) %collective-permute-start.6) | collective-permute-done | bytes 327712 | tf_op jit(solution)/shard_map/ppermute | solution.py:22
  55.8 3.7 %collective-permute-start.4 = (bf16[256,2560]{1,0:T(8,128)(2,1)}, bf16[256,2560]{1,0:T(8,128)(2,1)S(1)}, u32[]{:S(2)}, u32[]{:S(2)}) collective-permute-start(bf16[256,2560]{1,0:T(8,128)(2,1)} %collective-permute-done.crossed), channel_id=1, source_target_pairs={{0,4},{4,8},{8,12},{1,5},{5,9},{9,13},{6,2},{10,6},{14,10},{7,3},{... | collective-permute-start | bytes 3932168 | tf_op jit(solution)/shard_map/ppermute | solution.py:22
  59.6 6.7 %shard_map.58 = (f32[256,2560]{1,0:T(8,128)S(1)}, f32[256,2560]{1,0:T(8,128)S(1)}, f32[256,2560]{1,0:T(8,128)S(1)}) custom-call(s32[16,64]{1,0:T(8,128)S(1)} %bitcast.4, s32[1,4,2]{2,1,0:T(4,128)S(1)} %copy.13.counts, bf16[256,2560]{1,0:T(8,128)(2,1)S(1)} %copy-done, bf16[256,2560]{1,0:T(8,128)(2,1)} %collective-permute-done.crossed, ...), custom_call_target="tpu_custom_call" | custom-call | flops 1000 | bytes 1000 | tf_op jit(solution)/shard_map/pallas_call | solution.py:341
  66.4 3.4 %collective-permute-done.8.rest = bf16[128,2560]{1,0:T(8,128)(2,1)S(1)} collective-permute-done((bf16[128,2560]{1,0:T(8,128)(2,1)S(1)}, bf16[128,2560]{1,0:T(8,128)(2,1)S(1)}, u32[]{:S(2)}, u32[]{:S(2)}) %collective-permute-start.8) | collective-permute-done | bytes 655392 | tf_op jit(solution)/shard_map/ppermute | solution.py:22
  69.7 3.3 %collective-permute-done.7 = bf16[256,2560]{1,0:T(8,128)(2,1)S(1)} collective-permute-done((bf16[256,2560]{1,0:T(8,128)(2,1)S(1)}, bf16[256,2560]{1,0:T(8,128)(2,1)S(1)}, u32[]{:S(2)}, u32[]{:S(2)}) %collective-permute-start.7) | collective-permute-done | bytes 1310752 | tf_op jit(solution)/shard_map/ppermute | solution.py:22
  73.1 1.9 %collective-permute-start.12 = (bf16[256,2560]{1,0:T(8,128)(2,1)S(1)}, bf16[256,2560]{1,0:T(8,128)(2,1)S(1)}, u32[]{:S(2)}, u32[]{:S(2)}) collective-permute-start(bf16[256,2560]{1,0:T(8,128)(2,1)S(1)} %collective-permute-done.7), channel_id=1, source_target_pairs={{0,3},{4,7},{8,11},{12,15},{3,0},{7,4},{11,8},{15,12},{16,19},{20,... | collective-permute-start | bytes 3932168 | tf_op jit(solution)/shard_map/ppermute | solution.py:22
  75.0 10.3 %collective-permute-done.4.passed = bf16[256,2560]{1,0:T(8,128)(2,1)S(1)} collective-permute-done((bf16[256,2560]{1,0:T(8,128)(2,1)}, bf16[256,2560]{1,0:T(8,128)(2,1)S(1)}, u32[]{:S(2)}, u32[]{:S(2)}) %collective-permute-start.4) | collective-permute-done | bytes 1310752 | tf_op jit(solution)/shard_map/ppermute | solution.py:22
  85.3 1.3 %collective-permute-start.11 = (bf16[256,2560]{1,0:T(8,128)(2,1)S(1)}, bf16[256,2560]{1,0:T(8,128)(2,1)S(1)}, u32[]{:S(2)}, u32[]{:S(2)}) collective-permute-start(bf16[256,2560]{1,0:T(8,128)(2,1)S(1)} %collective-permute-done.4.passed), channel_id=1, source_target_pairs={{1,0},{5,4},{9,8},{13,12},{2,3},{6,7},{10,11},{14,15},{17,16},{21,... | collective-permute-start | bytes 3932168 | tf_op jit(solution)/shard_map/ppermute | solution.py:22
  86.6 5.4 %collective-permute-done.12.third = bf16[256,2560]{1,0:T(8,128)(2,1)S(1)} collective-permute-done((bf16[256,2560]{1,0:T(8,128)(2,1)S(1)}, bf16[256,2560]{1,0:T(8,128)(2,1)S(1)}, u32[]{:S(2)}, u32[]{:S(2)}) %collective-permute-start.12) | collective-permute-done | bytes 1310752 | tf_op jit(solution)/shard_map/ppermute | solution.py:22
  92.0 1.4 %collective-permute-start.13 = (bf16[256,2560]{1,0:T(8,128)(2,1)S(1)}, bf16[256,2560]{1,0:T(8,128)(2,1)S(1)}, u32[]{:S(2)}, u32[]{:S(2)}) collective-permute-start(bf16[256,2560]{1,0:T(8,128)(2,1)S(1)} %collective-permute-done.12.third), channel_id=1, source_target_pairs={{0,1},{4,5},{8,9},{12,13},{3,2},{7,6},{11,10},{15,14},{16,17},{20,... | collective-permute-start | bytes 3932168 | tf_op jit(solution)/shard_map/ppermute | solution.py:22
  93.4 3.0 %shard_map.59 = (f32[256,2560]{1,0:T(8,128)S(1)}, f32[256,2560]{1,0:T(8,128)S(1)}, f32[256,2560]{1,0:T(8,128)S(1)}) custom-call(s32[16,64]{1,0:T(8,128)S(1)} %bitcast.5, s32[1,4,2]{2,1,0:T(4,128)S(1)} %copy.13.counts, bf16[256,2560]{1,0:T(8,128)(2,1)S(1)} %copy-done, bf16[128,2560]{1,0:T(8,128)(2,1)S(1)} %collective-permute-done.8.rest, ...), custom_call_target="tpu_custom_call" | custom-call | flops 1000 | bytes 1000 | tf_op jit(solution)/shard_map/pallas_call | solution.py:341
  96.3 4.3 %shard_map.60 = bf16[256,2560]{1,0:T(8,128)(2,1)} custom-call(s32[16,64]{1,0:T(8,128)S(1)} %bitcast.6, s32[1,4,2]{2,1,0:T(4,128)S(1)} %copy.13.counts, bf16[256,2560]{1,0:T(8,128)(2,1)S(1)} %copy-done, bf16[256,2560]{1,0:T(8,128)(2,1)S(1)} %collective-permute-done.11.passed_core, bf16[256,2560]{1,0:T(8,128)(2,1)S(1)} %collective-permute-done.12.third, ...), custom_call_target="tpu_custom_call" | custom-call | flops 1000 | bytes 1000 | tf_op jit(solution)/shard_map/pallas_call | solution.py:341
  (21 shorter events, 3.8 us)
Async XLA Ops:
  0.0 2.4 %copy-start.1 = (s32[1,4,2,8]{3,2,1,0:T(2,128)S(1)}, s32[1,4,2,8]{3,2,1,0:T(2,128)}, u32[]{:S(2)}) copy-start(s32[1,4,2,8]{3,2,1,0:T(2,128)} %param.8) | copy-start | bytes 772
  1.9 27.4 %copy-start.2 = (s32[1,4,2]{1,2,0:T(2,128)S(1)}, s32[1,4,2]{1,2,0:T(2,128)}, u32[]{:S(2)}) copy-start(s32[1,4,2]{1,2,0:T(2,128)} %param.9) | copy-start | bytes 100
  1.9 26.1 %collective-permute-start.1 = (bf16[512,2560]{1,0:T(8,128)(2,1)S(1)}, bf16[512,2560]{1,0:T(8,128)(2,1)}, u32[]{:S(2)}, u32[]{:S(2)}) collective-permute-start(bf16[512,2560]{1,0:T(8,128)(2,1)S(1)} %pad_maximum_fusion.own), channel_id=1, source_target_pairs={{0,1},{1,0},{2,3},{3,2},{4,5},{5,4},{6,7},{7,6},{8,9},{9,8},{10,11... | collective-permute-start | bytes 7864328 | tf_op jit(solution)/shard_map/ppermute | solution.py:22
  18.4 30.8 %collective-permute-start = (bf16[256,2560]{1,0:T(8,128)(2,1)}, bf16[256,2560]{1,0:T(8,128)(2,1)}, u32[]{:S(2)}, u32[]{:S(2)}) collective-permute-start(bf16[256,2560]{1,0:T(8,128)(2,1)} %get-tuple-element.36), channel_id=1, source_target_pairs={{0,2},{1,3},{2,0},{3,1},{4,6},{5,7},{6,4},{7,5},{8,10},{9,11},{10,... | collective-permute-start | bytes 3932168 | tf_op jit(solution)/shard_map/ppermute | solution.py:22
  18.9 17.9 %collective-permute-start.2 = (bf16[128,2560]{1,0:T(8,128)(2,1)}, bf16[128,2560]{1,0:T(8,128)(2,1)S(1)}, u32[]{:S(2)}, u32[]{:S(2)}) collective-permute-start(bf16[128,2560]{1,0:T(8,128)(2,1)} %get-tuple-element.41), channel_id=1, source_target_pairs={{0,4},{1,5},{2,6},{3,7},{4,8},{5,9},{6,10},{7,11},{8,12},{9,13},{1... | collective-permute-start | bytes 1966088 | tf_op jit(solution)/shard_map/ppermute | solution.py:22
  21.4 18.7 %collective-permute-start.3 = (bf16[128,2560]{1,0:T(8,128)(2,1)}, bf16[128,2560]{1,0:T(8,128)(2,1)}, u32[]{:S(2)}, u32[]{:S(2)}) collective-permute-start(bf16[128,2560]{1,0:T(8,128)(2,1)} %get-tuple-element.42), channel_id=1, source_target_pairs={{4,0},{5,1},{6,2},{7,3},{8,4},{9,5},{10,6},{11,7},{12,8},{13,9},{1... | collective-permute-start | bytes 1966088 | tf_op jit(solution)/shard_map/ppermute | solution.py:22
  22.7 27.8 %collective-permute-start.5 = (bf16[64,2560]{1,0:T(8,128)(2,1)}, bf16[64,2560]{1,0:T(8,128)(2,1)}, u32[]{:S(2)}, u32[]{:S(2)}) collective-permute-start(bf16[64,2560]{1,0:T(8,128)(2,1)} %get-tuple-element.47), channel_id=1, source_target_pairs={{0,8},{1,9},{2,10},{3,11},{4,12},{5,13},{6,14},{7,15},{16,24},{17,... | collective-permute-start | bytes 983048 | tf_op jit(solution)/shard_map/ppermute | solution.py:22
  28.0 25.6 %collective-permute-start.6 = (bf16[64,2560]{1,0:T(8,128)(2,1)}, bf16[64,2560]{1,0:T(8,128)(2,1)}, u32[]{:S(2)}, u32[]{:S(2)}) collective-permute-start(bf16[64,2560]{1,0:T(8,128)(2,1)} %get-tuple-element.48), channel_id=1, source_target_pairs={{8,0},{9,1},{10,2},{11,3},{12,4},{13,5},{14,6},{15,7},{24,16},{25,... | collective-permute-start | bytes 983048 | tf_op jit(solution)/shard_map/ppermute | solution.py:22
  29.4 2.1 %copy-start = (bf16[256,2560]{1,0:T(8,128)(2,1)S(1)}, bf16[256,2560]{1,0:T(8,128)(2,1)}, u32[]{:S(2)}) copy-start(bf16[256,2560]{1,0:T(8,128)(2,1)} %q.7) | copy-start | bytes 3932164
  49.2 10.4 %collective-permute-start.9 = (bf16[256,2560]{1,0:T(8,128)(2,1)}, bf16[256,2560]{1,0:T(8,128)(2,1)S(1)}, u32[]{:S(2)}, u32[]{:S(2)}) collective-permute-start(bf16[256,2560]{1,0:T(8,128)(2,1)} %collective-permute-done.crossed), channel_id=1, source_target_pairs={{0,1},{4,5},{8,9},{12,13},{3,2},{7,6},{11,10},{15,14},{16,17},{20,... | collective-permute-start | bytes 3932168 | tf_op jit(solution)/shard_map/ppermute | solution.py:22
  53.6 19.5 %collective-permute-start.7 = (bf16[256,2560]{1,0:T(8,128)(2,1)S(1)}, bf16[256,2560]{1,0:T(8,128)(2,1)S(1)}, u32[]{:S(2)}, u32[]{:S(2)}) collective-permute-start(bf16[256,2560]{1,0:T(8,128)(2,1)S(1)} %get-tuple-element.49), channel_id=1, source_target_pairs={{3,7},{7,11},{11,15},{4,0},{8,4},{12,8},{19,23},{23,27},{27,31},{2... | collective-permute-start | bytes 3932168 | tf_op jit(solution)/shard_map/ppermute | solution.py:22
  54.9 14.9 %collective-permute-start.8 = (bf16[128,2560]{1,0:T(8,128)(2,1)S(1)}, bf16[128,2560]{1,0:T(8,128)(2,1)S(1)}, u32[]{:S(2)}, u32[]{:S(2)}) collective-permute-start(bf16[128,2560]{1,0:T(8,128)(2,1)S(1)} %get-tuple-element.50), channel_id=1, source_target_pairs={{0,2},{1,3},{2,0},{3,1},{4,6},{5,7},{6,4},{7,5},{8,10},{9,11},{10,... | collective-permute-start | bytes 1966088 | tf_op jit(solution)/shard_map/ppermute | solution.py:22
  55.8 29.5 %collective-permute-start.4 = (bf16[256,2560]{1,0:T(8,128)(2,1)}, bf16[256,2560]{1,0:T(8,128)(2,1)S(1)}, u32[]{:S(2)}, u32[]{:S(2)}) collective-permute-start(bf16[256,2560]{1,0:T(8,128)(2,1)} %collective-permute-done.crossed), channel_id=1, source_target_pairs={{0,4},{4,8},{8,12},{1,5},{5,9},{9,13},{6,2},{10,6},{14,10},{7,3},{... | collective-permute-start | bytes 3932168 | tf_op jit(solution)/shard_map/ppermute | solution.py:22
  73.1 12.3 %collective-permute-start.10 = (bf16[128,2560]{1,0:T(8,128)(2,1)S(1)}, bf16[128,2560]{1,0:T(8,128)(2,1)S(1)}, u32[]{:S(2)}, u32[]{:S(2)}) collective-permute-start(bf16[128,2560]{1,0:T(8,128)(2,1)S(1)} %collective-permute-done.8.rest), channel_id=1, source_target_pairs={{0,1},{1,0},{2,3},{3,2},{4,5},{5,4},{6,7},{7,6},{8,9},{9,8},{10,11... | collective-permute-start | bytes 1966088 | tf_op jit(solution)/shard_map/ppermute | solution.py:22
  73.1 18.9 %collective-permute-start.12 = (bf16[256,2560]{1,0:T(8,128)(2,1)S(1)}, bf16[256,2560]{1,0:T(8,128)(2,1)S(1)}, u32[]{:S(2)}, u32[]{:S(2)}) collective-permute-start(bf16[256,2560]{1,0:T(8,128)(2,1)S(1)} %collective-permute-done.7), channel_id=1, source_target_pairs={{0,3},{4,7},{8,11},{12,15},{3,0},{7,4},{11,8},{15,12},{16,19},{20,... | collective-permute-start | bytes 3932168 | tf_op jit(solution)/shard_map/ppermute | solution.py:22
  85.3 6.7 %collective-permute-start.11 = (bf16[256,2560]{1,0:T(8,128)(2,1)S(1)}, bf16[256,2560]{1,0:T(8,128)(2,1)S(1)}, u32[]{:S(2)}, u32[]{:S(2)}) collective-permute-start(bf16[256,2560]{1,0:T(8,128)(2,1)S(1)} %collective-permute-done.4.passed), channel_id=1, source_target_pairs={{1,0},{5,4},{9,8},{13,12},{2,3},{6,7},{10,11},{14,15},{17,16},{21,... | collective-permute-start | bytes 3932168 | tf_op jit(solution)/shard_map/ppermute | solution.py:22
  92.0 4.3 %collective-permute-start.13 = (bf16[256,2560]{1,0:T(8,128)(2,1)S(1)}, bf16[256,2560]{1,0:T(8,128)(2,1)S(1)}, u32[]{:S(2)}, u32[]{:S(2)}) collective-permute-start(bf16[256,2560]{1,0:T(8,128)(2,1)S(1)} %collective-permute-done.12.third), channel_id=1, source_target_pairs={{0,1},{4,5},{8,9},{12,13},{3,2},{7,6},{11,10},{15,14},{16,17},{20,... | collective-permute-start | bytes 3932168 | tf_op jit(solution)/shard_map/ppermute | solution.py:22

commit v3 on v2

--- a/solution.py
+++ b/solution.py
@@ -62,8 +62,8 @@
 
 
 def reader_names(lists, me, shape):
-    first = me % 4 == 0
-    reader = jnp.where(first, me + 2, me - 2)
+    first = me % 4 < 2
+    reader = me - me % 4 + jnp.where(first, 2, 1)
     return [listed(lists, reader, 1, jnp.where(first, 0, 1), j, shape) for j in range(shape["blocks"] // 2)]
 
 
@@ -90,16 +90,18 @@
     spot = me % 4
     outer = jnp.logical_or(spot == 0, spot == 3)
     quarter = shape["blocks"] // 4
+    others(found, reader_names(lists, me, shape), shape["blocks"])
+    late = [found[j] for j in range(2 * quarter)]
 
     @pl.when(outer)
     def _():
+        gather(own, along, late[:quarter], shape["rows"])
         _, rest = crossing_names(found, lists, me, jnp.where(spot == 0, me + 1, me - 1), shape)
         gather(other, out, rest[quarter:], shape["rows"])
-        others(found, reader_names(lists, me, shape), shape["blocks"])
-        gather(own, along, [found[j] for j in range(2 * quarter)], shape["rows"])
 
     @pl.when(jnp.logical_not(outer))
     def _():
+        gather(other, along, late[quarter:], shape["rows"])
         _, rest = crossing_names(found, lists, me, me, shape)
         gather(own, out, rest[:quarter], shape["rows"])
 
@@ -310,14 +312,18 @@
     spot = me % 4
     blocks = shape["blocks"]
     half = blocks // 2
+    quarter = half // 2
     names, rest = giver_names(found, lists, me, shape)
     outer = jnp.logical_or(spot == 0, spot == 3)
 
-    def heads(sources):
-        mask = spread(flags, 0, blocks, shape["rows"])
+    def heads(sources, count):
+        filler = -count % blocks
+        for b in range(count, count + filler):
+            flags[b] = jnp.float32(MASKED)
+        mask = spread(flags, 0, count + filler, shape["rows"])
 
         def head(c):
-            keys, values = packed(sources, c, (blocks - half * len(sources)) * shape["rows"])
+            keys, values = packed(sources, c, filler * shape["rows"])
             _, total, weighted = attend(q[:, c], load_state(before, c), keys, values, [(keys.shape[0], mask)])
             out[:, c] = (weighted / total).astype(BF16)
 
@@ -325,15 +331,13 @@
 
     @pl.when(outer)
     def _():
-        member_flags(flags, 0, names + rest, lists, counts, me, 0, me % 2, shape)
-        heads([passed_core, third])
+        member_flags(flags, 0, names + rest[quarter:] + rest[:quarter], lists, counts, me, 0, me % 2, shape)
+        heads([passed_core, third, third_core], 2 * half)
 
     @pl.when(jnp.logical_not(outer))
     def _():
         member_flags(flags, 0, rest, lists, counts, me, 1, jnp.where(spot < 2, 0, 1), shape)
-        for b in range(half, blocks):
-            flags[b] = jnp.float32(MASKED)
-        heads([third_core])
+        heads([third, third_core], half)
 
 
 def attend_call(body, shape, smem, arrays, state=(), last=False, scratch=()):
@@ -367,8 +371,7 @@
     spot = {i: [d for d in every if d % 4 == i] for i in range(4)}
     other_core = [(d, d ^ 1) for d in every]
     over_y = [(d, d ^ 2) for d in every]
-    outer_swap = [(d, d ^ 3) for d in spot[0] + spot[3]]
-    outer_along = [(d, d + 4) for d in spot[3]] + [(d, d - 4) for d in spot[0]]
+    outward = [(d, d + 4) for d in spot[2] + spot[3]] + [(d, d - 4) for d in spot[0] + spot[1]]
     pass_on = [(d, d + 4) for d in spot[0] + spot[1]] + [(d, d - 4) for d in spot[2] + spot[3]]
     outer_in = [(d, d ^ 1) for d in spot[0] + spot[3]]
     inner_out = [(d, d ^ 1) for d in spot[1] + spot[2]]
@@ -387,22 +390,25 @@
         step = (1 << level) * (1 - 2 * way)
         far.append(permute(pack, devices, [(d, d + step) for d in every]))
     rest_pack, along_pack = pack_call(
-        second_pack, shape, lists, (own, other), [row_count // 2, row_count], chosen
+        second_pack, shape, lists, (own, other), [row_count // 2, row_count // 2], chosen
     )
     state = attend_call(near_kernel, shape, smem, (queries, own, other))
 
-    crossed, rest_pack, state, *far[:2] = lax.optimization_barrier((crossed, rest_pack, state, *far[:2]))
+    crossed, rest_pack, along_pack, state, *far = lax.optimization_barrier(
+        (crossed, rest_pack, along_pack, state, *far)
+    )
     passed = permute(crossed, devices, pass_on)
     rest = permute(rest_pack, devices, over_y)
     crossed_core = permute(crossed, devices, outer_in)
-    along = permute(after(along_pack, *far), devices, outer_along)
+    along = permute(along_pack, devices, outward)
     state = attend_call(quad_kernel, shape, smem, (queries, crossed, crossed_core, *far), state, False, chosen)
 
     along, rest, state = lax.optimization_barrier((along, rest, state))
-    third = permute(along, devices, outer_swap)
+    third = permute(along, devices, over_y)
     rest_core = permute(rest, devices, other_core)
-    passed_core = permute(after(passed, rest_core), devices, inner_out)
-    third_core = permute(after(third, passed_core), devices, outer_in)
+    passed, rest_core, third = lax.optimization_barrier((passed, rest_core, third))
+    passed_core = permute(passed, devices, inner_out)
+    third_core = permute(third, devices, other_core)
     state = attend_call(passed_kernel, shape, smem, (queries, rest, rest_core, passed), state, False, chosen)
     return attend_call(last_kernel, shape, smem, (queries, passed_core, third, third_core), state, True, chosen)
 

time: 101 us -> 102 us (level)
  transfers between devices with their start and end apart: 14 -> 14, of which waited for: 8 -> 7; matrix products, arithmetic and copies ran while one was open for 0% -> 0% of each run, Pallas kernels for 19% -> 19%
where the time goes in v3:
time: 102 us; the launch traced here: 101 us
  waiting for transfers between devices  38.8 us (38%)
  Pallas kernels  23.7 us (23%)
  starting transfers between devices  22.6 us (22%)
  blocking collectives  13.3 us (13%)
  other arithmetic  1.89 us (2%)
    ppermute x14, waiting for transfers between devices, permute(): return lax.ppermute(block, 'ctx', pairs)  38.8 us
    ppermute x14, starting transfers between devices, permute(): return lax.ppermute(block, 'ctx', pairs)  22.6 us
    pallas_call x4, Pallas kernels, attend_call(): pl.pallas_call(functools.partial(body, shape), out_shape=jax.ShapeDtypeSt...  19 us
    all_to_all x1, blocking collectives, shards(): lists = lax.all_to_all(sent, 'ctx', 0, 0, tiled=True)  13.3 us
    pallas_call x2, Pallas kernels, pack_call(): pl.pallas_call(functools.partial(body, shape), out_shape=tuple((jax.Shape...  4.63 us
  transfers between devices with their start and end apart: 14, of which 7 were waited for; matrix products, arithmetic and copies ran while one was open for 0% of the time, Pallas kernels for 19%

profile of v3, /device:TPU:0, one launch (start us, length us, event | category | flops | bytes accessed | tf_op | source)
XLA Modules:
  0.0 100.6 jit_solution(8405804631331131256)
XLA Ops:
  0.0 1.9 %pad_maximum_fusion.own = bf16[512,2560]{1,0:T(8,128)(2,1)S(1)} fusion(bf16[256,2560]{1,0:T(8,128)(2,1)} %param.7, bf16[256,2560]{1,0:T(8,128)(2,1)} %param.6), kind=kLoop, calls=%fused_computation | loop fusion | flops 5242880 | bytes 5242880 | tf_op jit(solution)/shard_map/concatenate | solution.py:383
  2.5 13.3 %all_to_all.8 = s32[16,1,64]{2,1,0:T(1,128)S(1)} all-to-all(s32[16,1,64]{2,1,0:T(1,128)S(1)} %broadcast_in_dim.8), channel_id=1, replica_groups=mesh['groups'=2,'ctx'=16] {'ctx'}, dimensions={0} | all-to-all | bytes 8192 | tf_op jit(solution)/shard_map/all_to_all | solution.py:381
  15.8 2.6 %shard_map.55 = (bf16[256,2560]{1,0:T(8,128)(2,1)}, bf16[128,2560]{1,0:T(8,128)(2,1)}, bf16[128,2560]{1,0:T(8,128)(2,1)}, bf16[64,2560]{1,0:T(8,128)(2,1)}, bf16[64,2560]{1,0:T(8,128)(2,1)}) custom-call(s32[16,64]{1,0:T(8,128)S(1)} %bitcast.1, bf16[512,2560]{1,0:T(8,128)(2,1)S(1)} %pad_maximum_fusion.own), custom_call_target="tpu_custom_call" | custom-call | flops 1000 | bytes 1000 | tf_op jit(solution)/shard_map/pallas_call | solution.py:115
  18.9 2.5 %collective-permute-start.2 = (bf16[128,2560]{1,0:T(8,128)(2,1)}, bf16[128,2560]{1,0:T(8,128)(2,1)S(1)}, u32[]{:S(2)}, u32[]{:S(2)}) collective-permute-start(bf16[128,2560]{1,0:T(8,128)(2,1)} %get-tuple-element.45), channel_id=1, source_target_pairs={{0,4},{1,5},{2,6},{3,7},{4,8},{5,9},{6,10},{7,11},{8,12},{9,13},{1... | collective-permute-start | bytes 1966088 | tf_op jit(solution)/shard_map/ppermute | solution.py:22
  21.4 1.3 %collective-permute-start.3 = (bf16[128,2560]{1,0:T(8,128)(2,1)}, bf16[128,2560]{1,0:T(8,128)(2,1)}, u32[]{:S(2)}, u32[]{:S(2)}) collective-permute-start(bf16[128,2560]{1,0:T(8,128)(2,1)} %get-tuple-element.46), channel_id=1, source_target_pairs={{4,0},{5,1},{6,2},{7,3},{8,4},{9,5},{10,6},{11,7},{12,8},{13,9},{1... | collective-permute-start | bytes 1966088 | tf_op jit(solution)/shard_map/ppermute | solution.py:22
  22.7 5.3 %collective-permute-start.4 = (bf16[64,2560]{1,0:T(8,128)(2,1)}, bf16[64,2560]{1,0:T(8,128)(2,1)}, u32[]{:S(2)}, u32[]{:S(2)}) collective-permute-start(bf16[64,2560]{1,0:T(8,128)(2,1)} %get-tuple-element.47), channel_id=1, source_target_pairs={{0,8},{1,9},{2,10},{3,11},{4,12},{5,13},{6,14},{7,15},{16,24},{17,... | collective-permute-start | bytes 983048 | tf_op jit(solution)/shard_map/ppermute | solution.py:22
  28.0 1.3 %collective-permute-start.5 = (bf16[64,2560]{1,0:T(8,128)(2,1)}, bf16[64,2560]{1,0:T(8,128)(2,1)}, u32[]{:S(2)}, u32[]{:S(2)}) collective-permute-start(bf16[64,2560]{1,0:T(8,128)(2,1)} %get-tuple-element.48), channel_id=1, source_target_pairs={{8,0},{9,1},{10,2},{11,3},{12,4},{13,5},{14,6},{15,7},{24,16},{25,... | collective-permute-start | bytes 983048 | tf_op jit(solution)/shard_map/ppermute | solution.py:22
  29.4 2.0 %shard_map.56 = (bf16[128,2560]{1,0:T(8,128)(2,1)S(1)}, bf16[128,2560]{1,0:T(8,128)(2,1)S(1)}) custom-call(s32[16,64]{1,0:T(8,128)S(1)} %bitcast.2, bf16[512,2560]{1,0:T(8,128)(2,1)S(1)} %pad_maximum_fusion.own, bf16[512,2560]{1,0:T(8,128)(2,1)} %collective-permute-done.1.other), custom_call_target="tpu_custom_call" | custom-call | flops 1000 | bytes 1000 | tf_op jit(solution)/shard_map/pallas_call | solution.py:115
  31.5 5.1 %shard_map.57 = (f32[256,2560]{1,0:T(8,128)S(1)}, f32[256,2560]{1,0:T(8,128)S(1)}, f32[256,2560]{1,0:T(8,128)S(1)}) custom-call(s32[16,64]{1,0:T(8,128)S(1)} %bitcast.3, s32[1,4,2]{2,1,0:T(4,128)S(1)} %copy.13.counts, bf16[256,2560]{1,0:T(8,128)(2,1)S(1)} %copy-done, bf16[512,2560]{1,0:T(8,128)(2,1)S(1)} %pad_maximum_fusion.own, ...), custom_call_target="tpu_custom_call" | custom-call | flops 1000 | bytes 1000 | tf_op jit(solution)/shard_map/pallas_call | solution.py:345
  36.6 5.9 %collective-permute-done.4.refs_2_ = bf16[64,2560]{1,0:T(8,128)(2,1)} collective-permute-done((bf16[64,2560]{1,0:T(8,128)(2,1)}, bf16[64,2560]{1,0:T(8,128)(2,1)}, u32[]{:S(2)}, u32[]{:S(2)}) %collective-permute-start.4) | collective-permute-done | bytes 327712 | tf_op jit(solution)/shard_map/ppermute | solution.py:22
  42.5 11.1 %collective-permute-done.5.refs_3_ = bf16[64,2560]{1,0:T(8,128)(2,1)} collective-permute-done((bf16[64,2560]{1,0:T(8,128)(2,1)}, bf16[64,2560]{1,0:T(8,128)(2,1)}, u32[]{:S(2)}, u32[]{:S(2)}) %collective-permute-start.5) | collective-permute-done | bytes 327712 | tf_op jit(solution)/shard_map/ppermute | solution.py:22
  53.6 1.4 %collective-permute-start.9 = (bf16[256,2560]{1,0:T(8,128)(2,1)}, bf16[256,2560]{1,0:T(8,128)(2,1)S(1)}, u32[]{:S(2)}, u32[]{:S(2)}) collective-permute-start(bf16[256,2560]{1,0:T(8,128)(2,1)} %collective-permute-done.crossed), channel_id=1, source_target_pairs={{0,1},{4,5},{8,9},{12,13},{3,2},{7,6},{11,10},{15,14},{16,17},{20,... | collective-permute-start | bytes 3932168 | tf_op jit(solution)/shard_map/ppermute | solution.py:22
  55.0 1.3 %collective-permute-start.7 = (bf16[128,2560]{1,0:T(8,128)(2,1)S(1)}, bf16[128,2560]{1,0:T(8,128)(2,1)S(1)}, u32[]{:S(2)}, u32[]{:S(2)}) collective-permute-start(bf16[128,2560]{1,0:T(8,128)(2,1)S(1)} %get-tuple-element.50), channel_id=1, source_target_pairs={{2,6},{6,10},{10,14},{3,7},{7,11},{11,15},{4,0},{8,4},{12,8},{5,1}... | collective-permute-start | bytes 1966088 | tf_op jit(solution)/shard_map/ppermute | solution.py:22
  56.3 1.5 %collective-permute-start.8 = (bf16[128,2560]{1,0:T(8,128)(2,1)S(1)}, bf16[128,2560]{1,0:T(8,128)(2,1)S(1)}, u32[]{:S(2)}, u32[]{:S(2)}) collective-permute-start(bf16[128,2560]{1,0:T(8,128)(2,1)S(1)} %get-tuple-element.51), channel_id=1, source_target_pairs={{0,2},{1,3},{2,0},{3,1},{4,6},{5,7},{6,4},{7,5},{8,10},{9,11},{10,... | collective-permute-start | bytes 1966088 | tf_op jit(solution)/shard_map/ppermute | solution.py:22
  57.8 3.2 %collective-permute-start.6 = (bf16[256,2560]{1,0:T(8,128)(2,1)}, bf16[256,2560]{1,0:T(8,128)(2,1)S(1)}, u32[]{:S(2)}, u32[]{:S(2)}) collective-permute-start(bf16[256,2560]{1,0:T(8,128)(2,1)} %collective-permute-done.crossed), channel_id=1, source_target_pairs={{0,4},{4,8},{8,12},{1,5},{5,9},{9,13},{6,2},{10,6},{14,10},{7,3},{... | collective-permute-start | bytes 3932168 | tf_op jit(solution)/shard_map/ppermute | solution.py:22
  61.0 6.7 %shard_map.58 = (f32[256,2560]{1,0:T(8,128)S(1)}, f32[256,2560]{1,0:T(8,128)S(1)}, f32[256,2560]{1,0:T(8,128)S(1)}) custom-call(s32[16,64]{1,0:T(8,128)S(1)} %bitcast.4, s32[1,4,2]{2,1,0:T(4,128)S(1)} %copy.13.counts, bf16[256,2560]{1,0:T(8,128)(2,1)S(1)} %copy-done, bf16[256,2560]{1,0:T(8,128)(2,1)} %collective-permute-done.crossed, ...), custom_call_target="tpu_custom_call" | custom-call | flops 1000 | bytes 1000 | tf_op jit(solution)/shard_map/pallas_call | solution.py:345
  67.8 4.0 %collective-permute-done.7 = bf16[128,2560]{1,0:T(8,128)(2,1)S(1)} collective-permute-done((bf16[128,2560]{1,0:T(8,128)(2,1)S(1)}, bf16[128,2560]{1,0:T(8,128)(2,1)S(1)}, u32[]{:S(2)}, u32[]{:S(2)}) %collective-permute-start.7) | collective-permute-done | bytes 655392 | tf_op jit(solution)/shard_map/ppermute | solution.py:22
  71.8 2.1 %collective-permute-done.8.rest = bf16[128,2560]{1,0:T(8,128)(2,1)S(1)} collective-permute-done((bf16[128,2560]{1,0:T(8,128)(2,1)S(1)}, bf16[128,2560]{1,0:T(8,128)(2,1)S(1)}, u32[]{:S(2)}, u32[]{:S(2)}) %collective-permute-start.8) | collective-permute-done | bytes 655392 | tf_op jit(solution)/shard_map/ppermute | solution.py:22
  73.9 1.3 %collective-permute-start.11 = (bf16[128,2560]{1,0:T(8,128)(2,1)S(1)}, bf16[128,2560]{1,0:T(8,128)(2,1)S(1)}, u32[]{:S(2)}, u32[]{:S(2)}) collective-permute-start(bf16[128,2560]{1,0:T(8,128)(2,1)S(1)} %collective-permute-done.7), channel_id=1, source_target_pairs={{0,2},{1,3},{2,0},{3,1},{4,6},{5,7},{6,4},{7,5},{8,10},{9,11},{10,... | collective-permute-start | bytes 1966088 | tf_op jit(solution)/shard_map/ppermute | solution.py:22
  75.2 14.3 %collective-permute-done.6.passed = bf16[256,2560]{1,0:T(8,128)(2,1)S(1)} collective-permute-done((bf16[256,2560]{1,0:T(8,128)(2,1)}, bf16[256,2560]{1,0:T(8,128)(2,1)S(1)}, u32[]{:S(2)}, u32[]{:S(2)}) %collective-permute-start.6) | collective-permute-done | bytes 1310752 | tf_op jit(solution)/shard_map/ppermute | solution.py:22
  90.5 1.3 %collective-permute-start.12 = (bf16[256,2560]{1,0:T(8,128)(2,1)S(1)}, bf16[256,2560]{1,0:T(8,128)(2,1)S(1)}, u32[]{:S(2)}, u32[]{:S(2)}) collective-permute-start(bf16[256,2560]{1,0:T(8,128)(2,1)S(1)} %collective-permute-done.6.passed), channel_id=1, source_target_pairs={{1,0},{5,4},{9,8},{13,12},{2,3},{6,7},{10,11},{14,15},{17,16},{21,... | collective-permute-start | bytes 3932168 | tf_op jit(solution)/shard_map/ppermute | solution.py:22
  91.8 1.3 %collective-permute-start.13 = (bf16[128,2560]{1,0:T(8,128)(2,1)S(1)}, bf16[128,2560]{1,0:T(8,128)(2,1)S(1)}, u32[]{:S(2)}, u32[]{:S(2)}) collective-permute-start(bf16[128,2560]{1,0:T(8,128)(2,1)S(1)} %collective-permute-done.11.third), channel_id=1, source_target_pairs={{0,1},{1,0},{2,3},{3,2},{4,5},{5,4},{6,7},{7,6},{8,9},{9,8},{10,11... | collective-permute-start | bytes 1966088 | tf_op jit(solution)/shard_map/ppermute | solution.py:22
  93.1 3.0 %shard_map.59 = (f32[256,2560]{1,0:T(8,128)S(1)}, f32[256,2560]{1,0:T(8,128)S(1)}, f32[256,2560]{1,0:T(8,128)S(1)}) custom-call(s32[16,64]{1,0:T(8,128)S(1)} %bitcast.5, s32[1,4,2]{2,1,0:T(4,128)S(1)} %copy.13.counts, bf16[256,2560]{1,0:T(8,128)(2,1)S(1)} %copy-done, bf16[128,2560]{1,0:T(8,128)(2,1)S(1)} %collective-permute-done.8.rest, ...), custom_call_target="tpu_custom_call" | custom-call | flops 1000 | bytes 1000 | tf_op jit(solution)/shard_map/pallas_call | solution.py:345
  96.4 4.2 %shard_map.60 = bf16[256,2560]{1,0:T(8,128)(2,1)} custom-call(s32[16,64]{1,0:T(8,128)S(1)} %bitcast.6, s32[1,4,2]{2,1,0:T(4,128)S(1)} %copy.13.counts, bf16[256,2560]{1,0:T(8,128)(2,1)S(1)} %copy-done, bf16[256,2560]{1,0:T(8,128)(2,1)S(1)} %collective-permute-done.12.passed_core, bf16[128,2560]{1,0:T(8,128)(2,1)S(1)} %collective-permute-done.11.third, ...), custom_call_target="tpu_custom_call" | custom-call | flops 1000 | bytes 1000 | tf_op jit(solution)/shard_map/pallas_call | solution.py:345
  (21 shorter events, 2.8 us)
Async XLA Ops:
  0.0 2.4 %copy-start.1 = (s32[1,4,2,8]{3,2,1,0:T(2,128)S(1)}, s32[1,4,2,8]{3,2,1,0:T(2,128)}, u32[]{:S(2)}) copy-start(s32[1,4,2,8]{3,2,1,0:T(2,128)} %param.8) | copy-start | bytes 772
  1.9 27.4 %copy-start.2 = (s32[1,4,2]{1,2,0:T(2,128)S(1)}, s32[1,4,2]{1,2,0:T(2,128)}, u32[]{:S(2)}) copy-start(s32[1,4,2]{1,2,0:T(2,128)} %param.9) | copy-start | bytes 100
  1.9 26.1 %collective-permute-start.1 = (bf16[512,2560]{1,0:T(8,128)(2,1)S(1)}, bf16[512,2560]{1,0:T(8,128)(2,1)}, u32[]{:S(2)}, u32[]{:S(2)}) collective-permute-start(bf16[512,2560]{1,0:T(8,128)(2,1)S(1)} %pad_maximum_fusion.own), channel_id=1, source_target_pairs={{0,1},{1,0},{2,3},{3,2},{4,5},{5,4},{6,7},{7,6},{8,9},{9,8},{10,11... | collective-permute-start | bytes 7864328 | tf_op jit(solution)/shard_map/ppermute | solution.py:22
  18.4 35.2 %collective-permute-start = (bf16[256,2560]{1,0:T(8,128)(2,1)}, bf16[256,2560]{1,0:T(8,128)(2,1)}, u32[]{:S(2)}, u32[]{:S(2)}) collective-permute-start(bf16[256,2560]{1,0:T(8,128)(2,1)} %get-tuple-element.39), channel_id=1, source_target_pairs={{0,2},{1,3},{2,0},{3,1},{4,6},{5,7},{6,4},{7,5},{8,10},{9,11},{10,... | collective-permute-start | bytes 3932168 | tf_op jit(solution)/shard_map/ppermute | solution.py:22
  18.9 34.7 %collective-permute-start.2 = (bf16[128,2560]{1,0:T(8,128)(2,1)}, bf16[128,2560]{1,0:T(8,128)(2,1)S(1)}, u32[]{:S(2)}, u32[]{:S(2)}) collective-permute-start(bf16[128,2560]{1,0:T(8,128)(2,1)} %get-tuple-element.45), channel_id=1, source_target_pairs={{0,4},{1,5},{2,6},{3,7},{4,8},{5,9},{6,10},{7,11},{8,12},{9,13},{1... | collective-permute-start | bytes 1966088 | tf_op jit(solution)/shard_map/ppermute | solution.py:22
  21.4 32.2 %collective-permute-start.3 = (bf16[128,2560]{1,0:T(8,128)(2,1)}, bf16[128,2560]{1,0:T(8,128)(2,1)}, u32[]{:S(2)}, u32[]{:S(2)}) collective-permute-start(bf16[128,2560]{1,0:T(8,128)(2,1)} %get-tuple-element.46), channel_id=1, source_target_pairs={{4,0},{5,1},{6,2},{7,3},{8,4},{9,5},{10,6},{11,7},{12,8},{13,9},{1... | collective-permute-start | bytes 1966088 | tf_op jit(solution)/shard_map/ppermute | solution.py:22
  22.7 19.8 %collective-permute-start.4 = (bf16[64,2560]{1,0:T(8,128)(2,1)}, bf16[64,2560]{1,0:T(8,128)(2,1)}, u32[]{:S(2)}, u32[]{:S(2)}) collective-permute-start(bf16[64,2560]{1,0:T(8,128)(2,1)} %get-tuple-element.47), channel_id=1, source_target_pairs={{0,8},{1,9},{2,10},{3,11},{4,12},{5,13},{6,14},{7,15},{16,24},{17,... | collective-permute-start | bytes 983048 | tf_op jit(solution)/shard_map/ppermute | solution.py:22
  28.0 25.6 %collective-permute-start.5 = (bf16[64,2560]{1,0:T(8,128)(2,1)}, bf16[64,2560]{1,0:T(8,128)(2,1)}, u32[]{:S(2)}, u32[]{:S(2)}) collective-permute-start(bf16[64,2560]{1,0:T(8,128)(2,1)} %get-tuple-element.48), channel_id=1, source_target_pairs={{8,0},{9,1},{10,2},{11,3},{12,4},{13,5},{14,6},{15,7},{24,16},{25,... | collective-permute-start | bytes 983048 | tf_op jit(solution)/shard_map/ppermute | solution.py:22
  29.4 2.1 %copy-start = (bf16[256,2560]{1,0:T(8,128)(2,1)S(1)}, bf16[256,2560]{1,0:T(8,128)(2,1)}, u32[]{:S(2)}) copy-start(bf16[256,2560]{1,0:T(8,128)(2,1)} %q.7) | copy-start | bytes 3932164
  53.6 7.4 %collective-permute-start.9 = (bf16[256,2560]{1,0:T(8,128)(2,1)}, bf16[256,2560]{1,0:T(8,128)(2,1)S(1)}, u32[]{:S(2)}, u32[]{:S(2)}) collective-permute-start(bf16[256,2560]{1,0:T(8,128)(2,1)} %collective-permute-done.crossed), channel_id=1, source_target_pairs={{0,1},{4,5},{8,9},{12,13},{3,2},{7,6},{11,10},{15,14},{16,17},{20,... | collective-permute-start | bytes 3932168 | tf_op jit(solution)/shard_map/ppermute | solution.py:22
  55.0 16.8 %collective-permute-start.7 = (bf16[128,2560]{1,0:T(8,128)(2,1)S(1)}, bf16[128,2560]{1,0:T(8,128)(2,1)S(1)}, u32[]{:S(2)}, u32[]{:S(2)}) collective-permute-start(bf16[128,2560]{1,0:T(8,128)(2,1)S(1)} %get-tuple-element.50), channel_id=1, source_target_pairs={{2,6},{6,10},{10,14},{3,7},{7,11},{11,15},{4,0},{8,4},{12,8},{5,1}... | collective-permute-start | bytes 1966088 | tf_op jit(solution)/shard_map/ppermute | solution.py:22
  56.3 17.6 %collective-permute-start.8 = (bf16[128,2560]{1,0:T(8,128)(2,1)S(1)}, bf16[128,2560]{1,0:T(8,128)(2,1)S(1)}, u32[]{:S(2)}, u32[]{:S(2)}) collective-permute-start(bf16[128,2560]{1,0:T(8,128)(2,1)S(1)} %get-tuple-element.51), channel_id=1, source_target_pairs={{0,2},{1,3},{2,0},{3,1},{4,6},{5,7},{6,4},{7,5},{8,10},{9,11},{10,... | collective-permute-start | bytes 1966088 | tf_op jit(solution)/shard_map/ppermute | solution.py:22
  57.8 31.7 %collective-permute-start.6 = (bf16[256,2560]{1,0:T(8,128)(2,1)}, bf16[256,2560]{1,0:T(8,128)(2,1)S(1)}, u32[]{:S(2)}, u32[]{:S(2)}) collective-permute-start(bf16[256,2560]{1,0:T(8,128)(2,1)} %collective-permute-done.crossed), channel_id=1, source_target_pairs={{0,4},{4,8},{8,12},{1,5},{5,9},{9,13},{6,2},{10,6},{14,10},{7,3},{... | collective-permute-start | bytes 3932168 | tf_op jit(solution)/shard_map/ppermute | solution.py:22
  73.9 16.7 %collective-permute-start.11 = (bf16[128,2560]{1,0:T(8,128)(2,1)S(1)}, bf16[128,2560]{1,0:T(8,128)(2,1)S(1)}, u32[]{:S(2)}, u32[]{:S(2)}) collective-permute-start(bf16[128,2560]{1,0:T(8,128)(2,1)S(1)} %collective-permute-done.7), channel_id=1, source_target_pairs={{0,2},{1,3},{2,0},{3,1},{4,6},{5,7},{6,4},{7,5},{8,10},{9,11},{10,... | collective-permute-start | bytes 1966088 | tf_op jit(solution)/shard_map/ppermute | solution.py:22
  75.1 15.4 %collective-permute-start.10 = (bf16[128,2560]{1,0:T(8,128)(2,1)S(1)}, bf16[128,2560]{1,0:T(8,128)(2,1)S(1)}, u32[]{:S(2)}, u32[]{:S(2)}) collective-permute-start(bf16[128,2560]{1,0:T(8,128)(2,1)S(1)} %collective-permute-done.8.rest), channel_id=1, source_target_pairs={{0,1},{1,0},{2,3},{3,2},{4,5},{5,4},{6,7},{7,6},{8,9},{9,8},{10,11... | collective-permute-start | bytes 1966088 | tf_op jit(solution)/shard_map/ppermute | solution.py:22
  90.5 5.9 %collective-permute-start.12 = (bf16[256,2560]{1,0:T(8,128)(2,1)S(1)}, bf16[256,2560]{1,0:T(8,128)(2,1)S(1)}, u32[]{:S(2)}, u32[]{:S(2)}) collective-permute-start(bf16[256,2560]{1,0:T(8,128)(2,1)S(1)} %collective-permute-done.6.passed), channel_id=1, source_target_pairs={{1,0},{5,4},{9,8},{13,12},{2,3},{6,7},{10,11},{14,15},{17,16},{21,... | collective-permute-start | bytes 3932168 | tf_op jit(solution)/shard_map/ppermute | solution.py:22
  91.8 4.6 %collective-permute-start.13 = (bf16[128,2560]{1,0:T(8,128)(2,1)S(1)}, bf16[128,2560]{1,0:T(8,128)(2,1)S(1)}, u32[]{:S(2)}, u32[]{:S(2)}) collective-permute-start(bf16[128,2560]{1,0:T(8,128)(2,1)S(1)} %collective-permute-done.11.third), channel_id=1, source_target_pairs={{0,1},{1,0},{2,3},{3,2},{4,5},{5,4},{6,7},{7,6},{8,9},{9,8},{10,11... | collective-permute-start | bytes 1966088 | tf_op jit(solution)/shard_map/ppermute | solution.py:22

commit v4 on v3

--- a/solution.py
+++ b/solution.py
@@ -242,7 +242,7 @@
     over_heads(shape["width"], head)
 
 
-def quad_kernel(shape, lists, counts, q, crossed, crossed_core, *refs):
+def quad_kernel(shape, lists, counts, q, crossed, *refs):
     far, before, after, flags, found = refs[:-8], refs[-8:-5], refs[-5:-2], refs[-2], refs[-1]
     me = lax.axis_index("ctx")
     spot = me % 4
@@ -264,9 +264,7 @@
     @pl.when(jnp.logical_not(outer))
     def _():
         order_flags(flags, begun, half, counts, 1, near_side)
-        names, _ = crossing_names(found, lists, me, jnp.where(spot == 1, me + 1, me - 1), shape)
-        member_flags(flags, begun + half, names, lists, counts, me, 0, me % 2, shape)
-        more_heads(shape, flags, begun + 2 * half, q, before, after, [*far, crossed, crossed_core])
+        more_heads(shape, flags, begun + half, q, before, after, [*far, crossed])
 
 
 def giver_names(found, lists, me, shape):
@@ -280,30 +278,46 @@
     return names, [found[j] for j in range(half)]
 
 
-def passed_kernel(shape, lists, counts, q, rest, rest_core, passed, *refs):
+def rest_kernel(shape, lists, counts, q, rest, rest_core, *refs):
     before, after, flags, found = refs[:3], refs[3:6], refs[6], refs[7]
     me = lax.axis_index("ctx")
     spot = me % 4
-    blocks = shape["blocks"]
-    half = blocks // 2
-    quarter = blocks // 4
+    quarter = shape["blocks"] // 4
+    outer = jnp.logical_or(spot == 0, spot == 3)
+
+    @pl.when(outer)
+    def _():
+        _, ids = crossing_names(found, lists, me, jnp.where(spot == 0, me + 2, me - 2), shape)
+        member_flags(flags, 0, ids, lists, counts, me, 1, jnp.where(spot < 2, 1, 0), shape)
+
+    @pl.when(jnp.logical_not(outer))
+    def _():
+        _, ids = crossing_names(found, lists, me, jnp.where(spot == 1, me + 1, me - 1), shape)
+        member_flags(flags, 0, ids[quarter:] + ids[:quarter], lists, counts, me, 0, me % 2, shape)
+
+    more_heads(shape, flags, 2 * quarter, q, before, after, [rest, rest_core])
+
+
+def passed_kernel(shape, lists, counts, q, crossed_core, passed, *refs):
+    before, after, flags, found = refs[:3], refs[3:6], refs[6], refs[7]
+    me = lax.axis_index("ctx")
+    spot = me % 4
+    half = shape["blocks"] // 2
     outer = jnp.logical_or(spot == 0, spot == 3)
     far_side = jnp.where(spot < 2, 0, 1)
 
     @pl.when(outer)
     def _():
-        _, others_ = crossing_names(found, lists, me, jnp.where(spot == 0, me + 2, me - 2), shape)
-        member_flags(flags, 0, others_, lists, counts, me, 1, jnp.where(spot < 2, 1, 0), shape)
-        order_flags(flags, half, half, counts, 1, far_side)
-
-    @pl.when(jnp.logical_not(outer))
-    def _():
-        _, others_ = crossing_names(found, lists, me, jnp.where(spot == 1, me + 1, me - 1), shape)
-        member_flags(flags, 0, others_[quarter:] + others_[:quarter], lists, counts, me, 0, me % 2, shape)
+        order_flags(flags, 0, half, counts, 1, far_side)
+        more_heads(shape, flags, half, q, before, after, [passed])
+
+    @pl.when(jnp.logical_not(outer))
+    def _():
+        names, _ = crossing_names(found, lists, me, jnp.where(spot == 1, me + 1, me - 1), shape)
+        member_flags(flags, 0, names, lists, counts, me, 0, me % 2, shape)
         names, _ = giver_names(found, lists, me, shape)
         member_flags(flags, half, names, lists, counts, me, 1, far_side, shape)
-
-    more_heads(shape, flags, 2 * half, q, before, after, [rest, rest_core, passed])
+        more_heads(shape, flags, 2 * half, q, before, after, [crossed_core, passed])
 
 
 def last_kernel(shape, lists, counts, q, passed_core, third, third_core, *refs):
@@ -399,17 +413,21 @@
     )
     passed = permute(crossed, devices, pass_on)
     rest = permute(rest_pack, devices, over_y)
-    crossed_core = permute(crossed, devices, outer_in)
     along = permute(along_pack, devices, outward)
-    state = attend_call(quad_kernel, shape, smem, (queries, crossed, crossed_core, *far), state, False, chosen)
-
-    along, rest, state = lax.optimization_barrier((along, rest, state))
+    state = attend_call(quad_kernel, shape, smem, (queries, crossed, *far), state, False, chosen)
+
+    along, rest, crossed, state = lax.optimization_barrier((along, rest, crossed, state))
     third = permute(along, devices, over_y)
     rest_core = permute(rest, devices, other_core)
-    passed, rest_core, third = lax.optimization_barrier((passed, rest_core, third))
+    crossed_core = permute(crossed, devices, outer_in)
+    state = attend_call(rest_kernel, shape, smem, (queries, rest, rest_core), state, False, chosen)
+    passed, third, state = lax.optimization_barrier((passed, third, state))
     passed_core = permute(passed, devices, inner_out)
+    third, crossed_core = lax.optimization_barrier((third, crossed_core))
     third_core = permute(third, devices, other_core)
-    state = attend_call(passed_kernel, shape, smem, (queries, rest, rest_core, passed), state, False, chosen)
+    state = attend_call(
+        passed_kernel, shape, smem, (queries, crossed_core, passed), state, False, chosen
+    )
     return attend_call(last_kernel, shape, smem, (queries, passed_core, third, third_core), state, True, chosen)
 
 

time: 102 us -> 99.1 us (0.972)
  waiting for transfers between devices: 38.8 us -> 31.1 us
  Pallas kernels: 23.7 us -> 29 us
    ppermute x14, waiting for transfers between devices: 38.8 us -> 31.1 us  [permute(): return lax.ppermute(block, 'ctx', pairs)]
    pallas_call x4 -> x5, Pallas kernels: 19 us -> 24.3 us  [attend_call(): pl.pallas_call(functools.partial(body, shape), out_shape=jax.ShapeDtypeSt...]
  transfers between devices with their start and end apart: 14 -> 14, of which waited for: 7 -> 4; matrix products, arithmetic and copies ran while one was open for 0% -> 0% of each run, Pallas kernels for 19% -> 25%
where the time goes in v4:
time: 99.1 us; the launch traced here: 98.7 us
  waiting for transfers between devices  31.1 us (31%)
  Pallas kernels  29 us (29%)
  starting transfers between devices  23.1 us (23%)
  blocking collectives  13.3 us (13%)
  other arithmetic  1.89 us (2%)
    ppermute x14, waiting for transfers between devices, permute(): return lax.ppermute(block, 'ctx', pairs)  31.1 us
    pallas_call x5, Pallas kernels, attend_call(): pl.pallas_call(functools.partial(body, shape), out_shape=jax.ShapeDtypeSt...  24.3 us
    ppermute x14, starting transfers between devices, permute(): return lax.ppermute(block, 'ctx', pairs)  23.1 us
    all_to_all x1, blocking collectives, shards(): lists = lax.all_to_all(sent, 'ctx', 0, 0, tiled=True)  13.3 us
    pallas_call x2, Pallas kernels, pack_call(): pl.pallas_call(functools.partial(body, shape), out_shape=tuple((jax.Shape...  4.64 us
  transfers between devices with their start and end apart: 14, of which 4 were waited for; matrix products, arithmetic and copies ran while one was open for 0% of the time, Pallas kernels for 25%

profile of v4, /device:TPU:0, one launch (start us, length us, event | category | flops | bytes accessed | tf_op | source)
XLA Modules:
  0.0 98.7 jit_solution(2496062155375977776)
XLA Ops:
  0.0 1.9 %pad_maximum_fusion.own = bf16[512,2560]{1,0:T(8,128)(2,1)S(1)} fusion(bf16[256,2560]{1,0:T(8,128)(2,1)} %param.7, bf16[256,2560]{1,0:T(8,128)(2,1)} %param.6), kind=kLoop, calls=%fused_computation | loop fusion | flops 5242880 | bytes 5242880 | tf_op jit(solution)/shard_map/concatenate | solution.py:397
  2.5 13.3 %all_to_all.8 = s32[16,1,64]{2,1,0:T(1,128)S(1)} all-to-all(s32[16,1,64]{2,1,0:T(1,128)S(1)} %broadcast_in_dim.8), channel_id=1, replica_groups=mesh['groups'=2,'ctx'=16] {'ctx'}, dimensions={0} | all-to-all | bytes 8192 | tf_op jit(solution)/shard_map/all_to_all | solution.py:395
  15.8 2.6 %shard_map.55 = (bf16[256,2560]{1,0:T(8,128)(2,1)}, bf16[128,2560]{1,0:T(8,128)(2,1)}, bf16[128,2560]{1,0:T(8,128)(2,1)}, bf16[64,2560]{1,0:T(8,128)(2,1)}, bf16[64,2560]{1,0:T(8,128)(2,1)}) custom-call(s32[16,64]{1,0:T(8,128)S(1)} %bitcast.1, bf16[512,2560]{1,0:T(8,128)(2,1)S(1)} %pad_maximum_fusion.own), custom_call_target="tpu_custom_call" | custom-call | flops 1000 | bytes 1000 | tf_op jit(solution)/shard_map/pallas_call | solution.py:115
  18.9 2.5 %collective-permute-start.2 = (bf16[128,2560]{1,0:T(8,128)(2,1)}, bf16[128,2560]{1,0:T(8,128)(2,1)S(1)}, u32[]{:S(2)}, u32[]{:S(2)}) collective-permute-start(bf16[128,2560]{1,0:T(8,128)(2,1)} %get-tuple-element.53), channel_id=1, source_target_pairs={{0,4},{1,5},{2,6},{3,7},{4,8},{5,9},{6,10},{7,11},{8,12},{9,13},{1... | collective-permute-start | bytes 1966088 | tf_op jit(solution)/shard_map/ppermute | solution.py:22
  21.4 1.3 %collective-permute-start.3 = (bf16[128,2560]{1,0:T(8,128)(2,1)}, bf16[128,2560]{1,0:T(8,128)(2,1)}, u32[]{:S(2)}, u32[]{:S(2)}) collective-permute-start(bf16[128,2560]{1,0:T(8,128)(2,1)} %get-tuple-element.54), channel_id=1, source_target_pairs={{4,0},{5,1},{6,2},{7,3},{8,4},{9,5},{10,6},{11,7},{12,8},{13,9},{1... | collective-permute-start | bytes 1966088 | tf_op jit(solution)/shard_map/ppermute | solution.py:22
  22.7 5.3 %collective-permute-start.4 = (bf16[64,2560]{1,0:T(8,128)(2,1)}, bf16[64,2560]{1,0:T(8,128)(2,1)}, u32[]{:S(2)}, u32[]{:S(2)}) collective-permute-start(bf16[64,2560]{1,0:T(8,128)(2,1)} %get-tuple-element.55), channel_id=1, source_target_pairs={{0,8},{1,9},{2,10},{3,11},{4,12},{5,13},{6,14},{7,15},{16,24},{17,... | collective-permute-start | bytes 983048 | tf_op jit(solution)/shard_map/ppermute | solution.py:22
  28.0 1.3 %collective-permute-start.5 = (bf16[64,2560]{1,0:T(8,128)(2,1)}, bf16[64,2560]{1,0:T(8,128)(2,1)}, u32[]{:S(2)}, u32[]{:S(2)}) collective-permute-start(bf16[64,2560]{1,0:T(8,128)(2,1)} %get-tuple-element.56), channel_id=1, source_target_pairs={{8,0},{9,1},{10,2},{11,3},{12,4},{13,5},{14,6},{15,7},{24,16},{25,... | collective-permute-start | bytes 983048 | tf_op jit(solution)/shard_map/ppermute | solution.py:22
  29.4 2.0 %shard_map.56 = (bf16[128,2560]{1,0:T(8,128)(2,1)S(1)}, bf16[128,2560]{1,0:T(8,128)(2,1)S(1)}) custom-call(s32[16,64]{1,0:T(8,128)S(1)} %bitcast.2, bf16[512,2560]{1,0:T(8,128)(2,1)S(1)} %pad_maximum_fusion.own, bf16[512,2560]{1,0:T(8,128)(2,1)} %collective-permute-done.1.other), custom_call_target="tpu_custom_call" | custom-call | flops 1000 | bytes 1000 | tf_op jit(solution)/shard_map/pallas_call | solution.py:115
  31.5 5.1 %shard_map.57 = (f32[256,2560]{1,0:T(8,128)S(1)}, f32[256,2560]{1,0:T(8,128)S(1)}, f32[256,2560]{1,0:T(8,128)S(1)}) custom-call(s32[16,64]{1,0:T(8,128)S(1)} %bitcast.3, s32[1,4,2]{2,1,0:T(4,128)S(1)} %copy.15.counts, bf16[256,2560]{1,0:T(8,128)(2,1)S(1)} %copy-done, bf16[512,2560]{1,0:T(8,128)(2,1)S(1)} %pad_maximum_fusion.own, ...), custom_call_target="tpu_custom_call" | custom-call | flops 1000 | bytes 1000 | tf_op jit(solution)/shard_map/pallas_call | solution.py:359
  36.6 5.9 %collective-permute-done.4.refs_2_ = bf16[64,2560]{1,0:T(8,128)(2,1)} collective-permute-done((bf16[64,2560]{1,0:T(8,128)(2,1)}, bf16[64,2560]{1,0:T(8,128)(2,1)}, u32[]{:S(2)}, u32[]{:S(2)}) %collective-permute-start.4) | collective-permute-done | bytes 327712 | tf_op jit(solution)/shard_map/ppermute | solution.py:22
  42.5 11.1 %collective-permute-done.5.refs_3_ = bf16[64,2560]{1,0:T(8,128)(2,1)} collective-permute-done((bf16[64,2560]{1,0:T(8,128)(2,1)}, bf16[64,2560]{1,0:T(8,128)(2,1)}, u32[]{:S(2)}, u32[]{:S(2)}) %collective-permute-start.5) | collective-permute-done | bytes 327712 | tf_op jit(solution)/shard_map/ppermute | solution.py:22
  53.6 1.3 %collective-permute-start.7 = (bf16[128,2560]{1,0:T(8,128)(2,1)S(1)}, bf16[128,2560]{1,0:T(8,128)(2,1)S(1)}, u32[]{:S(2)}, u32[]{:S(2)}) collective-permute-start(bf16[128,2560]{1,0:T(8,128)(2,1)S(1)} %get-tuple-element.58), channel_id=1, source_target_pairs={{2,6},{6,10},{10,14},{3,7},{7,11},{11,15},{4,0},{8,4},{12,8},{5,1}... | collective-permute-start | bytes 1966088 | tf_op jit(solution)/shard_map/ppermute | solution.py:22
  54.9 1.6 %collective-permute-start.8 = (bf16[128,2560]{1,0:T(8,128)(2,1)S(1)}, bf16[128,2560]{1,0:T(8,128)(2,1)S(1)}, u32[]{:S(2)}, u32[]{:S(2)}) collective-permute-start(bf16[128,2560]{1,0:T(8,128)(2,1)S(1)} %get-tuple-element.59), channel_id=1, source_target_pairs={{0,2},{1,3},{2,0},{3,1},{4,6},{5,7},{6,4},{7,5},{8,10},{9,11},{10,... | collective-permute-start | bytes 1966088 | tf_op jit(solution)/shard_map/ppermute | solution.py:22
  56.5 3.2 %collective-permute-start.6 = (bf16[256,2560]{1,0:T(8,128)(2,1)}, bf16[256,2560]{1,0:T(8,128)(2,1)S(1)}, u32[]{:S(2)}, u32[]{:S(2)}) collective-permute-start(bf16[256,2560]{1,0:T(8,128)(2,1)} %collective-permute-done.crossed), channel_id=1, source_target_pairs={{0,4},{4,8},{8,12},{1,5},{5,9},{9,13},{6,2},{10,6},{14,10},{7,3},{... | collective-permute-start | bytes 3932168 | tf_op jit(solution)/shard_map/ppermute | solution.py:22
  59.6 6.7 %shard_map.58 = (f32[256,2560]{1,0:T(8,128)S(1)}, f32[256,2560]{1,0:T(8,128)S(1)}, f32[256,2560]{1,0:T(8,128)S(1)}) custom-call(s32[16,64]{1,0:T(8,128)S(1)} %bitcast.4, s32[1,4,2]{2,1,0:T(4,128)S(1)} %copy.15.counts, bf16[256,2560]{1,0:T(8,128)(2,1)S(1)} %copy-done, bf16[256,2560]{1,0:T(8,128)(2,1)} %collective-permute-done.crossed, ...), custom_call_target="tpu_custom_call" | custom-call | flops 1000 | bytes 1000 | tf_op jit(solution)/shard_map/pallas_call | solution.py:359
  66.4 4.1 %collective-permute-done.7 = bf16[128,2560]{1,0:T(8,128)(2,1)S(1)} collective-permute-done((bf16[128,2560]{1,0:T(8,128)(2,1)S(1)}, bf16[128,2560]{1,0:T(8,128)(2,1)S(1)}, u32[]{:S(2)}, u32[]{:S(2)}) %collective-permute-start.7) | collective-permute-done | bytes 655392 | tf_op jit(solution)/shard_map/ppermute | solution.py:22
  70.5 1.0 collective-permute-start.9
  71.5 2.2 %collective-permute-start.12 = (bf16[256,2560]{1,0:T(8,128)(2,1)}, bf16[256,2560]{1,0:T(8,128)(2,1)S(1)}, u32[]{:S(2)}, u32[]{:S(2)}) collective-permute-start(bf16[256,2560]{1,0:T(8,128)(2,1)} %collective-permute-done.crossed), channel_id=1, source_target_pairs={{0,1},{4,5},{8,9},{12,13},{3,2},{7,6},{11,10},{15,14},{16,17},{20,... | collective-permute-start | bytes 3932168 | tf_op jit(solution)/shard_map/ppermute | solution.py:22
  73.7 4.0 %shard_map.59 = (f32[256,2560]{1,0:T(8,128)S(1)}, f32[256,2560]{1,0:T(8,128)S(1)}, f32[256,2560]{1,0:T(8,128)S(1)}) custom-call(s32[16,64]{1,0:T(8,128)S(1)} %bitcast.5, s32[1,4,2]{2,1,0:T(4,128)S(1)} %copy.15.counts, bf16[256,2560]{1,0:T(8,128)(2,1)S(1)} %copy-done, bf16[128,2560]{1,0:T(8,128)(2,1)S(1)} %collective-permute-done.8.rest, ...), custom_call_target="tpu_custom_call" | custom-call | flops 1000 | bytes 1000 | tf_op jit(solution)/shard_map/pallas_call | solution.py:359
  77.7 9.9 %collective-permute-done.9.third = bf16[128,2560]{1,0:T(8,128)(2,1)S(1)} collective-permute-done((bf16[128,2560]{1,0:T(8,128)(2,1)S(1)}, bf16[128,2560]{1,0:T(8,128)(2,1)S(1)}, u32[]{:S(2)}, u32[]{:S(2)}) %collective-permute-start.9) | collective-permute-done | bytes 655392 | tf_op jit(solution)/shard_map/ppermute | solution.py:22
  87.7 1.3 %collective-permute-start.11 = (bf16[256,2560]{1,0:T(8,128)(2,1)S(1)}, bf16[256,2560]{1,0:T(8,128)(2,1)S(1)}, u32[]{:S(2)}, u32[]{:S(2)}) collective-permute-start(bf16[256,2560]{1,0:T(8,128)(2,1)S(1)} %collective-permute-done.6.passed), channel_id=1, source_target_pairs={{1,0},{5,4},{9,8},{13,12},{2,3},{6,7},{10,11},{14,15},{17,16},{21,... | collective-permute-start | bytes 3932168 | tf_op jit(solution)/shard_map/ppermute | solution.py:22
  89.0 1.3 %collective-permute-start.13 = (bf16[128,2560]{1,0:T(8,128)(2,1)S(1)}, bf16[128,2560]{1,0:T(8,128)(2,1)S(1)}, u32[]{:S(2)}, u32[]{:S(2)}) collective-permute-start(bf16[128,2560]{1,0:T(8,128)(2,1)S(1)} %collective-permute-done.9.third), channel_id=1, source_target_pairs={{0,1},{1,0},{2,3},{3,2},{4,5},{5,4},{6,7},{7,6},{8,9},{9,8},{10,11... | collective-permute-start | bytes 1966088 | tf_op jit(solution)/shard_map/ppermute | solution.py:22
  90.2 4.2 %shard_map.60 = (f32[256,2560]{1,0:T(8,128)S(1)}, f32[256,2560]{1,0:T(8,128)S(1)}, f32[256,2560]{1,0:T(8,128)S(1)}) custom-call(s32[16,64]{1,0:T(8,128)S(1)} %bitcast.6, s32[1,4,2]{2,1,0:T(4,128)S(1)} %copy.15.counts, bf16[256,2560]{1,0:T(8,128)(2,1)S(1)} %copy-done, bf16[256,2560]{1,0:T(8,128)(2,1)S(1)} %collective-permute-done.12.crossed_core, ...), custom_call_target="tpu_custom_call" | custom-call | flops 1000 | bytes 1000 | tf_op jit(solution)/shard_map/pallas_call | solution.py:359
  94.4 4.3 %shard_map.61 = bf16[256,2560]{1,0:T(8,128)(2,1)} custom-call(s32[16,64]{1,0:T(8,128)S(1)} %bitcast.7, s32[1,4,2]{2,1,0:T(4,128)S(1)} %copy.15.counts, bf16[256,2560]{1,0:T(8,128)(2,1)S(1)} %copy-done, bf16[256,2560]{1,0:T(8,128)(2,1)S(1)} %collective-permute-done.11.passed_core, bf16[128,2560]{1,0:T(8,128)(2,1)S(1)} %collective-permute-done.9.third, ...), custom_call_target="tpu_custom_call" | custom-call | flops 1000 | bytes 1000 | tf_op jit(solution)/shard_map/pallas_call | solution.py:359
  (22 shorter events, 1.3 us)
Async XLA Ops:
  0.0 2.4 %copy-start.1 = (s32[1,4,2,8]{3,2,1,0:T(2,128)S(1)}, s32[1,4,2,8]{3,2,1,0:T(2,128)}, u32[]{:S(2)}) copy-start(s32[1,4,2,8]{3,2,1,0:T(2,128)} %param.8) | copy-start | bytes 772
  1.9 27.4 %copy-start.2 = (s32[1,4,2]{1,2,0:T(2,128)S(1)}, s32[1,4,2]{1,2,0:T(2,128)}, u32[]{:S(2)}) copy-start(s32[1,4,2]{1,2,0:T(2,128)} %param.9) | copy-start | bytes 100
  1.9 26.1 %collective-permute-start.1 = (bf16[512,2560]{1,0:T(8,128)(2,1)S(1)}, bf16[512,2560]{1,0:T(8,128)(2,1)}, u32[]{:S(2)}, u32[]{:S(2)}) collective-permute-start(bf16[512,2560]{1,0:T(8,128)(2,1)S(1)} %pad_maximum_fusion.own), channel_id=1, source_target_pairs={{0,1},{1,0},{2,3},{3,2},{4,5},{5,4},{6,7},{7,6},{8,9},{9,8},{10,11... | collective-permute-start | bytes 7864328 | tf_op jit(solution)/shard_map/ppermute | solution.py:22
  18.4 35.2 %collective-permute-start = (bf16[256,2560]{1,0:T(8,128)(2,1)}, bf16[256,2560]{1,0:T(8,128)(2,1)}, u32[]{:S(2)}, u32[]{:S(2)}) collective-permute-start(bf16[256,2560]{1,0:T(8,128)(2,1)} %get-tuple-element.47), channel_id=1, source_target_pairs={{0,2},{1,3},{2,0},{3,1},{4,6},{5,7},{6,4},{7,5},{8,10},{9,11},{10,... | collective-permute-start | bytes 3932168 | tf_op jit(solution)/shard_map/ppermute | solution.py:22
  18.9 34.7 %collective-permute-start.2 = (bf16[128,2560]{1,0:T(8,128)(2,1)}, bf16[128,2560]{1,0:T(8,128)(2,1)S(1)}, u32[]{:S(2)}, u32[]{:S(2)}) collective-permute-start(bf16[128,2560]{1,0:T(8,128)(2,1)} %get-tuple-element.53), channel_id=1, source_target_pairs={{0,4},{1,5},{2,6},{3,7},{4,8},{5,9},{6,10},{7,11},{8,12},{9,13},{1... | collective-permute-start | bytes 1966088 | tf_op jit(solution)/shard_map/ppermute | solution.py:22
  21.4 32.2 %collective-permute-start.3 = (bf16[128,2560]{1,0:T(8,128)(2,1)}, bf16[128,2560]{1,0:T(8,128)(2,1)}, u32[]{:S(2)}, u32[]{:S(2)}) collective-permute-start(bf16[128,2560]{1,0:T(8,128)(2,1)} %get-tuple-element.54), channel_id=1, source_target_pairs={{4,0},{5,1},{6,2},{7,3},{8,4},{9,5},{10,6},{11,7},{12,8},{13,9},{1... | collective-permute-start | bytes 1966088 | tf_op jit(solution)/shard_map/ppermute | solution.py:22
  22.7 19.8 %collective-permute-start.4 = (bf16[64,2560]{1,0:T(8,128)(2,1)}, bf16[64,2560]{1,0:T(8,128)(2,1)}, u32[]{:S(2)}, u32[]{:S(2)}) collective-permute-start(bf16[64,2560]{1,0:T(8,128)(2,1)} %get-tuple-element.55), channel_id=1, source_target_pairs={{0,8},{1,9},{2,10},{3,11},{4,12},{5,13},{6,14},{7,15},{16,24},{17,... | collective-permute-start | bytes 983048 | tf_op jit(solution)/shard_map/ppermute | solution.py:22
  28.0 25.6 %collective-permute-start.5 = (bf16[64,2560]{1,0:T(8,128)(2,1)}, bf16[64,2560]{1,0:T(8,128)(2,1)}, u32[]{:S(2)}, u32[]{:S(2)}) collective-permute-start(bf16[64,2560]{1,0:T(8,128)(2,1)} %get-tuple-element.56), channel_id=1, source_target_pairs={{8,0},{9,1},{10,2},{11,3},{12,4},{13,5},{14,6},{15,7},{24,16},{25,... | collective-permute-start | bytes 983048 | tf_op jit(solution)/shard_map/ppermute | solution.py:22
  29.4 2.1 %copy-start = (bf16[256,2560]{1,0:T(8,128)(2,1)S(1)}, bf16[256,2560]{1,0:T(8,128)(2,1)}, u32[]{:S(2)}) copy-start(bf16[256,2560]{1,0:T(8,128)(2,1)} %q.9) | copy-start | bytes 3932164
  53.6 16.9 %collective-permute-start.7 = (bf16[128,2560]{1,0:T(8,128)(2,1)S(1)}, bf16[128,2560]{1,0:T(8,128)(2,1)S(1)}, u32[]{:S(2)}, u32[]{:S(2)}) collective-permute-start(bf16[128,2560]{1,0:T(8,128)(2,1)S(1)} %get-tuple-element.58), channel_id=1, source_target_pairs={{2,6},{6,10},{10,14},{3,7},{7,11},{11,15},{4,0},{8,4},{12,8},{5,1}... | collective-permute-start | bytes 1966088 | tf_op jit(solution)/shard_map/ppermute | solution.py:22
  54.9 15.6 %collective-permute-start.8 = (bf16[128,2560]{1,0:T(8,128)(2,1)S(1)}, bf16[128,2560]{1,0:T(8,128)(2,1)S(1)}, u32[]{:S(2)}, u32[]{:S(2)}) collective-permute-start(bf16[128,2560]{1,0:T(8,128)(2,1)S(1)} %get-tuple-element.59), channel_id=1, source_target_pairs={{0,2},{1,3},{2,0},{3,1},{4,6},{5,7},{6,4},{7,5},{8,10},{9,11},{10,... | collective-permute-start | bytes 1966088 | tf_op jit(solution)/shard_map/ppermute | solution.py:22
  56.5 31.2 %collective-permute-start.6 = (bf16[256,2560]{1,0:T(8,128)(2,1)}, bf16[256,2560]{1,0:T(8,128)(2,1)S(1)}, u32[]{:S(2)}, u32[]{:S(2)}) collective-permute-start(bf16[256,2560]{1,0:T(8,128)(2,1)} %collective-permute-done.crossed), channel_id=1, source_target_pairs={{0,4},{4,8},{8,12},{1,5},{5,9},{9,13},{6,2},{10,6},{14,10},{7,3},{... | collective-permute-start | bytes 3932168 | tf_op jit(solution)/shard_map/ppermute | solution.py:22
  70.5 3.2 %collective-permute-start.10 = (bf16[128,2560]{1,0:T(8,128)(2,1)S(1)}, bf16[128,2560]{1,0:T(8,128)(2,1)S(1)}, u32[]{:S(2)}, u32[]{:S(2)}) collective-permute-start(bf16[128,2560]{1,0:T(8,128)(2,1)S(1)} %collective-permute-done.8.rest), channel_id=1, source_target_pairs={{0,1},{1,0},{2,3},{3,2},{4,5},{5,4},{6,7},{7,6},{8,9},{9,8},{10,11... | collective-permute-start | bytes 1966088 | tf_op jit(solution)/shard_map/ppermute | solution.py:22
  70.5 17.1 %collective-permute-start.9 = (bf16[128,2560]{1,0:T(8,128)(2,1)S(1)}, bf16[128,2560]{1,0:T(8,128)(2,1)S(1)}, u32[]{:S(2)}, u32[]{:S(2)}) collective-permute-start(bf16[128,2560]{1,0:T(8,128)(2,1)S(1)} %collective-permute-done.7), channel_id=1, source_target_pairs={{0,2},{1,3},{2,0},{3,1},{4,6},{5,7},{6,4},{7,5},{8,10},{9,11},{10,... | collective-permute-start | bytes 1966088 | tf_op jit(solution)/shard_map/ppermute | solution.py:22
  71.5 17.5 %collective-permute-start.12 = (bf16[256,2560]{1,0:T(8,128)(2,1)}, bf16[256,2560]{1,0:T(8,128)(2,1)S(1)}, u32[]{:S(2)}, u32[]{:S(2)}) collective-permute-start(bf16[256,2560]{1,0:T(8,128)(2,1)} %collective-permute-done.crossed), channel_id=1, source_target_pairs={{0,1},{4,5},{8,9},{12,13},{3,2},{7,6},{11,10},{15,14},{16,17},{20,... | collective-permute-start | bytes 3932168 | tf_op jit(solution)/shard_map/ppermute | solution.py:22
  87.7 6.8 %collective-permute-start.11 = (bf16[256,2560]{1,0:T(8,128)(2,1)S(1)}, bf16[256,2560]{1,0:T(8,128)(2,1)S(1)}, u32[]{:S(2)}, u32[]{:S(2)}) collective-permute-start(bf16[256,2560]{1,0:T(8,128)(2,1)S(1)} %collective-permute-done.6.passed), channel_id=1, source_target_pairs={{1,0},{5,4},{9,8},{13,12},{2,3},{6,7},{10,11},{14,15},{17,16},{21,... | collective-permute-start | bytes 3932168 | tf_op jit(solution)/shard_map/ppermute | solution.py:22
  89.0 5.5 %collective-permute-start.13 = (bf16[128,2560]{1,0:T(8,128)(2,1)S(1)}, bf16[128,2560]{1,0:T(8,128)(2,1)S(1)}, u32[]{:S(2)}, u32[]{:S(2)}) collective-permute-start(bf16[128,2560]{1,0:T(8,128)(2,1)S(1)} %collective-permute-done.9.third), channel_id=1, source_target_pairs={{0,1},{1,0},{2,3},{3,2},{4,5},{5,4},{6,7},{7,6},{8,9},{9,8},{10,11... | collective-permute-start | bytes 1966088 | tf_op jit(solution)/shard_map/ppermute | solution.py:22

commit v5 on v4

--- a/solution.py
+++ b/solution.py
@@ -298,7 +298,7 @@
     more_heads(shape, flags, 2 * quarter, q, before, after, [rest, rest_core])
 
 
-def passed_kernel(shape, lists, counts, q, crossed_core, passed, *refs):
+def passed_kernel(shape, lists, counts, q, passed, *refs):
     before, after, flags, found = refs[:3], refs[3:6], refs[6], refs[7]
     me = lax.axis_index("ctx")
     spot = me % 4
@@ -309,18 +309,16 @@
     @pl.when(outer)
     def _():
         order_flags(flags, 0, half, counts, 1, far_side)
-        more_heads(shape, flags, half, q, before, after, [passed])
-
-    @pl.when(jnp.logical_not(outer))
-    def _():
-        names, _ = crossing_names(found, lists, me, jnp.where(spot == 1, me + 1, me - 1), shape)
-        member_flags(flags, 0, names, lists, counts, me, 0, me % 2, shape)
+
+    @pl.when(jnp.logical_not(outer))
+    def _():
         names, _ = giver_names(found, lists, me, shape)
-        member_flags(flags, half, names, lists, counts, me, 1, far_side, shape)
-        more_heads(shape, flags, 2 * half, q, before, after, [crossed_core, passed])
-
-
-def last_kernel(shape, lists, counts, q, passed_core, third, third_core, *refs):
+        member_flags(flags, 0, names, lists, counts, me, 1, far_side, shape)
+
+    more_heads(shape, flags, half, q, before, after, [passed])
+
+
+def last_kernel(shape, lists, counts, q, passed_core, crossed_core, third, third_core, *refs):
     before, out, flags, found = refs[:3], refs[3], refs[4], refs[5]
     me = lax.axis_index("ctx")
     spot = me % 4
@@ -330,28 +328,29 @@
     names, rest = giver_names(found, lists, me, shape)
     outer = jnp.logical_or(spot == 0, spot == 3)
 
-    def heads(sources, count):
-        filler = -count % blocks
-        for b in range(count, count + filler):
-            flags[b] = jnp.float32(MASKED)
-        mask = spread(flags, 0, count + filler, shape["rows"])
-
-        def head(c):
-            keys, values = packed(sources, c, filler * shape["rows"])
-            _, total, weighted = attend(q[:, c], load_state(before, c), keys, values, [(keys.shape[0], mask)])
-            out[:, c] = (weighted / total).astype(BF16)
-
-        over_heads(shape["width"], head)
-
     @pl.when(outer)
     def _():
         member_flags(flags, 0, names + rest[quarter:] + rest[:quarter], lists, counts, me, 0, me % 2, shape)
-        heads([passed_core, third, third_core], 2 * half)
-
-    @pl.when(jnp.logical_not(outer))
-    def _():
-        member_flags(flags, 0, rest, lists, counts, me, 1, jnp.where(spot < 2, 0, 1), shape)
-        heads([third, third_core], half)
+
+    @pl.when(jnp.logical_not(outer))
+    def _():
+        member_flags(flags, half, rest, lists, counts, me, 1, jnp.where(spot < 2, 0, 1), shape)
+        crossed, _ = crossing_names(found, lists, me, jnp.where(spot == 1, me + 1, me - 1), shape)
+        member_flags(flags, 0, crossed, lists, counts, me, 0, me % 2, shape)
+
+    mask = spread(flags, 0, blocks, shape["rows"])
+
+    def head(c):
+        outer_parts = packed([passed_core], c)
+        inner_parts = packed([crossed_core], c)
+        later = packed([third, third_core], c)
+        keys, values = [
+            jnp.concatenate([jnp.where(outer, x, y), z], axis=0) for x, y, z in zip(outer_parts, inner_parts, later)
+        ]
+        _, total, weighted = attend(q[:, c], load_state(before, c), keys, values, [(keys.shape[0], mask)])
+        out[:, c] = (weighted / total).astype(BF16)
+
+    over_heads(shape["width"], head)
 
 
 def attend_call(body, shape, smem, arrays, state=(), last=False, scratch=()):
@@ -426,9 +425,9 @@
     third, crossed_core = lax.optimization_barrier((third, crossed_core))
     third_core = permute(third, devices, other_core)
     state = attend_call(
-        passed_kernel, shape, smem, (queries, crossed_core, passed), state, False, chosen
+        passed_kernel, shape, smem, (queries, passed), state, False, chosen
     )
-    return attend_call(last_kernel, shape, smem, (queries, passed_core, third, third_core), state, True, chosen)
+    return attend_call(last_kernel, shape, smem, (queries, passed_core, crossed_core, third, third_core), state, True, chosen)
 
 
 def solution(mesh):

time: 99.1 us -> 99.2 us (level)
  no operation moved by 1% of the time
where the time goes in v5:
time: 99.2 us; the launch traced here: 98.8 us
  waiting for transfers between devices  31.1 us (31%)
  Pallas kernels  29.1 us (29%)
  starting transfers between devices  23.1 us (23%)
  blocking collectives  13.3 us (13%)
  other arithmetic  1.89 us (2%)
    ppermute x14, waiting for transfers between devices, permute(): return lax.ppermute(block, 'ctx', pairs)  31.1 us
    pallas_call x5, Pallas kernels, attend_call(): pl.pallas_call(functools.partial(body, shape), out_shape=jax.ShapeDtypeSt...  24.5 us
    ppermute x14, starting transfers between devices, permute(): return lax.ppermute(block, 'ctx', pairs)  23.1 us
    all_to_all x1, blocking collectives, shards(): lists = lax.all_to_all(sent, 'ctx', 0, 0, tiled=True)  13.3 us
    pallas_call x2, Pallas kernels, pack_call(): pl.pallas_call(functools.partial(body, shape), out_shape=tuple((jax.Shape...  4.64 us
  transfers between devices with their start and end apart: 14, of which 4 were waited for; matrix products, arithmetic and copies ran while one was open for 0% of the time, Pallas kernels for 25%

profile of v5, /device:TPU:0, one launch (start us, length us, event | category | flops | bytes accessed | tf_op | source)
XLA Modules:
  0.0 98.8 jit_solution(17029090522263282666)
XLA Ops:
  0.0 1.9 %pad_maximum_fusion.own = bf16[512,2560]{1,0:T(8,128)(2,1)S(1)} fusion(bf16[256,2560]{1,0:T(8,128)(2,1)} %param.7, bf16[256,2560]{1,0:T(8,128)(2,1)} %param.6), kind=kLoop, calls=%fused_computation | loop fusion | flops 5242880 | bytes 5242880 | tf_op jit(solution)/shard_map/concatenate | solution.py:396
  2.5 13.3 %all_to_all.8 = s32[16,1,64]{2,1,0:T(1,128)S(1)} all-to-all(s32[16,1,64]{2,1,0:T(1,128)S(1)} %broadcast_in_dim.8), channel_id=1, replica_groups=mesh['groups'=2,'ctx'=16] {'ctx'}, dimensions={0} | all-to-all | bytes 8192 | tf_op jit(solution)/shard_map/all_to_all | solution.py:394
  15.8 2.6 %shard_map.55 = (bf16[256,2560]{1,0:T(8,128)(2,1)}, bf16[128,2560]{1,0:T(8,128)(2,1)}, bf16[128,2560]{1,0:T(8,128)(2,1)}, bf16[64,2560]{1,0:T(8,128)(2,1)}, bf16[64,2560]{1,0:T(8,128)(2,1)}) custom-call(s32[16,64]{1,0:T(8,128)S(1)} %bitcast.1, bf16[512,2560]{1,0:T(8,128)(2,1)S(1)} %pad_maximum_fusion.own), custom_call_target="tpu_custom_call" | custom-call | flops 1000 | bytes 1000 | tf_op jit(solution)/shard_map/pallas_call | solution.py:115
  18.9 2.5 %collective-permute-start.2 = (bf16[128,2560]{1,0:T(8,128)(2,1)}, bf16[128,2560]{1,0:T(8,128)(2,1)S(1)}, u32[]{:S(2)}, u32[]{:S(2)}) collective-permute-start(bf16[128,2560]{1,0:T(8,128)(2,1)} %get-tuple-element.53), channel_id=1, source_target_pairs={{0,4},{1,5},{2,6},{3,7},{4,8},{5,9},{6,10},{7,11},{8,12},{9,13},{1... | collective-permute-start | bytes 1966088 | tf_op jit(solution)/shard_map/ppermute | solution.py:22
  21.4 1.3 %collective-permute-start.3 = (bf16[128,2560]{1,0:T(8,128)(2,1)}, bf16[128,2560]{1,0:T(8,128)(2,1)}, u32[]{:S(2)}, u32[]{:S(2)}) collective-permute-start(bf16[128,2560]{1,0:T(8,128)(2,1)} %get-tuple-element.54), channel_id=1, source_target_pairs={{4,0},{5,1},{6,2},{7,3},{8,4},{9,5},{10,6},{11,7},{12,8},{13,9},{1... | collective-permute-start | bytes 1966088 | tf_op jit(solution)/shard_map/ppermute | solution.py:22
  22.7 5.3 %collective-permute-start.4 = (bf16[64,2560]{1,0:T(8,128)(2,1)}, bf16[64,2560]{1,0:T(8,128)(2,1)}, u32[]{:S(2)}, u32[]{:S(2)}) collective-permute-start(bf16[64,2560]{1,0:T(8,128)(2,1)} %get-tuple-element.55), channel_id=1, source_target_pairs={{0,8},{1,9},{2,10},{3,11},{4,12},{5,13},{6,14},{7,15},{16,24},{17,... | collective-permute-start | bytes 983048 | tf_op jit(solution)/shard_map/ppermute | solution.py:22
  28.0 1.3 %collective-permute-start.5 = (bf16[64,2560]{1,0:T(8,128)(2,1)}, bf16[64,2560]{1,0:T(8,128)(2,1)}, u32[]{:S(2)}, u32[]{:S(2)}) collective-permute-start(bf16[64,2560]{1,0:T(8,128)(2,1)} %get-tuple-element.56), channel_id=1, source_target_pairs={{8,0},{9,1},{10,2},{11,3},{12,4},{13,5},{14,6},{15,7},{24,16},{25,... | collective-permute-start | bytes 983048 | tf_op jit(solution)/shard_map/ppermute | solution.py:22
  29.4 2.0 %shard_map.56 = (bf16[128,2560]{1,0:T(8,128)(2,1)S(1)}, bf16[128,2560]{1,0:T(8,128)(2,1)S(1)}) custom-call(s32[16,64]{1,0:T(8,128)S(1)} %bitcast.2, bf16[512,2560]{1,0:T(8,128)(2,1)S(1)} %pad_maximum_fusion.own, bf16[512,2560]{1,0:T(8,128)(2,1)} %collective-permute-done.1.other), custom_call_target="tpu_custom_call" | custom-call | flops 1000 | bytes 1000 | tf_op jit(solution)/shard_map/pallas_call | solution.py:115
  31.5 5.1 %shard_map.57 = (f32[256,2560]{1,0:T(8,128)S(1)}, f32[256,2560]{1,0:T(8,128)S(1)}, f32[256,2560]{1,0:T(8,128)S(1)}) custom-call(s32[16,64]{1,0:T(8,128)S(1)} %bitcast.3, s32[1,4,2]{2,1,0:T(4,128)S(1)} %copy.15.counts, bf16[256,2560]{1,0:T(8,128)(2,1)S(1)} %copy-done, bf16[512,2560]{1,0:T(8,128)(2,1)S(1)} %pad_maximum_fusion.own, ...), custom_call_target="tpu_custom_call" | custom-call | flops 1000 | bytes 1000 | tf_op jit(solution)/shard_map/pallas_call | solution.py:358
  36.6 5.9 %collective-permute-done.4.refs_2_ = bf16[64,2560]{1,0:T(8,128)(2,1)} collective-permute-done((bf16[64,2560]{1,0:T(8,128)(2,1)}, bf16[64,2560]{1,0:T(8,128)(2,1)}, u32[]{:S(2)}, u32[]{:S(2)}) %collective-permute-start.4) | collective-permute-done | bytes 327712 | tf_op jit(solution)/shard_map/ppermute | solution.py:22
  42.5 11.1 %collective-permute-done.5.refs_3_ = bf16[64,2560]{1,0:T(8,128)(2,1)} collective-permute-done((bf16[64,2560]{1,0:T(8,128)(2,1)}, bf16[64,2560]{1,0:T(8,128)(2,1)}, u32[]{:S(2)}, u32[]{:S(2)}) %collective-permute-start.5) | collective-permute-done | bytes 327712 | tf_op jit(solution)/shard_map/ppermute | solution.py:22
  53.6 1.3 %collective-permute-start.7 = (bf16[128,2560]{1,0:T(8,128)(2,1)S(1)}, bf16[128,2560]{1,0:T(8,128)(2,1)S(1)}, u32[]{:S(2)}, u32[]{:S(2)}) collective-permute-start(bf16[128,2560]{1,0:T(8,128)(2,1)S(1)} %get-tuple-element.58), channel_id=1, source_target_pairs={{2,6},{6,10},{10,14},{3,7},{7,11},{11,15},{4,0},{8,4},{12,8},{5,1}... | collective-permute-start | bytes 1966088 | tf_op jit(solution)/shard_map/ppermute | solution.py:22
  54.9 1.6 %collective-permute-start.8 = (bf16[128,2560]{1,0:T(8,128)(2,1)S(1)}, bf16[128,2560]{1,0:T(8,128)(2,1)S(1)}, u32[]{:S(2)}, u32[]{:S(2)}) collective-permute-start(bf16[128,2560]{1,0:T(8,128)(2,1)S(1)} %get-tuple-element.59), channel_id=1, source_target_pairs={{0,2},{1,3},{2,0},{3,1},{4,6},{5,7},{6,4},{7,5},{8,10},{9,11},{10,... | collective-permute-start | bytes 1966088 | tf_op jit(solution)/shard_map/ppermute | solution.py:22
  56.5 3.2 %collective-permute-start.6 = (bf16[256,2560]{1,0:T(8,128)(2,1)}, bf16[256,2560]{1,0:T(8,128)(2,1)S(1)}, u32[]{:S(2)}, u32[]{:S(2)}) collective-permute-start(bf16[256,2560]{1,0:T(8,128)(2,1)} %collective-permute-done.crossed), channel_id=1, source_target_pairs={{0,4},{4,8},{8,12},{1,5},{5,9},{9,13},{6,2},{10,6},{14,10},{7,3},{... | collective-permute-start | bytes 3932168 | tf_op jit(solution)/shard_map/ppermute | solution.py:22
  59.6 6.7 %shard_map.58 = (f32[256,2560]{1,0:T(8,128)S(1)}, f32[256,2560]{1,0:T(8,128)S(1)}, f32[256,2560]{1,0:T(8,128)S(1)}) custom-call(s32[16,64]{1,0:T(8,128)S(1)} %bitcast.4, s32[1,4,2]{2,1,0:T(4,128)S(1)} %copy.15.counts, bf16[256,2560]{1,0:T(8,128)(2,1)S(1)} %copy-done, bf16[256,2560]{1,0:T(8,128)(2,1)} %collective-permute-done.crossed, ...), custom_call_target="tpu_custom_call" | custom-call | flops 1000 | bytes 1000 | tf_op jit(solution)/shard_map/pallas_call | solution.py:358
  66.4 4.1 %collective-permute-done.7 = bf16[128,2560]{1,0:T(8,128)(2,1)S(1)} collective-permute-done((bf16[128,2560]{1,0:T(8,128)(2,1)S(1)}, bf16[128,2560]{1,0:T(8,128)(2,1)S(1)}, u32[]{:S(2)}, u32[]{:S(2)}) %collective-permute-start.7) | collective-permute-done | bytes 655392 | tf_op jit(solution)/shard_map/ppermute | solution.py:22
  70.5 1.0 collective-permute-start.9
  71.5 2.2 %collective-permute-start.12 = (bf16[256,2560]{1,0:T(8,128)(2,1)}, bf16[256,2560]{1,0:T(8,128)(2,1)S(1)}, u32[]{:S(2)}, u32[]{:S(2)}) collective-permute-start(bf16[256,2560]{1,0:T(8,128)(2,1)} %collective-permute-done.crossed), channel_id=1, source_target_pairs={{0,1},{4,5},{8,9},{12,13},{3,2},{7,6},{11,10},{15,14},{16,17},{20,... | collective-permute-start | bytes 3932168 | tf_op jit(solution)/shard_map/ppermute | solution.py:22
  73.7 4.0 %shard_map.59 = (f32[256,2560]{1,0:T(8,128)S(1)}, f32[256,2560]{1,0:T(8,128)S(1)}, f32[256,2560]{1,0:T(8,128)S(1)}) custom-call(s32[16,64]{1,0:T(8,128)S(1)} %bitcast.5, s32[1,4,2]{2,1,0:T(4,128)S(1)} %copy.15.counts, bf16[256,2560]{1,0:T(8,128)(2,1)S(1)} %copy-done, bf16[128,2560]{1,0:T(8,128)(2,1)S(1)} %collective-permute-done.8.rest, ...), custom_call_target="tpu_custom_call" | custom-call | flops 1000 | bytes 1000 | tf_op jit(solution)/shard_map/pallas_call | solution.py:358
  77.7 9.9 %collective-permute-done.9.third = bf16[128,2560]{1,0:T(8,128)(2,1)S(1)} collective-permute-done((bf16[128,2560]{1,0:T(8,128)(2,1)S(1)}, bf16[128,2560]{1,0:T(8,128)(2,1)S(1)}, u32[]{:S(2)}, u32[]{:S(2)}) %collective-permute-start.9) | collective-permute-done | bytes 655392 | tf_op jit(solution)/shard_map/ppermute | solution.py:22
  87.7 1.3 %collective-permute-start.11 = (bf16[256,2560]{1,0:T(8,128)(2,1)S(1)}, bf16[256,2560]{1,0:T(8,128)(2,1)S(1)}, u32[]{:S(2)}, u32[]{:S(2)}) collective-permute-start(bf16[256,2560]{1,0:T(8,128)(2,1)S(1)} %collective-permute-done.6.passed), channel_id=1, source_target_pairs={{1,0},{5,4},{9,8},{13,12},{2,3},{6,7},{10,11},{14,15},{17,16},{21,... | collective-permute-start | bytes 3932168 | tf_op jit(solution)/shard_map/ppermute | solution.py:22
  89.0 1.3 %collective-permute-start.13 = (bf16[128,2560]{1,0:T(8,128)(2,1)S(1)}, bf16[128,2560]{1,0:T(8,128)(2,1)S(1)}, u32[]{:S(2)}, u32[]{:S(2)}) collective-permute-start(bf16[128,2560]{1,0:T(8,128)(2,1)S(1)} %collective-permute-done.9.third), channel_id=1, source_target_pairs={{0,1},{1,0},{2,3},{3,2},{4,5},{5,4},{6,7},{7,6},{8,9},{9,8},{10,11... | collective-permute-start | bytes 1966088 | tf_op jit(solution)/shard_map/ppermute | solution.py:22
  90.2 4.0 %shard_map.60 = (f32[256,2560]{1,0:T(8,128)S(1)}, f32[256,2560]{1,0:T(8,128)S(1)}, f32[256,2560]{1,0:T(8,128)S(1)}) custom-call(s32[16,64]{1,0:T(8,128)S(1)} %bitcast.6, s32[1,4,2]{2,1,0:T(4,128)S(1)} %copy.15.counts, bf16[256,2560]{1,0:T(8,128)(2,1)S(1)} %copy-done, bf16[256,2560]{1,0:T(8,128)(2,1)S(1)} %collective-permute-done.6.passed, ...), custom_call_target="tpu_custom_call" | custom-call | flops 1000 | bytes 1000 | tf_op jit(solution)/shard_map/pallas_call | solution.py:358
  94.2 4.6 %shard_map.61 = bf16[256,2560]{1,0:T(8,128)(2,1)} custom-call(s32[16,64]{1,0:T(8,128)S(1)} %bitcast.7, s32[1,4,2]{2,1,0:T(4,128)S(1)} %copy.15.counts, bf16[256,2560]{1,0:T(8,128)(2,1)S(1)} %copy-done, bf16[256,2560]{1,0:T(8,128)(2,1)S(1)} %collective-permute-done.11.passed_core, bf16[256,2560]{1,0:T(8,128)(2,1)S(1)} %collective-permute-done.12.crossed_core, ...), custom_call_target="tpu_custom_call" | custom-call | flops 1000 | bytes 1000 | tf_op jit(solution)/shard_map/pallas_call | solution.py:358
  (22 shorter events, 1.3 us)
Async XLA Ops:
  0.0 2.4 %copy-start.1 = (s32[1,4,2,8]{3,2,1,0:T(2,128)S(1)}, s32[1,4,2,8]{3,2,1,0:T(2,128)}, u32[]{:S(2)}) copy-start(s32[1,4,2,8]{3,2,1,0:T(2,128)} %param.8) | copy-start | bytes 772
  1.9 27.4 %copy-start.2 = (s32[1,4,2]{1,2,0:T(2,128)S(1)}, s32[1,4,2]{1,2,0:T(2,128)}, u32[]{:S(2)}) copy-start(s32[1,4,2]{1,2,0:T(2,128)} %param.9) | copy-start | bytes 100
  1.9 26.1 %collective-permute-start.1 = (bf16[512,2560]{1,0:T(8,128)(2,1)S(1)}, bf16[512,2560]{1,0:T(8,128)(2,1)}, u32[]{:S(2)}, u32[]{:S(2)}) collective-permute-start(bf16[512,2560]{1,0:T(8,128)(2,1)S(1)} %pad_maximum_fusion.own), channel_id=1, source_target_pairs={{0,1},{1,0},{2,3},{3,2},{4,5},{5,4},{6,7},{7,6},{8,9},{9,8},{10,11... | collective-permute-start | bytes 7864328 | tf_op jit(solution)/shard_map/ppermute | solution.py:22
  18.4 35.2 %collective-permute-start = (bf16[256,2560]{1,0:T(8,128)(2,1)}, bf16[256,2560]{1,0:T(8,128)(2,1)}, u32[]{:S(2)}, u32[]{:S(2)}) collective-permute-start(bf16[256,2560]{1,0:T(8,128)(2,1)} %get-tuple-element.47), channel_id=1, source_target_pairs={{0,2},{1,3},{2,0},{3,1},{4,6},{5,7},{6,4},{7,5},{8,10},{9,11},{10,... | collective-permute-start | bytes 3932168 | tf_op jit(solution)/shard_map/ppermute | solution.py:22
  18.9 34.7 %collective-permute-start.2 = (bf16[128,2560]{1,0:T(8,128)(2,1)}, bf16[128,2560]{1,0:T(8,128)(2,1)S(1)}, u32[]{:S(2)}, u32[]{:S(2)}) collective-permute-start(bf16[128,2560]{1,0:T(8,128)(2,1)} %get-tuple-element.53), channel_id=1, source_target_pairs={{0,4},{1,5},{2,6},{3,7},{4,8},{5,9},{6,10},{7,11},{8,12},{9,13},{1... | collective-permute-start | bytes 1966088 | tf_op jit(solution)/shard_map/ppermute | solution.py:22
  21.4 32.2 %collective-permute-start.3 = (bf16[128,2560]{1,0:T(8,128)(2,1)}, bf16[128,2560]{1,0:T(8,128)(2,1)}, u32[]{:S(2)}, u32[]{:S(2)}) collective-permute-start(bf16[128,2560]{1,0:T(8,128)(2,1)} %get-tuple-element.54), channel_id=1, source_target_pairs={{4,0},{5,1},{6,2},{7,3},{8,4},{9,5},{10,6},{11,7},{12,8},{13,9},{1... | collective-permute-start | bytes 1966088 | tf_op jit(solution)/shard_map/ppermute | solution.py:22
  22.7 19.8 %collective-permute-start.4 = (bf16[64,2560]{1,0:T(8,128)(2,1)}, bf16[64,2560]{1,0:T(8,128)(2,1)}, u32[]{:S(2)}, u32[]{:S(2)}) collective-permute-start(bf16[64,2560]{1,0:T(8,128)(2,1)} %get-tuple-element.55), channel_id=1, source_target_pairs={{0,8},{1,9},{2,10},{3,11},{4,12},{5,13},{6,14},{7,15},{16,24},{17,... | collective-permute-start | bytes 983048 | tf_op jit(solution)/shard_map/ppermute | solution.py:22
  28.0 25.6 %collective-permute-start.5 = (bf16[64,2560]{1,0:T(8,128)(2,1)}, bf16[64,2560]{1,0:T(8,128)(2,1)}, u32[]{:S(2)}, u32[]{:S(2)}) collective-permute-start(bf16[64,2560]{1,0:T(8,128)(2,1)} %get-tuple-element.56), channel_id=1, source_target_pairs={{8,0},{9,1},{10,2},{11,3},{12,4},{13,5},{14,6},{15,7},{24,16},{25,... | collective-permute-start | bytes 983048 | tf_op jit(solution)/shard_map/ppermute | solution.py:22
  29.4 2.1 %copy-start = (bf16[256,2560]{1,0:T(8,128)(2,1)S(1)}, bf16[256,2560]{1,0:T(8,128)(2,1)}, u32[]{:S(2)}) copy-start(bf16[256,2560]{1,0:T(8,128)(2,1)} %q.9) | copy-start | bytes 3932164
  53.6 16.9 %collective-permute-start.7 = (bf16[128,2560]{1,0:T(8,128)(2,1)S(1)}, bf16[128,2560]{1,0:T(8,128)(2,1)S(1)}, u32[]{:S(2)}, u32[]{:S(2)}) collective-permute-start(bf16[128,2560]{1,0:T(8,128)(2,1)S(1)} %get-tuple-element.58), channel_id=1, source_target_pairs={{2,6},{6,10},{10,14},{3,7},{7,11},{11,15},{4,0},{8,4},{12,8},{5,1}... | collective-permute-start | bytes 1966088 | tf_op jit(solution)/shard_map/ppermute | solution.py:22
  54.9 15.6 %collective-permute-start.8 = (bf16[128,2560]{1,0:T(8,128)(2,1)S(1)}, bf16[128,2560]{1,0:T(8,128)(2,1)S(1)}, u32[]{:S(2)}, u32[]{:S(2)}) collective-permute-start(bf16[128,2560]{1,0:T(8,128)(2,1)S(1)} %get-tuple-element.59), channel_id=1, source_target_pairs={{0,2},{1,3},{2,0},{3,1},{4,6},{5,7},{6,4},{7,5},{8,10},{9,11},{10,... | collective-permute-start | bytes 1966088 | tf_op jit(solution)/shard_map/ppermute | solution.py:22
  56.5 31.2 %collective-permute-start.6 = (bf16[256,2560]{1,0:T(8,128)(2,1)}, bf16[256,2560]{1,0:T(8,128)(2,1)S(1)}, u32[]{:S(2)}, u32[]{:S(2)}) collective-permute-start(bf16[256,2560]{1,0:T(8,128)(2,1)} %collective-permute-done.crossed), channel_id=1, source_target_pairs={{0,4},{4,8},{8,12},{1,5},{5,9},{9,13},{6,2},{10,6},{14,10},{7,3},{... | collective-permute-start | bytes 3932168 | tf_op jit(solution)/shard_map/ppermute | solution.py:22
  70.5 3.2 %collective-permute-start.10 = (bf16[128,2560]{1,0:T(8,128)(2,1)S(1)}, bf16[128,2560]{1,0:T(8,128)(2,1)S(1)}, u32[]{:S(2)}, u32[]{:S(2)}) collective-permute-start(bf16[128,2560]{1,0:T(8,128)(2,1)S(1)} %collective-permute-done.8.rest), channel_id=1, source_target_pairs={{0,1},{1,0},{2,3},{3,2},{4,5},{5,4},{6,7},{7,6},{8,9},{9,8},{10,11... | collective-permute-start | bytes 1966088 | tf_op jit(solution)/shard_map/ppermute | solution.py:22
  70.5 17.1 %collective-permute-start.9 = (bf16[128,2560]{1,0:T(8,128)(2,1)S(1)}, bf16[128,2560]{1,0:T(8,128)(2,1)S(1)}, u32[]{:S(2)}, u32[]{:S(2)}) collective-permute-start(bf16[128,2560]{1,0:T(8,128)(2,1)S(1)} %collective-permute-done.7), channel_id=1, source_target_pairs={{0,2},{1,3},{2,0},{3,1},{4,6},{5,7},{6,4},{7,5},{8,10},{9,11},{10,... | collective-permute-start | bytes 1966088 | tf_op jit(solution)/shard_map/ppermute | solution.py:22
  71.5 17.5 %collective-permute-start.12 = (bf16[256,2560]{1,0:T(8,128)(2,1)}, bf16[256,2560]{1,0:T(8,128)(2,1)S(1)}, u32[]{:S(2)}, u32[]{:S(2)}) collective-permute-start(bf16[256,2560]{1,0:T(8,128)(2,1)} %collective-permute-done.crossed), channel_id=1, source_target_pairs={{0,1},{4,5},{8,9},{12,13},{3,2},{7,6},{11,10},{15,14},{16,17},{20,... | collective-permute-start | bytes 3932168 | tf_op jit(solution)/shard_map/ppermute | solution.py:22
  87.7 6.5 %collective-permute-start.11 = (bf16[256,2560]{1,0:T(8,128)(2,1)S(1)}, bf16[256,2560]{1,0:T(8,128)(2,1)S(1)}, u32[]{:S(2)}, u32[]{:S(2)}) collective-permute-start(bf16[256,2560]{1,0:T(8,128)(2,1)S(1)} %collective-permute-done.6.passed), channel_id=1, source_target_pairs={{1,0},{5,4},{9,8},{13,12},{2,3},{6,7},{10,11},{14,15},{17,16},{21,... | collective-permute-start | bytes 3932168 | tf_op jit(solution)/shard_map/ppermute | solution.py:22
  89.0 5.2 %collective-permute-start.13 = (bf16[128,2560]{1,0:T(8,128)(2,1)S(1)}, bf16[128,2560]{1,0:T(8,128)(2,1)S(1)}, u32[]{:S(2)}, u32[]{:S(2)}) collective-permute-start(bf16[128,2560]{1,0:T(8,128)(2,1)S(1)} %collective-permute-done.9.third), channel_id=1, source_target_pairs={{0,1},{1,0},{2,3},{3,2},{4,5},{5,4},{6,7},{7,6},{8,9},{9,8},{10,11... | collective-permute-start | bytes 1966088 | tf_op jit(solution)/shard_map/ppermute | solution.py:22
